TPU v7x, 512 devices: a whole 4x4x16 slice. The times are simulated.
512 devices in a mesh: tm: 8 (over x_hi, y), space: 64 (over x_lo, z, core).
Axes of the slice: x: 4 (x_hi: 2, x_lo: 2; x = x_hi * 2 + x_lo), y: 4, z: 16, core: 2. Of those that a mesh axis runs over, the one named last changes fastest.
Arguments:
- frames_in: bfloat16 [16, 256, 128, 256], P('tm', 'space'), may hold values from -6 to 6
- w_space: bfloat16 [9, 256, 256], replicated, may hold values from -0.125 to 0.125
- w_time: bfloat16 [3, 256, 256], replicated, may hold values from -0.21875 to 0.21875
- grad_out: bfloat16 [16, 256, 128, 256], P('tm', 'space'), may hold values from -16 to 16
Outputs:
- block_out: bfloat16 [16, 256, 128, 256], P('tm', 'space')
- grad_in: bfloat16 [16, 256, 128, 256], P('tm', 'space')
- grad_space: float32 [9, 256, 256], P(None, 'tm', 'space')
- grad_time: float32 [3, 256, 256], P(None, 'tm', 'space')
All inputs are finite; a program needn't handle non-finite values.
Results may differ from a plain program's by a relative error of at most 0.0057.
Values may be sent and summed in bfloat16 or wider, within the bound.
No kernel may reach another device: no remote copies, remote signals or barrier semaphores. Data moves between devices by JAX's collectives and lax.ppermute only.
A program may use at most 64 MiB of HBM per device.

v0:
```python
import jax
import jax.numpy as jnp
from jax import lax
from jax.sharding import PartitionSpec as P


def extended_2(block, sides, width):
    for axis, dim in sides:
        count = lax.axis_size(axis)
        forward = [(i, i + 1) for i in range(count - 1)]
        backward = [(target, source) for source, target in forward]
        low = lax.ppermute(
            lax.slice_in_dim(block, block.shape[dim] - width, None, axis=dim), axis, forward
        )
        high = lax.ppermute(lax.slice_in_dim(block, 0, width, axis=dim), axis, backward)
        block = jnp.concatenate([low, block, high], axis=dim)
    return block


def pad_columns(field):
    return jnp.pad(field, ((0, 0), (0, 0), (1, 1), (0, 0)))


def temporal(past_ext, grad_ext, w_time, count):
    chans = past_ext.shape[-1]
    shape = grad_ext[0:count].shape
    flat_grad = grad_ext[0:count].reshape(-1, chans)
    out_sum = jnp.zeros(flat_grad.shape, jnp.float32)
    back_sum = jnp.zeros(flat_grad.shape, jnp.float32)
    filters = []
    for k in range(3):
        source = past_ext[k : k + count].reshape(-1, chans)
        out_sum = out_sum + jnp.dot(source, w_time[k], preferred_element_type=jnp.float32)
        later = grad_ext[2 - k : 2 - k + count].reshape(-1, chans)
        back_sum = back_sum + lax.dot_general(
            later, w_time[k], (((1,), (1,)), ((), ())), preferred_element_type=jnp.float32
        )
        filters.append(
            lax.dot_general(
                flat_grad, source, (((0,), (0,)), ((), ())), preferred_element_type=jnp.float32
            )
        )
    return (
        out_sum.reshape(shape).astype(jnp.bfloat16),
        back_sum.reshape(shape).astype(jnp.bfloat16),
        jnp.stack(filters, axis=1),
    )


def body(frames_in, w_space, w_time, grad_out):
    count, height, width, chans = frames_in.shape
    extended = pad_columns(extended_2(frames_in, (("space", 1),), 1))
    pre = jnp.zeros((count * height * width, chans), jnp.float32)
    for i in range(3):
        for j in range(3):
            window = extended[:, i : i + height, j : j + width].reshape(-1, chans)
            pre = pre + jnp.dot(window, w_space[3 * i + j], preferred_element_type=jnp.float32)
    pre = pre.reshape(count, height, width, chans)
    hidden = jax.nn.silu(pre).astype(jnp.bfloat16)
    hid_cols, grad_cols = (
        lax.all_to_all(hidden, "tm", split_axis=2, concat_axis=0, tiled=True),
        lax.all_to_all(grad_out, "tm", split_axis=2, concat_axis=0, tiled=True),
    )
    blank = jnp.zeros((2,) + hid_cols.shape[1:], jnp.bfloat16)
    past_ext = jnp.concatenate([blank, hid_cols], axis=0)
    grad_ext = jnp.concatenate([grad_cols, blank], axis=0)
    out_cols, back_cols, time_terms = temporal(past_ext, grad_ext, w_time, hid_cols.shape[0])
    block_out, grad_hidden = (
        lax.all_to_all(out_cols, "tm", split_axis=0, concat_axis=2, tiled=True),
        lax.all_to_all(back_cols, "tm", split_axis=0, concat_axis=2, tiled=True),
    )
    sig = jax.nn.sigmoid(pre)
    grad_pre = (grad_hidden.astype(jnp.float32) * sig * (1.0 + pre * (1.0 - sig))).astype(
        jnp.bfloat16
    )
    grad_ext_rows = pad_columns(extended_2(grad_pre, (("space", 1),), 1))
    flat_pre = grad_pre.reshape(-1, chans)
    back = jnp.zeros((count * height * width, chans), jnp.float32)
    space_terms = []
    for i in range(3):
        for j in range(3):
            window = grad_ext_rows[:, 2 - i : 2 - i + height, 2 - j : 2 - j + width].reshape(
                -1, chans
            )
            back = back + lax.dot_general(
                window,
                w_space[3 * i + j],
                (((1,), (1,)), ((), ())),
                preferred_element_type=jnp.float32,
            )
            source = extended[:, i : i + height, j : j + width].reshape(-1, chans)
            space_terms.append(
                lax.dot_general(
                    flat_pre, source, (((0,), (0,)), ((), ())), preferred_element_type=jnp.float32
                )
            )
    grad_in = back.reshape(count, height, width, chans).astype(jnp.bfloat16)
    space_sum = jnp.stack(space_terms, axis=1)
    partial_space, partial_time = (
        lax.psum_scatter(space_sum, "space", scatter_dimension=0, tiled=True),
        lax.psum_scatter(time_terms, "space", scatter_dimension=0, tiled=True),
    )
    owned_space, owned_time = (
        lax.psum_scatter(partial_space, "tm", scatter_dimension=2, tiled=True),
        lax.psum_scatter(partial_time, "tm", scatter_dimension=2, tiled=True),
    )
    grad_space = jnp.transpose(owned_space, (1, 2, 0))
    grad_time = jnp.transpose(owned_time, (1, 2, 0))
    return (block_out, grad_in, grad_space, grad_time)


def solution(mesh):
    in_specs = (P("tm", "space", None, None), P(), P(), P("tm", "space", None, None))
    out_specs = (
        P("tm", "space", None, None),
        P("tm", "space", None, None),
        P(None, "tm", "space"),
        P(None, "tm", "space"),
    )
    return jax.shard_map(body, mesh=mesh, in_specs=in_specs, out_specs=out_specs, check_vma=False)
```

profile of v0, /device:TPU:24, one launch (start us, length us, event | category | flops | bytes accessed | tf_op | source)
XLA Modules:
  0.0 706.6 jit_solution(7725443780179404535)
XLA Ops:
  8.2 1.7 collective-permute-start
  11.3 2.2 copy.53
  13.5 9.2 %all-to-all-start.2 = ((bf16[2,4,128,256]{3,1,0,2:T(4,128)(2,1)}), bf16[2,4,128,256]{3,1,0,2:T(4,128)(2,1)}, u32[]{:S(2)}, u32[]{:S(2)}) async-start(bf16[2,4,128,256]{3,1,0,2:T(4,128)(2,1)} %copy.53), calls=%async_computation.2 | async-start | bytes 1048576 | tf_op jit(solution)/shard_map/all_to_all | solution.py:62
  28.8 1.3 convolution_add_fusion.13
  30.1 3.0 all-to-all-done.2
  36.2 5.5 all-to-all-start.3
  41.7 2.5 fusion.32
  44.2 1.3 convolution_add_fusion.12
  45.5 5.7 all-to-all-done.3
  51.2 1.3 convert_bitcast_fusion
  53.0 1.4 fusion.16
  57.1 6.0 all-to-all-start
  64.4 1.5 collective-permute-start.3
  75.8 1.6 fusion.84
  77.5 1.5 convolution_bitcast_fusion
  81.0 1.4 copy.67
  85.3 1.3 fusion.30
  90.5 1.4 convolution_add_fusion.1
  93.5 7.2 %all-to-all-start.1 = ((bf16[16,4,16,256]{3,2,1,0:T(8,128)(2,1)}), bf16[16,4,16,256]{3,2,1,0:T(8,128)(2,1)}, u32[]{:S(2)}, u32[]{:S(2)}) async-start(bf16[16,4,16,256]{3,2,1,0:T(8,128)(2,1)} %bitcast.28), calls=%async_computation.1 | async-start | bytes 1048576 | tf_op jit(solution)/shard_map/all_to_all | solution.py:69
  100.8 428.0 %all-reduce.9.cloned.1.call-done = (f32[256,9,256]{2,0,1:T(8,128)}, f32[256,3,256]{2,1,0:T(4,128)}) async-done(((f32[256,9,256]{2,0,1:T(8,128)}, f32[256,3,256]{2,1,0:T(4,128)}), (f32[256,9,256]{2,0,1:T(8,128)}, f32[256,3,256]{2,1,0:T(4,128)})) %all-reduce.9.cloned.1.call-update) | async-done | bytes 3145744
  534.1 2.6 fusion.3
  536.6 1.9 copy.52
  538.5 71.1 %reduce-scatter.10.cloned.1.call-done = f32[32,12]{1,0:T(8,128)} async-done(((f32[256,12]{1,0:T(8,128)}), f32[32,12]{1,0:T(8,128)}) %reduce-scatter.10.cloned.1.call-update) | async-done | bytes 1552
  611.1 87.4 %reduce-scatter.8.cloned.1.call-done = f32[32,36]{1,0:T(8,128)} async-done(((f32[256,36]{1,0:T(8,128)}), f32[32,36]{1,0:T(8,128)}) %reduce-scatter.8.cloned.1.call-update) | async-done | bytes 4624
  (116 shorter events, 43.7 us)
Async XLA Ops:
  7.2 17.5 %copy-start = (bf16[2,4,128,256]{3,2,1,0:T(8,128)(2,1)S(1)}, bf16[2,4,128,256]{3,2,1,0:T(8,128)(2,1)}, u32[]{:S(2)}) copy-start(bf16[2,4,128,256]{3,2,1,0:T(8,128)(2,1)} %param.4) | copy-start | bytes 1572868
  8.2 16.4 %collective-permute-start = (bf16[2,1,128,256]{3,2,1,0:T(8,128)(2,1)S(1)}, bf16[2,1,128,256]{3,2,1,0:T(8,128)(2,1)S(1)}, u32[]{:S(2)}, u32[]{:S(2)}) collective-permute-start(bf16[2,1,128,256]{3,2,1,0:T(8,128)(2,1)S(1)} %get-tuple-element.46), channel_id=1, source_target_pairs={{0,1},{1,2},{2,3},{3,4},{4,5},{5,6},{6,7},{7,8},{8,9},{9,10},{10,1... | collective-permute-start | bytes 393224 | tf_op jit(solution)/shard_map/ppermute | solution.py:12
  10.0 14.7 %collective-permute-start.1 = (bf16[2,1,128,256]{3,2,1,0:T(8,128)(2,1)S(1)}, bf16[2,1,128,256]{3,2,1,0:T(8,128)(2,1)S(1)}, u32[]{:S(2)}, u32[]{:S(2)}) collective-permute-start(bf16[2,1,128,256]{3,2,1,0:T(8,128)(2,1)S(1)} %get-tuple-element.47), channel_id=1, source_target_pairs={{1,0},{2,1},{3,2},{4,3},{5,4},{6,5},{7,6},{8,7},{9,8},{10,9},{11,1... | collective-permute-start | bytes 393224 | tf_op jit(solution)/shard_map/ppermute | solution.py:15
  13.5 19.5 %all-to-all-start.2 = ((bf16[2,4,128,256]{3,1,0,2:T(4,128)(2,1)}), bf16[2,4,128,256]{3,1,0,2:T(4,128)(2,1)}, u32[]{:S(2)}, u32[]{:S(2)}) async-start(bf16[2,4,128,256]{3,1,0,2:T(4,128)(2,1)} %copy.53), calls=%async_computation.2 | async-start | bytes 1048576 | tf_op jit(solution)/shard_map/all_to_all | solution.py:62
  24.9 1.3 copy-start.1
  30.1 4.2 copy-start.13
  36.2 15.0 %all-to-all-start.3 = ((bf16[16,4,16,256]{3,2,1,0:T(8,128)(2,1)}), bf16[16,4,16,256]{3,2,1,0:T(8,128)(2,1)}, u32[]{:S(2)}, u32[]{:S(2)}) async-start(bf16[16,4,16,256]{3,2,1,0:T(8,128)(2,1)} %bitcast.277), calls=%async_computation.3 | async-start | bytes 1048576 | tf_op jit(solution)/shard_map/all_to_all | solution.py:70
  41.7 2.5 copy-start.4
  41.7 2.5 copy-start.12
  51.2 1.4 copy-start.15
  51.2 1.7 copy-start.16
  51.2 1.8 copy-start.21
  54.9 11.1 %copy-start.7 = (bf16[2,4,128,256]{3,2,1,0:T(8,128)(2,1)S(1)}, bf16[2,4,128,256]{3,2,1,0:T(8,128)(2,1)}, u32[]{:S(2)}) copy-start(bf16[2,4,128,256]{3,2,1,0:T(8,128)(2,1)} %copy-done.6) | copy-start | bytes 1572868
  57.1 20.3 %all-to-all-start = ((bf16[2,4,128,256]{3,1,0,2:T(4,128)(2,1)}), bf16[2,4,128,256]{3,1,0,2:T(4,128)(2,1)}, u32[]{:S(2)}, u32[]{:S(2)}) async-start(bf16[2,4,128,256]{3,1,0,2:T(4,128)(2,1)} %copy.49), calls=%async_computation | async-start | bytes 1048576 | tf_op jit(solution)/shard_map/all_to_all | solution.py:61
  63.1 465.6 %all-reduce.9.cloned.1.call-start = ((), (), s32[]{:S(2)}) async-start(), calls=%async_computation.8 | async-start | bytes 6815744
  63.1 11.2 %collective-permute-start.2 = (bf16[2,1,128,256]{3,2,1,0:T(8,128)(2,1)S(1)}, bf16[2,1,128,256]{3,2,1,0:T(8,128)(2,1)S(1)}, u32[]{:S(2)}, u32[]{:S(2)}) collective-permute-start(bf16[2,1,128,256]{3,2,1,0:T(8,128)(2,1)S(1)} %get-tuple-element.38), channel_id=1, source_target_pairs={{0,1},{1,2},{2,3},{3,4},{4,5},{5,6},{6,7},{7,8},{8,9},{9,10},{10,1... | collective-permute-start | bytes 393224 | tf_op jit(solution)/shard_map/ppermute | solution.py:12
  64.4 9.9 %collective-permute-start.3 = (bf16[2,1,128,256]{3,2,1,0:T(8,128)(2,1)S(1)}, bf16[2,1,128,256]{3,2,1,0:T(8,128)(2,1)S(1)}, u32[]{:S(2)}, u32[]{:S(2)}) collective-permute-start(bf16[2,1,128,256]{3,2,1,0:T(8,128)(2,1)S(1)} %get-tuple-element.39), channel_id=1, source_target_pairs={{1,0},{2,1},{3,2},{4,3},{5,4},{6,5},{7,6},{8,7},{9,8},{10,9},{11,1... | collective-permute-start | bytes 393224 | tf_op jit(solution)/shard_map/ppermute | solution.py:15
  70.1 2.1 copy-start.22
  83.4 1.5 copy-start.2
  83.4 1.6 copy-start.5
  89.8 2.1 copy-start.14
  93.5 443.1 %all-to-all-start.1 = ((bf16[16,4,16,256]{3,2,1,0:T(8,128)(2,1)}), bf16[16,4,16,256]{3,2,1,0:T(8,128)(2,1)}, u32[]{:S(2)}, u32[]{:S(2)}) async-start(bf16[16,4,16,256]{3,2,1,0:T(8,128)(2,1)} %bitcast.28), calls=%async_computation.1 | async-start | bytes 1048576 | tf_op jit(solution)/shard_map/all_to_all | solution.py:69
  100.8 508.9 %reduce-scatter.10.cloned.1.call-start = ((), (), s32[]{:S(2)}) async-start(), calls=%async_computation.7 | async-start | bytes 147456
  530.7 167.9 %reduce-scatter.8.cloned.1.call-start = ((), (), s32[]{:S(2)}) async-start(), calls=%async_computation.6 | async-start | bytes 147456
  (11 other events, 10.6 us)
Sparse Core Ops, SparseCore 0:
  82.6 446.1 all-reduce.8
  533.8 75.8 reduce-scatter.9
  614.6 83.8 reduce-scatter.7
where the time goes:
time: 708 us; the launch traced here: 707 us
  waiting for transfers between devices  595 us (84%)
  starting transfers between devices  33.8 us (5%)
  matrix products  30.3 us (4%)
  local copies, waits for them, and re-layouts  28.5 us (4%)
  between operations  14.8 us (2%)
    unnamed x6, waiting for transfers between devices  587 us
    unnamed x60, local copies, waits for them, and re-layouts  17.4 us
  transfers between devices with their start and end apart: 11, of which 5 were waited for; matrix products, arithmetic and copies ran while one was open for 6% of the time, Pallas kernels for 0%

commit v1 on v0

v1 whole, which is shorter than its diff:
```python
import jax
import jax.numpy as jnp
from jax import lax
from jax.experimental import pallas as pl
from jax.experimental.pallas import tpu as pltpu
from jax.sharding import Mesh
from jax.sharding import PartitionSpec as P

F32 = jnp.float32
BF16 = jnp.bfloat16
C = 256
COLS = 128
ROWS = 4
PIX = ROWS * COLS
TAPS = 12
VMEM_LIMIT = 48 * 1024 * 1024


def mm(a, b):
    return jnp.dot(a, b, preferred_element_type=F32)


def mm_t(a, b):
    return lax.dot_general(a, b, (((1,), (1,)), ((), ())), preferred_element_type=F32)


def column(shape):
    return lax.broadcasted_iota(jnp.int32, shape, 0) % COLS


def from_left(field):
    return jnp.where(column(field.shape) == 0, 0.0, pltpu.roll(field, 1, 0))


def from_right(field):
    return jnp.where(
        column(field.shape) == COLS - 1, 0.0, pltpu.roll(field, field.shape[0] - 1, 0)
    )


def shifted_transposes(pixels):
    wide = pixels.astype(F32)
    return [
        from_left(wide).astype(BF16).T,
        pixels.T,
        from_right(wide).astype(BF16).T,
    ]


def call(kernel, out_shape, flops, nbytes, *args):
    return pl.pallas_call(
        kernel,
        out_shape=out_shape,
        in_specs=[pl.BlockSpec(memory_space=pltpu.VMEM)] * len(args),
        out_specs=jax.tree.map(lambda _: pl.BlockSpec(memory_space=pltpu.VMEM), out_shape),
        compiler_params=pltpu.CompilerParams(vmem_limit_bytes=VMEM_LIMIT),
        cost_estimate=pl.CostEstimate(flops=flops, bytes_accessed=nbytes, transcendentals=0),
    )(*args)


def shape(dims, dtype):
    return jax.ShapeDtypeStruct(dims, dtype)


TAP_FLOPS = 2 * 2 * PIX * C * C


def own_kernel(x, g, ws, wt, pm, pre_ref, gh_ref, xt_ref, gp_ref):
    for f in range(2):
        for j in range(3):
            mid = mm(x[f].reshape(PIX, C), ws[3 + j])
            up = mm(x[f, 0:3].reshape(3 * COLS, C), ws[j])
            down = mm(x[f, 1:4].reshape(3 * COLS, C), ws[6 + j])
            zero = jnp.zeros((COLS, C), F32)
            total = (
                mid + jnp.concatenate([zero, up], 0) + jnp.concatenate([down, zero], 0)
            )
            if j == 0:
                acc = from_left(total)
            elif j == 1:
                acc = acc + total
            else:
                acc = acc + from_right(total)
        pre_ref[f] = acc
        for j, t in enumerate(shifted_transposes(x[f].reshape(PIX, C))):
            xt_ref[j, f] = t
        gp_ref[f] = mm(g[f].reshape(PIX, C), pm[...]).astype(BF16)
    g0, g1 = g[0].reshape(PIX, C), g[1].reshape(PIX, C)
    gh_ref[0] = mm_t(g0, wt[2]) + mm_t(g1, wt[1])
    gh_ref[1] = mm_t(g1, wt[2])


def edge_kernel(pre, lo, hi, ws, gp, hid_ref, fac_ref, ht_ref, xe_ref, gt_ref):
    for f in range(2):
        low, high = lo[f, 0], hi[f, 0]
        top = from_left(mm(low, ws[0])) + mm(low, ws[1]) + from_right(mm(low, ws[2]))
        end = from_left(mm(high, ws[6])) + mm(high, ws[7]) + from_right(mm(high, ws[8]))
        value = jnp.concatenate(
            [
                pre[f, 0:COLS] + top,
                pre[f, COLS : 3 * COLS],
                pre[f, 3 * COLS :] + end,
            ],
            0,
        )
        sig = jax.nn.sigmoid(value)
        hidden = (value * sig).astype(BF16)
        hid_ref[f] = hidden.reshape(ROWS, COLS, C)
        fac_ref[f] = sig * (1.0 + value * (1.0 - sig))
        ht_ref[f] = hidden.T
        lows, highs = shifted_transposes(low), shifted_transposes(high)
        for j in range(3):
            xe_ref[j, f, 0] = lows[j]
            xe_ref[j, f, 1] = highs[j]
    gt_ref[0] = mm(ht_ref[0], gp[1])
    gt_ref[1] = mm(ht_ref[0], gp[0]) + mm(ht_ref[1], gp[1])


def grad_kernel(n0, n1, gh, fac, xt, xe, ht, gt, wt, pm, gpre_ref, keep_ref, send_ref):
    def store(tap, value):
        keep_ref[tap] = value[:, : C // 2]
        send_ref[tap] = value[:, C // 2 :].astype(BF16)

    a0, a1 = n0[0].reshape(PIX, C), n1[0].reshape(PIX, C)
    back0 = gh[0] + mm_t(a0, wt[0])
    back1 = gh[1] + mm_t(a0, wt[1]) + mm_t(a1, wt[0])
    grads = []
    for f, back in enumerate((back0, back1)):
        gpre = (back.astype(BF16).astype(F32) * fac[f]).astype(BF16)
        gpre_ref[f] = gpre.reshape(ROWS, COLS, C)
        grads.append(mm(gpre, pm[...]).astype(BF16))
    p0 = mm(a0, pm[...]).astype(BF16)
    p1 = mm(a1, pm[...]).astype(BF16)
    store(9, mm(ht[0], p0) + mm(ht[1], p1))
    store(10, gt[0] + mm(ht[1], p0))
    store(11, gt[1])
    for j in range(3):
        for i in range(3):
            total = None
            for f in range(2):
                own = xt[j, f]
                if i == 0:
                    own = jnp.concatenate([xe[j, f, 0], own[:, : 3 * COLS]], 1)
                elif i == 2:
                    own = jnp.concatenate([own[:, COLS:], xe[j, f, 1]], 1)
                part = mm(own, grads[f])
                total = part if total is None else total + part
            store(3 * i + j, total)


def pair_kernel(keep, got, out_ref):
    half = C // 4
    for p in range(TAPS // 2):
        s0 = keep[2 * p] + got[2 * p].astype(F32)
        s1 = keep[2 * p + 1] + got[2 * p + 1].astype(F32)
        low = jnp.concatenate([s0[:, :half], s1[:, :half]], 1).astype(BF16)
        high = jnp.concatenate([s0[:, half:], s1[:, half:]], 1).astype(BF16)
        for a in range(8):
            out_ref[2 * a, :, p * 128 : (p + 1) * 128] = low[32 * a : 32 * a + 32]
            out_ref[2 * a + 1, :, p * 128 : (p + 1) * 128] = high[32 * a : 32 * a + 32]


def plane_kernel(got, out_ref):
    total = got[0].astype(F32)
    for n in range(1, 16):
        total = total + got[n].astype(F32)
    pieces = []
    for p in range(TAPS // 2):
        flipped = total[:, p * 128 : (p + 1) * 128].T
        pieces += [flipped[:64], flipped[64:]]
    wide = jnp.concatenate(pieces, 1)
    for z in range(16):
        out_ref[z] = wide[4 * z : 4 * z + 4]


def last_kernel(got, gs_ref, gt_ref):
    total = got[0]
    for n in range(1, 16):
        total = total + got[n]
    for t in range(9):
        gs_ref[t] = total[:, 32 * t : 32 * t + 32]
    for t in range(3):
        gt_ref[t] = total[:, 32 * (9 + t) : 32 * (9 + t) + 32]


def out_kernel(hid, past, wt, out_ref):
    h0, h1 = hid[0].reshape(PIX, C), hid[1].reshape(PIX, C)
    p0, p1 = past[0].reshape(PIX, C), past[1].reshape(PIX, C)
    first = mm(p0, wt[0]) + mm(p1, wt[1]) + mm(h0, wt[2])
    out_ref[0] = first.astype(BF16).reshape(ROWS, COLS, C)
    second = mm(p1, wt[0]) + mm(h0, wt[1]) + mm(h1, wt[2])
    out_ref[1] = second.astype(BF16).reshape(ROWS, COLS, C)


def back_kernel(gpre, lo, hi, ws, out_ref):
    for f in range(2):
        own = gpre[f].reshape(PIX, C)
        after = jnp.concatenate([own[COLS:], hi[f, 0]], 0)
        before = jnp.concatenate([lo[f, 0], own[: 3 * COLS]], 0)
        sums = [
            mm_t(after, ws[j]) + mm_t(own, ws[3 + j]) + mm_t(before, ws[6 + j])
            for j in range(3)
        ]
        total = from_right(sums[0]) + sums[1] + from_left(sums[2])
        out_ref[f] = total.astype(BF16).reshape(ROWS, COLS, C)


SPACE = ("xl", "z", "c")


def steps(count):
    forward = [(i, i + 1) for i in range(count - 1)]
    return forward, [(b, a) for a, b in forward]


def edges(field):
    forward, backward = steps(64)
    low = lax.ppermute(field[:, ROWS - 1 :], SPACE, forward)
    high = lax.ppermute(field[:, :1], SPACE, backward)
    return low, high


def body(frames_in, w_space, w_time, grad_out):
    forward, backward = steps(8)
    row = lax.broadcasted_iota(jnp.int32, (C, C), 0)
    col = lax.broadcasted_iota(jnp.int32, (C, C), 1)
    core = (col // 128) ^ lax.axis_index("c")
    source = ((col % 128) // 64) * 128 + ((col % 64) // 4) * 8 + core * 4 + col % 4
    order = (row == source).astype(BF16)

    low, high = edges(frames_in)
    next0 = lax.ppermute(grad_out[:1], "tm", backward)
    next1 = lax.ppermute(grad_out[1:], "tm", backward)
    pre_part, gh_part, xt, gp = call(
        own_kernel,
        (
            shape((2, PIX, C), F32),
            shape((2, PIX, C), F32),
            shape((3, 2, C, PIX), BF16),
            shape((2, PIX, C), BF16),
        ),
        12 * TAP_FLOPS,
        8 << 20,
        frames_in, grad_out, w_space, w_time, order,
    )
    hidden, factor, ht, xe, gt_part = call(
        edge_kernel,
        (
            shape((2, ROWS, COLS, C), BF16),
            shape((2, PIX, C), F32),
            shape((2, C, PIX), BF16),
            shape((3, 2, 2, C, COLS), BF16),
            shape((2, C, C), F32),
        ),
        5 * TAP_FLOPS,
        8 << 20,
        pre_part, low, high, w_space, gp,
    )
    past = lax.ppermute(hidden, "tm", forward)
    grad_pre, keep, send = call(
        grad_kernel,
        (
            shape((2, ROWS, COLS, C), BF16),
            shape((TAPS, C, C // 2), F32),
            shape((TAPS, C, C // 2), BF16),
        ),
        15 * TAP_FLOPS,
        10 << 20,
        next0, next1, gh_part, factor, xt, xe, ht, gt_part, w_time, order,
    )
    got = lax.ppermute(send, "c", [(0, 1), (1, 0)])
    chunks = call(pair_kernel, shape((16, 32, 768), BF16), 1 << 20, 4 << 20, keep, got)
    chunks = lax.all_to_all(chunks, ("tm", "xl"), split_axis=0, concat_axis=0, tiled=True)
    rows = call(plane_kernel, shape((16, 4, 384), F32), 1 << 20, 1 << 20, chunks)
    rows = lax.all_to_all(rows, "z", split_axis=0, concat_axis=0, tiled=True)
    grad_space, grad_time = call(
        last_kernel, (shape((9, 4, 32), F32), shape((3, 4, 32), F32)), 1 << 16, 1 << 18, rows
    )
    block_out = call(
        out_kernel,
        shape((2, ROWS, COLS, C), BF16),
        3 * TAP_FLOPS,
        2 << 20,
        hidden, past, w_time,
    )
    g_low, g_high = edges(grad_pre)
    grad_in = call(
        back_kernel,
        shape((2, ROWS, COLS, C), BF16),
        9 * TAP_FLOPS,
        4 << 20,
        grad_pre, g_low, g_high, w_space,
    )
    return (
        block_out,
        grad_in,
        jnp.transpose(grad_space, (0, 2, 1)),
        jnp.transpose(grad_time, (0, 2, 1)),
    )


def solution(mesh):
    fine = Mesh(mesh.devices.reshape(8, 2, 16, 2), ("tm",) + SPACE)
    in_specs = (P("tm", SPACE, None, None), P(), P(), P("tm", SPACE, None, None))
    out_specs = (
        P("tm", SPACE, None, None),
        P("tm", SPACE, None, None),
        P(None, "tm", SPACE),
        P(None, "tm", SPACE),
    )
    return jax.shard_map(body, mesh=fine, in_specs=in_specs, out_specs=out_specs, check_vma=False)
```

time: 708 us -> 104 us (0.15)
  the two profiles are of different devices: /device:TPU:24 before, /device:TPU:30 now
where the time goes in v1:
time: 104 us; the launch traced here: 103 us
  starting transfers between devices  55.6 us (53%)
  waiting for transfers between devices  19.6 us (19%)
  Pallas kernels  16.6 us (16%)
  local copies, waits for them, and re-layouts  10.1 us (10%)
    ppermute x2, starting transfers between devices, edges(): high = lax.ppermute(field[:, :1], SPACE, backward)  24.5 us
    pallas_call x8, Pallas kernels, call(): pl.pallas_call(kernel, out_shape=out_shape, in_specs=[pl.BlockSpec(memory...  16.6 us
    all_to_all x1, waiting for transfers between devices, body(): lax.all_to_all(chunks, ('tm', 'xl'), split_axis=0, concat_axis=0, tiled=T...  10.9 us
    all_to_all x1, starting transfers between devices, body(): rows = lax.all_to_all(rows, 'z', split_axis=0, concat_axis=0, tiled=True)  10.9 us
    all_to_all x1, starting transfers between devices, body(): lax.all_to_all(chunks, ('tm', 'xl'), split_axis=0, concat_axis=0, tiled=T...  8.15 us
    unnamed x20, local copies, waits for them, and re-layouts  6.27 us
    ppermute x2, waiting for transfers between devices, edges(): low = lax.ppermute(field[:, ROWS - 1:], SPACE, forward)  5.93 us
    ppermute x2, starting transfers between devices, edges(): low = lax.ppermute(field[:, ROWS - 1:], SPACE, forward)  3.84 us
  transfers between devices with their start and end apart: 10, of which 4 were waited for; matrix products, arithmetic and copies ran while one was open for 2% of the time, Pallas kernels for 9%

profile of v1, /device:TPU:30, one launch (start us, length us, event | category | flops | bytes accessed | tf_op | source)
XLA Modules:
  0.0 102.8 jit_solution(7737469627289628514)
XLA Ops:
  0.7 1.8 %fusion.23 = (bf16[2,1,128,256]{3,2,1,0:T(8,128)(2,1)}, bf16[2,1,128,256]{3,2,1,0:T(8,128)(2,1)S(1)}) fusion(bf16[2,4,128,256]{3,2,1,0:T(8,128)(2,1)} %x.1), kind=kLoop, calls=%fused_computation.47 | loop fusion | bytes 524288 | tf_op jit(solution)/shard_map/slice | solution.py:219
  2.4 11.1 %collective-permute-start.1 = (bf16[2,1,128,256]{3,2,1,0:T(8,128)(2,1)}, bf16[2,1,128,256]{3,2,1,0:T(8,128)(2,1)S(1)}, u32[]{:S(2)}, u32[]{:S(2)}) collective-permute-start(bf16[2,1,128,256]{3,2,1,0:T(8,128)(2,1)} %get-tuple-element.36), channel_id=1, source_target_pairs={{1,0},{2,1},{3,2},{4,3},{5,4},{6,5},{7,6},{8,7},{9,8},{10,9},{11,1... | collective-permute-start | bytes 393224 | tf_op jit(solution)/shard_map/ppermute | solution.py:219
  13.5 1.9 %collective-permute-start = (bf16[2,1,128,256]{3,2,1,0:T(8,128)(2,1)S(1)}, bf16[2,1,128,256]{3,2,1,0:T(8,128)(2,1)S(1)}, u32[]{:S(2)}, u32[]{:S(2)}) collective-permute-start(bf16[2,1,128,256]{3,2,1,0:T(8,128)(2,1)S(1)} %get-tuple-element.37), channel_id=1, source_target_pairs={{0,1},{1,2},{2,3},{3,4},{4,5},{5,6},{6,7},{7,8},{8,9},{9,10},{10,1... | collective-permute-start | bytes 393224 | tf_op jit(solution)/shard_map/ppermute | solution.py:218
  15.5 1.1 %fusion.22 = (bf16[1,4,128,256]{3,2,1,0:T(8,128)(2,1)S(1)}, bf16[1,4,128,256]{3,2,1,0:T(8,128)(2,1)S(1)}) fusion(bf16[2,4,128,256]{3,2,1,0:T(8,128)(2,1)} %g.1), kind=kLoop, calls=%fused_computation.46 | loop fusion | bytes 1048576 | tf_op jit(solution)/shard_map/slice | solution.py:233
  16.5 2.7 %collective-permute-start.4 = (bf16[1,4,128,256]{3,2,1,0:T(8,128)(2,1)S(1)}, bf16[1,4,128,256]{3,2,1,0:T(8,128)(2,1)S(1)}, u32[]{:S(2)}, u32[]{:S(2)}) collective-permute-start(bf16[1,4,128,256]{3,2,1,0:T(8,128)(2,1)S(1)} %get-tuple-element.34), channel_id=1, source_target_pairs={{64,0},{128,64},{192,128},{256,192},{320,256},{384,320},{448,384},... | collective-permute-start | bytes 786440 | tf_op jit(solution)/shard_map/ppermute | solution.py:233
  19.2 2.4 %collective-permute-start.3 = (bf16[1,4,128,256]{3,2,1,0:T(8,128)(2,1)S(1)}, bf16[1,4,128,256]{3,2,1,0:T(8,128)(2,1)S(1)}, u32[]{:S(2)}, u32[]{:S(2)}) collective-permute-start(bf16[1,4,128,256]{3,2,1,0:T(8,128)(2,1)S(1)} %get-tuple-element.35), channel_id=1, source_target_pairs={{64,0},{128,64},{192,128},{256,192},{320,256},{384,320},{448,384},... | collective-permute-start | bytes 786440 | tf_op jit(solution)/shard_map/ppermute | solution.py:232
  22.7 1.0 %copy-done.6 = bf16[2,4,128,256]{3,2,1,0:T(8,128)(2,1)S(1)} copy-done((bf16[2,4,128,256]{3,2,1,0:T(8,128)(2,1)S(1)}, bf16[2,4,128,256]{3,2,1,0:T(8,128)(2,1)}, u32[]{:S(2)}) %copy-start.6) | copy-done | bytes 524312
  23.8 2.7 %shard_map.75 = (f32[2,512,256]{2,1,0:T(8,128)S(1)}, f32[2,512,256]{2,1,0:T(8,128)S(1)}, bf16[3,2,256,512]{3,2,1,0:T(8,128)(2,1)}, bf16[2,512,256]{2,1,0:T(8,128)(2,1)S(1)}) custom-call(bf16[2,4,128,256]{3,2,1,0:T(8,128)(2,1)S(1)} %copy-done.6, bf16[2,4,128,256]{3,2,1,0:T(8,128)(2,1)S(1)} %copy-done.3, bf16[9,256,256]{2,1,0:T(8,128)(2,1)S(1)} %copy-done.1, ...), custom_call_target="tpu_custom_call" | custom-call | flops 1610612736 | bytes 8388608 | tf_op jit(solution)/shard_map/pallas_call | solution.py:51
  26.5 2.2 %shard_map.76 = (bf16[2,4,128,256]{3,2,1,0:T(8,128)(2,1)S(1)}, f32[2,512,256]{2,1,0:T(8,128)S(1)}, bf16[2,256,512]{2,1,0:T(8,128)(2,1)S(1)}, bf16[3,2,2,256,128]{4,3,2,1,0:T(8,128)(2,1)S(1)}, f32[2,256,256]{2,1,0:T(8,128)S(1)}) custom-call(f32[2,512,256]{2,1,0:T(8,128)S(1)} %get-tuple-element.18.pre, bf16[2,1,128,256]{3,2,1,0:T(8,128)(2,1)S(1)} %collective-permute-done.lo, ...), custom_call_target="tpu_custom_call" | custom-call | flops 671088640 | bytes 8388608 | tf_op jit(solution)/shard_map/pallas_call | solution.py:51
  29.7 5.3 %shard_map.78 = (bf16[2,4,128,256]{3,2,1,0:T(8,128)(2,1)S(1)}, f32[12,256,128]{2,1,0:T(8,128)}, bf16[12,256,128]{2,1,0:T(8,128)(2,1)S(1)}) custom-call(bf16[1,4,128,256]{3,2,1,0:T(8,128)(2,1)S(1)} %collective-permute-done.3.n0, bf16[1,4,128,256]{3,2,1,0:T(8,128)(2,1)S(1)} %collective-permute-done.4.n1, f32[2,512,256]{2,1,0:T(8,128)S(1)} %get-tuple-element.21.gh, ...), custom_call_target="tpu_custom_call" | custom-call | flops 2013265920 | bytes 10485760 | tf_op jit(solution)/shard_map/pallas_call | solution.py:51
  35.8 1.9 %collective-permute-start.7 = (bf16[12,256,128]{2,1,0:T(8,128)(2,1)S(1)}, bf16[12,256,128]{2,1,0:T(8,128)(2,1)S(1)}, u32[]{:S(2)}, u32[]{:S(2)}) collective-permute-start(bf16[12,256,128]{2,1,0:T(8,128)(2,1)S(1)} %get-tuple-element.29), channel_id=1, source_target_pairs={{0,1},{1,0},{2,3},{3,2},{4,5},{5,4},{6,7},{7,6},{8,9},{9,8},{10,11... | collective-permute-start | bytes 2359304 | tf_op jit(solution)/shard_map/ppermute | solution.py:271
  37.7 2.3 %collective-permute-done.7.got = bf16[12,256,128]{2,1,0:T(8,128)(2,1)S(1)} collective-permute-done((bf16[12,256,128]{2,1,0:T(8,128)(2,1)S(1)}, bf16[12,256,128]{2,1,0:T(8,128)(2,1)S(1)}, u32[]{:S(2)}, u32[]{:S(2)}) %collective-permute-start.7) | collective-permute-done | bytes 786464 | tf_op jit(solution)/shard_map/ppermute | solution.py:271
  39.9 1.4 %copy-done = f32[12,256,128]{2,1,0:T(8,128)S(1)} copy-done((f32[12,256,128]{2,1,0:T(8,128)S(1)}, f32[12,256,128]{2,1,0:T(8,128)}, u32[]{:S(2)}) %copy-start) | copy-done | bytes 1572888
  41.4 1.2 %shard_map.80 = bf16[16,32,768]{2,1,0:T(8,128)(2,1)} custom-call(f32[12,256,128]{2,1,0:T(8,128)S(1)} %copy-done, bf16[12,256,128]{2,1,0:T(8,128)(2,1)S(1)} %collective-permute-done.7.got), custom_call_target="tpu_custom_call" | custom-call | flops 1048576 | bytes 4194304 | tf_op jit(solution)/shard_map/pallas_call | solution.py:51
  42.6 8.1 %all-to-all-start = ((bf16[16,32,768]{2,1,0:T(8,128)(2,1)}), bf16[16,32,768]{2,1,0:T(8,128)(2,1)S(1)}, u32[]{:S(2)}, u32[]{:S(2)}) async-start(bf16[16,32,768]{2,1,0:T(8,128)(2,1)} %shard_map.80), calls=%async_computation | async-start | bytes 1572864 | tf_op jit(solution)/shard_map/all_to_all | solution.py:273
  50.7 1.3 %collective-permute-start.2 = (bf16[2,4,128,256]{3,2,1,0:T(8,128)(2,1)S(1)}, bf16[2,4,128,256]{3,2,1,0:T(8,128)(2,1)S(1)}, u32[]{:S(2)}, u32[]{:S(2)}) collective-permute-start(bf16[2,4,128,256]{3,2,1,0:T(8,128)(2,1)S(1)} %get-tuple-element.20.hid), channel_id=1, source_target_pairs={{0,64},{64,128},{128,192},{192,256},{256,320},{320,384},{384,448},... | collective-permute-start | bytes 1572872 | tf_op jit(solution)/shard_map/ppermute | solution.py:259
  52.0 10.9 %all-to-all-done.got = bf16[16,32,768]{2,1,0:T(8,128)(2,1)S(1)} async-done(((bf16[16,32,768]{2,1,0:T(8,128)(2,1)}), bf16[16,32,768]{2,1,0:T(8,128)(2,1)S(1)}, u32[]{:S(2)}, u32[]{:S(2)}) %all-to-all-start) | async-done | bytes 786464 | tf_op jit(solution)/shard_map/all_to_all | solution.py:273
  63.8 10.9 %all-to-all-start.1 = ((f32[16,4,384]{2,1,0:T(4,128)}), f32[16,4,384]{2,1,0:T(4,128)S(1)}, u32[]{:S(2)}, u32[]{:S(2)}) async-start(f32[16,4,384]{2,1,0:T(4,128)} %shard_map.81), calls=%async_computation.1 | async-start | bytes 196608 | tf_op jit(solution)/shard_map/all_to_all | solution.py:275
  75.7 13.4 %collective-permute-start.6 = (bf16[2,1,128,256]{3,2,1,0:T(8,128)(2,1)S(1)}, bf16[2,1,128,256]{3,2,1,0:T(8,128)(2,1)S(1)}, u32[]{:S(2)}, u32[]{:S(2)}) collective-permute-start(bf16[2,1,128,256]{3,2,1,0:T(8,128)(2,1)S(1)} %get-tuple-element.32), channel_id=1, source_target_pairs={{1,0},{2,1},{3,2},{4,3},{5,4},{6,5},{7,6},{8,7},{9,8},{10,9},{11,1... | collective-permute-start | bytes 393224 | tf_op jit(solution)/shard_map/ppermute | solution.py:219
  89.1 1.9 %collective-permute-start.5 = (bf16[2,1,128,256]{3,2,1,0:T(8,128)(2,1)S(1)}, bf16[2,1,128,256]{3,2,1,0:T(8,128)(2,1)S(1)}, u32[]{:S(2)}, u32[]{:S(2)}) collective-permute-start(bf16[2,1,128,256]{3,2,1,0:T(8,128)(2,1)S(1)} %get-tuple-element.33), channel_id=1, source_target_pairs={{0,1},{1,2},{2,3},{3,4},{4,5},{5,6},{6,7},{7,8},{8,9},{9,10},{10,1... | collective-permute-start | bytes 393224 | tf_op jit(solution)/shard_map/ppermute | solution.py:218
  91.6 5.9 %collective-permute-done.5.lo = bf16[2,1,128,256]{3,2,1,0:T(8,128)(2,1)S(1)} collective-permute-done((bf16[2,1,128,256]{3,2,1,0:T(8,128)(2,1)S(1)}, bf16[2,1,128,256]{3,2,1,0:T(8,128)(2,1)S(1)}, u32[]{:S(2)}, u32[]{:S(2)}) %collective-permute-start.5) | collective-permute-done | bytes 131104 | tf_op jit(solution)/shard_map/ppermute | solution.py:218
  97.5 1.0 %copy-done.8 = bf16[2,4,128,256]{3,2,1,0:T(8,128)(2,1)S(1)} copy-done((bf16[2,4,128,256]{3,2,1,0:T(8,128)(2,1)S(1)}, bf16[2,4,128,256]{3,2,1,0:T(8,128)(2,1)}, u32[]{:S(2)}) %copy-start.8) | copy-done | bytes 524312
  98.6 2.2 %shard_map.79 = bf16[2,4,128,256]{3,2,1,0:T(8,128)(2,1)} custom-call(bf16[2,4,128,256]{3,2,1,0:T(8,128)(2,1)S(1)} %copy-done.8, bf16[2,1,128,256]{3,2,1,0:T(8,128)(2,1)S(1)} %collective-permute-done.5.lo, bf16[2,1,128,256]{3,2,1,0:T(8,128)(2,1)S(1)} %collective-permute-done.6.hi, bf16[9,256,256]{2,1,0:T(8,128)(2,1)S(1)} %copy-done.2), custom_call_target="tpu_custom_call" | custom-call | flops 1207959552 | bytes 4194304 | tf_op jit(solution)/shard_map/pallas_call | solution.py:51
  100.8 1.4 %shard_map.77 = bf16[2,4,128,256]{3,2,1,0:T(8,128)(2,1)} custom-call(bf16[2,4,128,256]{3,2,1,0:T(8,128)(2,1)S(1)} %get-tuple-element.20.hid, bf16[2,4,128,256]{3,2,1,0:T(8,128)(2,1)S(1)} %collective-permute-done.2.past, bf16[3,256,256]{2,1,0:T(8,128)(2,1)S(1)} %copy-done.5), custom_call_target="tpu_custom_call" | custom-call | flops 402653184 | bytes 2097152 | tf_op jit(solution)/shard_map/pallas_call | solution.py:51
  (34 shorter events, 6.1 us)
Async XLA Ops:
  0.6 21.1 %copy-start.3 = (bf16[2,4,128,256]{3,2,1,0:T(8,128)(2,1)S(1)}, bf16[2,4,128,256]{3,2,1,0:T(8,128)(2,1)}, u32[]{:S(2)}) copy-start(bf16[2,4,128,256]{3,2,1,0:T(8,128)(2,1)} %g.1) | copy-start | bytes 1572868
  0.6 21.1 %copy-start.1 = (bf16[9,256,256]{2,1,0:T(8,128)(2,1)S(1)}, bf16[9,256,256]{2,1,0:T(8,128)(2,1)}, u32[]{:S(2)}) copy-start(bf16[9,256,256]{2,1,0:T(8,128)(2,1)} %ws.5) | copy-start | bytes 3538948
  2.4 24.1 %collective-permute-start.1 = (bf16[2,1,128,256]{3,2,1,0:T(8,128)(2,1)}, bf16[2,1,128,256]{3,2,1,0:T(8,128)(2,1)S(1)}, u32[]{:S(2)}, u32[]{:S(2)}) collective-permute-start(bf16[2,1,128,256]{3,2,1,0:T(8,128)(2,1)} %get-tuple-element.36), channel_id=1, source_target_pairs={{1,0},{2,1},{3,2},{4,3},{5,4},{6,5},{7,6},{8,7},{9,8},{10,9},{11,1... | collective-permute-start | bytes 393224 | tf_op jit(solution)/shard_map/ppermute | solution.py:219
  13.5 13.0 %collective-permute-start = (bf16[2,1,128,256]{3,2,1,0:T(8,128)(2,1)S(1)}, bf16[2,1,128,256]{3,2,1,0:T(8,128)(2,1)S(1)}, u32[]{:S(2)}, u32[]{:S(2)}) collective-permute-start(bf16[2,1,128,256]{3,2,1,0:T(8,128)(2,1)S(1)} %get-tuple-element.37), channel_id=1, source_target_pairs={{0,1},{1,2},{2,3},{3,4},{4,5},{5,6},{6,7},{7,8},{8,9},{9,10},{10,1... | collective-permute-start | bytes 393224 | tf_op jit(solution)/shard_map/ppermute | solution.py:218
  16.5 13.2 %collective-permute-start.4 = (bf16[1,4,128,256]{3,2,1,0:T(8,128)(2,1)S(1)}, bf16[1,4,128,256]{3,2,1,0:T(8,128)(2,1)S(1)}, u32[]{:S(2)}, u32[]{:S(2)}) collective-permute-start(bf16[1,4,128,256]{3,2,1,0:T(8,128)(2,1)S(1)} %get-tuple-element.34), channel_id=1, source_target_pairs={{64,0},{128,64},{192,128},{256,192},{320,256},{384,320},{448,384},... | collective-permute-start | bytes 786440 | tf_op jit(solution)/shard_map/ppermute | solution.py:233
  19.2 10.5 %collective-permute-start.3 = (bf16[1,4,128,256]{3,2,1,0:T(8,128)(2,1)S(1)}, bf16[1,4,128,256]{3,2,1,0:T(8,128)(2,1)S(1)}, u32[]{:S(2)}, u32[]{:S(2)}) collective-permute-start(bf16[1,4,128,256]{3,2,1,0:T(8,128)(2,1)S(1)} %get-tuple-element.35), channel_id=1, source_target_pairs={{64,0},{128,64},{192,128},{256,192},{320,256},{384,320},{448,384},... | collective-permute-start | bytes 786440 | tf_op jit(solution)/shard_map/ppermute | solution.py:232
  21.7 1.0 copy-start.4
  22.7 1.0 %copy-start.6 = (bf16[2,4,128,256]{3,2,1,0:T(8,128)(2,1)S(1)}, bf16[2,4,128,256]{3,2,1,0:T(8,128)(2,1)}, u32[]{:S(2)}) copy-start(bf16[2,4,128,256]{3,2,1,0:T(8,128)(2,1)} %x.1) | copy-start | bytes 1572868
  26.5 3.2 %copy-start.5 = (bf16[3,256,256]{2,1,0:T(8,128)(2,1)S(1)}, bf16[3,256,256]{2,1,0:T(8,128)(2,1)}, u32[]{:S(2)}) copy-start(bf16[3,256,256]{2,1,0:T(8,128)(2,1)} %wt.5) | copy-start | bytes 1179652
  28.7 1.0 copy-start.9
  35.0 0.8 copy-start.7
  35.8 4.2 %collective-permute-start.7 = (bf16[12,256,128]{2,1,0:T(8,128)(2,1)S(1)}, bf16[12,256,128]{2,1,0:T(8,128)(2,1)S(1)}, u32[]{:S(2)}, u32[]{:S(2)}) collective-permute-start(bf16[12,256,128]{2,1,0:T(8,128)(2,1)S(1)} %get-tuple-element.29), channel_id=1, source_target_pairs={{0,1},{1,0},{2,3},{3,2},{4,5},{5,4},{6,7},{7,6},{8,9},{9,8},{10,11... | collective-permute-start | bytes 2359304 | tf_op jit(solution)/shard_map/ppermute | solution.py:271
  39.9 1.4 %copy-start = (f32[12,256,128]{2,1,0:T(8,128)S(1)}, f32[12,256,128]{2,1,0:T(8,128)}, u32[]{:S(2)}) copy-start(f32[12,256,128]{2,1,0:T(8,128)} %get-tuple-element.28.keep) | copy-start | bytes 4718596
  42.6 54.9 %copy-start.2 = (bf16[9,256,256]{2,1,0:T(8,128)(2,1)S(1)}, bf16[9,256,256]{2,1,0:T(8,128)(2,1)}, u32[]{:S(2)}) copy-start(bf16[9,256,256]{2,1,0:T(8,128)(2,1)} %ws.5) | copy-start | bytes 3538948
  42.6 20.3 %all-to-all-start = ((bf16[16,32,768]{2,1,0:T(8,128)(2,1)}), bf16[16,32,768]{2,1,0:T(8,128)(2,1)S(1)}, u32[]{:S(2)}, u32[]{:S(2)}) async-start(bf16[16,32,768]{2,1,0:T(8,128)(2,1)} %shard_map.80), calls=%async_computation | async-start | bytes 1572864 | tf_op jit(solution)/shard_map/all_to_all | solution.py:273
  50.7 50.1 %collective-permute-start.2 = (bf16[2,4,128,256]{3,2,1,0:T(8,128)(2,1)S(1)}, bf16[2,4,128,256]{3,2,1,0:T(8,128)(2,1)S(1)}, u32[]{:S(2)}, u32[]{:S(2)}) collective-permute-start(bf16[2,4,128,256]{3,2,1,0:T(8,128)(2,1)S(1)} %get-tuple-element.20.hid), channel_id=1, source_target_pairs={{0,64},{64,128},{128,192},{192,256},{256,320},{320,384},{384,448},... | collective-permute-start | bytes 1572872 | tf_op jit(solution)/shard_map/ppermute | solution.py:259
  63.8 38.4 %all-to-all-start.1 = ((f32[16,4,384]{2,1,0:T(4,128)}), f32[16,4,384]{2,1,0:T(4,128)S(1)}, u32[]{:S(2)}, u32[]{:S(2)}) async-start(f32[16,4,384]{2,1,0:T(4,128)} %shard_map.81), calls=%async_computation.1 | async-start | bytes 196608 | tf_op jit(solution)/shard_map/all_to_all | solution.py:275
  75.7 15.9 %collective-permute-start.6 = (bf16[2,1,128,256]{3,2,1,0:T(8,128)(2,1)S(1)}, bf16[2,1,128,256]{3,2,1,0:T(8,128)(2,1)S(1)}, u32[]{:S(2)}, u32[]{:S(2)}) collective-permute-start(bf16[2,1,128,256]{3,2,1,0:T(8,128)(2,1)S(1)} %get-tuple-element.32), channel_id=1, source_target_pairs={{1,0},{2,1},{3,2},{4,3},{5,4},{6,5},{7,6},{8,7},{9,8},{10,9},{11,1... | collective-permute-start | bytes 393224 | tf_op jit(solution)/shard_map/ppermute | solution.py:219
  89.1 8.4 %collective-permute-start.5 = (bf16[2,1,128,256]{3,2,1,0:T(8,128)(2,1)S(1)}, bf16[2,1,128,256]{3,2,1,0:T(8,128)(2,1)S(1)}, u32[]{:S(2)}, u32[]{:S(2)}) collective-permute-start(bf16[2,1,128,256]{3,2,1,0:T(8,128)(2,1)S(1)} %get-tuple-element.33), channel_id=1, source_target_pairs={{0,1},{1,2},{2,3},{3,4},{4,5},{5,6},{6,7},{7,8},{8,9},{9,10},{10,1... | collective-permute-start | bytes 393224 | tf_op jit(solution)/shard_map/ppermute | solution.py:218
  97.5 1.0 %copy-start.8 = (bf16[2,4,128,256]{3,2,1,0:T(8,128)(2,1)S(1)}, bf16[2,4,128,256]{3,2,1,0:T(8,128)(2,1)}, u32[]{:S(2)}) copy-start(bf16[2,4,128,256]{3,2,1,0:T(8,128)(2,1)} %copy-done.7) | copy-start | bytes 1572868

commit v2 on v1

--- a/solution.py
+++ b/solution.py
@@ -13,7 +13,7 @@
 ROWS = 4
 PIX = ROWS * COLS
 TAPS = 12
-VMEM_LIMIT = 48 * 1024 * 1024
+VMEM_LIMIT = 16 * 1024 * 1024
 
 
 def mm(a, b):
@@ -47,11 +47,15 @@
     ]
 
 
+def place(arg):
+    return pltpu.SMEM if arg.dtype == jnp.int32 else pltpu.VMEM
+
+
 def call(kernel, out_shape, flops, nbytes, *args):
     return pl.pallas_call(
         kernel,
         out_shape=out_shape,
-        in_specs=[pl.BlockSpec(memory_space=pltpu.VMEM)] * len(args),
+        in_specs=[pl.BlockSpec(memory_space=place(arg)) for arg in args],
         out_specs=jax.tree.map(lambda _: pl.BlockSpec(memory_space=pltpu.VMEM), out_shape),
         compiler_params=pltpu.CompilerParams(vmem_limit_bytes=VMEM_LIMIT),
         cost_estimate=pl.CostEstimate(flops=flops, bytes_accessed=nbytes, transcendentals=0),
@@ -63,6 +67,40 @@
 
 
 TAP_FLOPS = 2 * 2 * PIX * C * C
+
+
+def send_kernel(core, x, g, pair_ref, chip_ref, g0_ref, g1_ref, sems):
+    c = core[0]
+    copies = [
+        pltpu.make_async_copy(g.at[0:1], g0_ref, sems.at[0]),
+        pltpu.make_async_copy(g.at[1:2], g1_ref, sems.at[1]),
+        pltpu.make_async_copy(x.at[:, pl.ds(3 - 3 * c, 1)], pair_ref, sems.at[2]),
+        pltpu.make_async_copy(x.at[:, pl.ds(3 * c, 1)], chip_ref, sems.at[3]),
+    ]
+    for copy in copies:
+        copy.start()
+    for copy in copies:
+        copy.wait()
+
+
+def first_sends(core, x, g):
+    rows = shape((2, 1, COLS, C), BF16)
+    frame = shape((1, ROWS, COLS, C), BF16)
+    whole = pl.BlockSpec(memory_space=pl.ANY)
+    return pl.pallas_call(
+        send_kernel,
+        out_shape=(rows, rows, frame, frame),
+        in_specs=[pl.BlockSpec(memory_space=pltpu.SMEM), whole, whole],
+        out_specs=[pl.BlockSpec(memory_space=pltpu.VMEM)] * 4,
+        scratch_shapes=[pltpu.SemaphoreType.DMA((4,))],
+        compiler_params=pltpu.CompilerParams(vmem_limit_bytes=VMEM_LIMIT),
+        cost_estimate=pl.CostEstimate(flops=0, bytes_accessed=2 << 20, transcendentals=0),
+    )(core, x, g)
+
+
+def low_high(core, pair, chip):
+    first = core[0] == 0
+    return jnp.where(first, chip, pair), jnp.where(first, pair, chip)
 
 
 def own_kernel(x, g, ws, wt, pm, pre_ref, gh_ref, xt_ref, gp_ref):
@@ -90,9 +128,9 @@
     gh_ref[1] = mm_t(g1, wt[2])
 
 
-def edge_kernel(pre, lo, hi, ws, gp, hid_ref, fac_ref, ht_ref, xe_ref, gt_ref):
+def edge_kernel(core, pre, pair, chip, ws, gp, hid_ref, fac_ref, ht_ref, xe_ref, gt_ref):
     for f in range(2):
-        low, high = lo[f, 0], hi[f, 0]
+        low, high = low_high(core, pair[f, 0], chip[f, 0])
         top = from_left(mm(low, ws[0])) + mm(low, ws[1]) + from_right(mm(low, ws[2]))
         end = from_left(mm(high, ws[6])) + mm(high, ws[7]) + from_right(mm(high, ws[8]))
         value = jnp.concatenate(
@@ -116,7 +154,9 @@
     gt_ref[1] = mm(ht_ref[0], gp[0]) + mm(ht_ref[1], gp[1])
 
 
-def grad_kernel(n0, n1, gh, fac, xt, xe, ht, gt, wt, pm, gpre_ref, keep_ref, send_ref):
+def grad_kernel(
+    core, n0, n1, gh, fac, xt, xe, ht, gt, wt, pm, gpre_ref, pair_ref, chip_ref, keep_ref, send_ref
+):
     def store(tap, value):
         keep_ref[tap] = value[:, : C // 2]
         send_ref[tap] = value[:, C // 2 :].astype(BF16)
@@ -128,6 +168,8 @@
     for f, back in enumerate((back0, back1)):
         gpre = (back.astype(BF16).astype(F32) * fac[f]).astype(BF16)
         gpre_ref[f] = gpre.reshape(ROWS, COLS, C)
+        pair_ref[f, 0] = gpre_ref[f, 3 - 3 * core[0]]
+        chip_ref[f, 0] = gpre_ref[f, 3 * core[0]]
         grads.append(mm(gpre, pm[...]).astype(BF16))
     p0 = mm(a0, pm[...]).astype(BF16)
     p1 = mm(a1, pm[...]).astype(BF16)
@@ -192,11 +234,12 @@
     out_ref[1] = second.astype(BF16).reshape(ROWS, COLS, C)
 
 
-def back_kernel(gpre, lo, hi, ws, out_ref):
+def back_kernel(core, gpre, pair, chip, ws, out_ref):
     for f in range(2):
+        low, high = low_high(core, pair[f, 0], chip[f, 0])
         own = gpre[f].reshape(PIX, C)
-        after = jnp.concatenate([own[COLS:], hi[f, 0]], 0)
-        before = jnp.concatenate([lo[f, 0], own[: 3 * COLS]], 0)
+        after = jnp.concatenate([own[COLS:], high], 0)
+        before = jnp.concatenate([low, own[: 3 * COLS]], 0)
         sums = [
             mm_t(after, ws[j]) + mm_t(own, ws[3 + j]) + mm_t(before, ws[6 + j])
             for j in range(3)
@@ -213,24 +256,26 @@
     return forward, [(b, a) for a, b in forward]
 
 
-def edges(field):
-    forward, backward = steps(64)
-    low = lax.ppermute(field[:, ROWS - 1 :], SPACE, forward)
-    high = lax.ppermute(field[:, :1], SPACE, backward)
-    return low, high
+def edges(pair, chip):
+    across = [(i, i + 1) for i in range(1, 63, 2)]
+    pair = lax.ppermute(pair, "c", [(0, 1), (1, 0)])
+    chip = lax.ppermute(chip, SPACE, across + [(b, a) for a, b in across])
+    return pair, chip
 
 
 def body(frames_in, w_space, w_time, grad_out):
     forward, backward = steps(8)
     row = lax.broadcasted_iota(jnp.int32, (C, C), 0)
     col = lax.broadcasted_iota(jnp.int32, (C, C), 1)
-    core = (col // 128) ^ lax.axis_index("c")
-    source = ((col % 128) // 64) * 128 + ((col % 64) // 4) * 8 + core * 4 + col % 4
+    side = (col // 128) ^ lax.axis_index("c")
+    source = ((col % 128) // 64) * 128 + ((col % 64) // 4) * 8 + side * 4 + col % 4
     order = (row == source).astype(BF16)
 
-    low, high = edges(frames_in)
-    next0 = lax.ppermute(grad_out[:1], "tm", backward)
-    next1 = lax.ppermute(grad_out[1:], "tm", backward)
+    core = lax.axis_index("c").reshape(1)
+    pair, chip, g0, g1 = first_sends(core, frames_in, grad_out)
+    next0 = lax.ppermute(g0, "tm", backward)
+    next1 = lax.ppermute(g1, "tm", backward)
+    pair, chip = edges(pair, chip)
     pre_part, gh_part, xt, gp = call(
         own_kernel,
         (
@@ -254,28 +299,26 @@
         ),
         5 * TAP_FLOPS,
         8 << 20,
-        pre_part, low, high, w_space, gp,
+        core, pre_part, pair, chip, w_space, gp,
     )
     past = lax.ppermute(hidden, "tm", forward)
-    grad_pre, keep, send = call(
+    rows = shape((2, 1, COLS, C), BF16)
+    grad_pre, pair, chip, keep, send = call(
         grad_kernel,
         (
             shape((2, ROWS, COLS, C), BF16),
+            rows,
+            rows,
             shape((TAPS, C, C // 2), F32),
             shape((TAPS, C, C // 2), BF16),
         ),
         15 * TAP_FLOPS,
         10 << 20,
-        next0, next1, gh_part, factor, xt, xe, ht, gt_part, w_time, order,
+        core, next0, next1, gh_part, factor, xt, xe, ht, gt_part, w_time, order,
     )
     got = lax.ppermute(send, "c", [(0, 1), (1, 0)])
     chunks = call(pair_kernel, shape((16, 32, 768), BF16), 1 << 20, 4 << 20, keep, got)
     chunks = lax.all_to_all(chunks, ("tm", "xl"), split_axis=0, concat_axis=0, tiled=True)
-    rows = call(plane_kernel, shape((16, 4, 384), F32), 1 << 20, 1 << 20, chunks)
-    rows = lax.all_to_all(rows, "z", split_axis=0, concat_axis=0, tiled=True)
-    grad_space, grad_time = call(
-        last_kernel, (shape((9, 4, 32), F32), shape((3, 4, 32), F32)), 1 << 16, 1 << 18, rows
-    )
     block_out = call(
         out_kernel,
         shape((2, ROWS, COLS, C), BF16),
@@ -283,13 +326,19 @@
         2 << 20,
         hidden, past, w_time,
     )
-    g_low, g_high = edges(grad_pre)
+    pair, chip = edges(pair, chip)
     grad_in = call(
         back_kernel,
         shape((2, ROWS, COLS, C), BF16),
         9 * TAP_FLOPS,
         4 << 20,
-        grad_pre, g_low, g_high, w_space,
+        core, grad_pre, pair, chip, w_space,
+    )
+    chunks, grad_in = lax.optimization_barrier((chunks, grad_in))
+    rows = call(plane_kernel, shape((16, 4, 384), F32), 1 << 20, 1 << 20, chunks)
+    rows = lax.all_to_all(rows, "z", split_axis=0, concat_axis=0, tiled=True)
+    grad_space, grad_time = call(
+        last_kernel, (shape((9, 4, 32), F32), shape((3, 4, 32), F32)), 1 << 16, 1 << 18, rows
     )
     return (
         block_out,

time: 104 us -> 85.7 us (0.82)
  the two profiles are of different devices: /device:TPU:30 before, /device:TPU:24 now
where the time goes in v2:
time: 85.7 us; the launch traced here: 84.9 us
  starting transfers between devices  40.3 us (47%)
  waiting for transfers between devices  25.8 us (30%)
  Pallas kernels  11.6 us (14%)
  local copies, waits for them, and re-layouts  6.17 us (7%)
  between operations  0.88 us (1%)
    all_to_all x1, waiting for transfers between devices, body(): rows = lax.all_to_all(rows, 'z', split_axis=0, concat_axis=0, tiled=True)  12.4 us
    all_to_all x1, starting transfers between devices, body(): rows = lax.all_to_all(rows, 'z', split_axis=0, concat_axis=0, tiled=True)  11.4 us
    pallas_call x8, Pallas kernels, call(): pl.pallas_call(kernel, out_shape=out_shape, in_specs=[pl.BlockSpec(memory...  11.4 us
    all_to_all x1, starting transfers between devices, body(): lax.all_to_all(chunks, ('tm', 'xl'), split_axis=0, concat_axis=0, tiled=T...  9.8 us
    ppermute x1, waiting for transfers between devices, body(): next1 = lax.ppermute(g1, 'tm', backward)  7.02 us
    unnamed x16, local copies, waits for them, and re-layouts  6.17 us
    ppermute x1, starting transfers between devices, body(): past = lax.ppermute(hidden, 'tm', forward)  4.88 us
    ppermute x1, starting transfers between devices, body(): got = lax.ppermute(send, 'c', [(0, 1), (1, 0)])  4.09 us
  transfers between devices with their start and end apart: 10, of which 5 were waited for; matrix products, arithmetic and copies ran while one was open for 0% of the time, Pallas kernels for 8%

profile of v2, /device:TPU:24, one launch (start us, length us, event | category | flops | bytes accessed | tf_op | source)
XLA Modules:
  0.0 84.9 jit_solution(8539729426829029628)
XLA Ops:
  0.6 1.0 %copy-done.2 = bf16[2,4,128,256]{3,2,1,0:T(8,128)(2,1)S(1)} copy-done((bf16[2,4,128,256]{3,2,1,0:T(8,128)(2,1)S(1)}, bf16[2,4,128,256]{3,2,1,0:T(8,128)(2,1)}, u32[]{:S(2)}) %copy-start.2) | copy-done | bytes 524312
  1.7 1.0 %copy-done.3 = bf16[2,4,128,256]{3,2,1,0:T(8,128)(2,1)S(1)} copy-done((bf16[2,4,128,256]{3,2,1,0:T(8,128)(2,1)S(1)}, bf16[2,4,128,256]{3,2,1,0:T(8,128)(2,1)}, u32[]{:S(2)}) %copy-start.3) | copy-done | bytes 524312
  3.0 1.9 %collective-permute-start = (bf16[2,1,128,256]{3,2,1,0:T(8,128)(2,1)S(1)}, bf16[2,1,128,256]{3,2,1,0:T(8,128)(2,1)S(1)}, u32[]{:S(2)}, u32[]{:S(2)}) collective-permute-start(bf16[2,1,128,256]{3,2,1,0:T(8,128)(2,1)S(1)} %get-tuple-element.27), channel_id=1, source_target_pairs={{0,1},{1,0},{2,3},{3,2},{4,5},{5,4},{6,7},{7,6},{8,9},{9,8},{10,11... | collective-permute-start | bytes 393224 | tf_op jit(solution)/shard_map/ppermute | solution.py:261
  5.6 2.7 %collective-permute-start.3 = (bf16[1,4,128,256]{3,2,1,0:T(8,128)(2,1)S(1)}, bf16[1,4,128,256]{3,2,1,0:T(8,128)(2,1)S(1)}, u32[]{:S(2)}, u32[]{:S(2)}) collective-permute-start(bf16[1,4,128,256]{3,2,1,0:T(8,128)(2,1)S(1)} %get-tuple-element.31), channel_id=1, source_target_pairs={{64,0},{128,64},{192,128},{256,192},{320,256},{384,320},{448,384},... | collective-permute-start | bytes 786440 | tf_op jit(solution)/shard_map/ppermute | solution.py:276
  8.2 2.4 %collective-permute-start.4 = (bf16[1,4,128,256]{3,2,1,0:T(8,128)(2,1)S(1)}, bf16[1,4,128,256]{3,2,1,0:T(8,128)(2,1)S(1)}, u32[]{:S(2)}, u32[]{:S(2)}) collective-permute-start(bf16[1,4,128,256]{3,2,1,0:T(8,128)(2,1)S(1)} %get-tuple-element.32), channel_id=1, source_target_pairs={{64,0},{128,64},{192,128},{256,192},{320,256},{384,320},{448,384},... | collective-permute-start | bytes 786440 | tf_op jit(solution)/shard_map/ppermute | solution.py:277
  10.7 1.3 %copy-done = bf16[9,256,256]{2,1,0:T(8,128)(2,1)S(1)} copy-done((bf16[9,256,256]{2,1,0:T(8,128)(2,1)S(1)}, bf16[9,256,256]{2,1,0:T(8,128)(2,1)}, u32[]{:S(2)}) %copy-start) | copy-done | bytes 1179672
  12.0 1.0 %copy-done.4 = bf16[3,256,256]{2,1,0:T(8,128)(2,1)S(1)} copy-done((bf16[3,256,256]{2,1,0:T(8,128)(2,1)S(1)}, bf16[3,256,256]{2,1,0:T(8,128)(2,1)}, u32[]{:S(2)}) %copy-start.4) | copy-done | bytes 393240
  13.0 1.6 %shard_map.75 = (f32[2,512,256]{2,1,0:T(8,128)S(1)}, f32[2,512,256]{2,1,0:T(8,128)S(1)}, bf16[3,2,256,512]{3,2,1,0:T(8,128)(2,1)S(1)}, bf16[2,512,256]{2,1,0:T(8,128)(2,1)S(1)}) custom-call(bf16[2,4,128,256]{3,2,1,0:T(8,128)(2,1)S(1)} %copy-done.2, bf16[2,4,128,256]{3,2,1,0:T(8,128)(2,1)S(1)} %copy-done.3, bf16[9,256,256]{2,1,0:T(8,128)(2,1)S(1)} %copy-done, ...), custom_call_target="tpu_custom_call" | custom-call | flops 1610612736 | bytes 8388608 | tf_op jit(solution)/shard_map/pallas_call | solution.py:55
  15.5 2.3 %collective-permute-done.3.n0 = bf16[1,4,128,256]{3,2,1,0:T(8,128)(2,1)S(1)} collective-permute-done((bf16[1,4,128,256]{3,2,1,0:T(8,128)(2,1)S(1)}, bf16[1,4,128,256]{3,2,1,0:T(8,128)(2,1)S(1)}, u32[]{:S(2)}, u32[]{:S(2)}) %collective-permute-start.3) | collective-permute-done | bytes 262176 | tf_op jit(solution)/shard_map/ppermute | solution.py:276
  17.9 7.0 %collective-permute-done.4.n1 = bf16[1,4,128,256]{3,2,1,0:T(8,128)(2,1)S(1)} collective-permute-done((bf16[1,4,128,256]{3,2,1,0:T(8,128)(2,1)S(1)}, bf16[1,4,128,256]{3,2,1,0:T(8,128)(2,1)S(1)}, u32[]{:S(2)}, u32[]{:S(2)}) %collective-permute-start.4) | collective-permute-done | bytes 262176 | tf_op jit(solution)/shard_map/ppermute | solution.py:277
  24.9 2.4 %shard_map.79 = (bf16[2,4,128,256]{3,2,1,0:T(8,128)(2,1)S(1)}, bf16[2,1,128,256]{3,2,1,0:T(8,128)(2,1)}, bf16[2,1,128,256]{3,2,1,0:T(8,128)(2,1)S(1)}, f32[12,25...) custom-call(s32[1]{0:T(128)} %bitcast.core, bf16[1,4,128,256]{3,2,1,0:T(8,128)(2,1)S(1)} %collective-permute-done.3.n0, ...), custom_call_target="tpu_custom_call" | custom-call | flops 2013265920 | bytes 10485760 | tf_op jit(solution)/shard_map/pallas_call | solution.py:55
  28.1 4.1 %collective-permute-start.5 = (bf16[12,256,128]{2,1,0:T(8,128)(2,1)S(1)}, bf16[12,256,128]{2,1,0:T(8,128)(2,1)S(1)}, u32[]{:S(2)}, u32[]{:S(2)}) collective-permute-start(bf16[12,256,128]{2,1,0:T(8,128)(2,1)S(1)} %get-tuple-element.40), channel_id=1, source_target_pairs={{0,1},{1,0},{2,3},{3,2},{4,5},{5,4},{6,7},{7,6},{8,9},{9,8},{10,11... | collective-permute-start | bytes 2359304 | tf_op jit(solution)/shard_map/ppermute | solution.py:319
  32.2 1.9 %collective-permute-done.5.got = bf16[12,256,128]{2,1,0:T(8,128)(2,1)S(1)} collective-permute-done((bf16[12,256,128]{2,1,0:T(8,128)(2,1)S(1)}, bf16[12,256,128]{2,1,0:T(8,128)(2,1)S(1)}, u32[]{:S(2)}, u32[]{:S(2)}) %collective-permute-start.5) | collective-permute-done | bytes 786464 | tf_op jit(solution)/shard_map/ppermute | solution.py:319
  34.1 1.2 %shard_map.80 = bf16[16,32,768]{2,1,0:T(8,128)(2,1)} custom-call(f32[12,256,128]{2,1,0:T(8,128)S(1)} %get-tuple-element.39.keep, bf16[12,256,128]{2,1,0:T(8,128)(2,1)S(1)} %collective-permute-done.5.got), custom_call_target="tpu_custom_call" | custom-call | flops 1048576 | bytes 4194304 | tf_op jit(solution)/shard_map/pallas_call | solution.py:55
  35.4 9.8 %all-to-all-start = ((bf16[16,32,768]{2,1,0:T(8,128)(2,1)}), bf16[16,32,768]{2,1,0:T(8,128)(2,1)S(1)}, u32[]{:S(2)}, u32[]{:S(2)}) async-start(bf16[16,32,768]{2,1,0:T(8,128)(2,1)} %shard_map.80), calls=%async_computation | async-start | bytes 1572864 | tf_op jit(solution)/shard_map/all_to_all | solution.py:321
  45.1 1.9 %collective-permute-start.6 = (bf16[2,1,128,256]{3,2,1,0:T(8,128)(2,1)}, bf16[2,1,128,256]{3,2,1,0:T(8,128)(2,1)S(1)}, u32[]{:S(2)}, u32[]{:S(2)}) collective-permute-start(bf16[2,1,128,256]{3,2,1,0:T(8,128)(2,1)} %get-tuple-element.42), channel_id=1, source_target_pairs={{0,1},{1,0},{2,3},{3,2},{4,5},{5,4},{6,7},{7,6},{8,9},{9,8},{10,11... | collective-permute-start | bytes 393224 | tf_op jit(solution)/shard_map/ppermute | solution.py:261
  47.7 4.9 %collective-permute-start.2 = (bf16[2,4,128,256]{3,2,1,0:T(8,128)(2,1)S(1)}, bf16[2,4,128,256]{3,2,1,0:T(8,128)(2,1)S(1)}, u32[]{:S(2)}, u32[]{:S(2)}) collective-permute-start(bf16[2,4,128,256]{3,2,1,0:T(8,128)(2,1)S(1)} %get-tuple-element.30.hid), channel_id=1, source_target_pairs={{0,64},{64,128},{128,192},{192,256},{256,320},{320,384},{384,448},... | collective-permute-start | bytes 1572872 | tf_op jit(solution)/shard_map/ppermute | solution.py:304
  52.7 1.0 %copy-done.7 = bf16[2,4,128,256]{3,2,1,0:T(8,128)(2,1)S(1)} copy-done((bf16[2,4,128,256]{3,2,1,0:T(8,128)(2,1)S(1)}, bf16[2,4,128,256]{3,2,1,0:T(8,128)(2,1)}, u32[]{:S(2)}) %copy-start.7) | copy-done | bytes 524312
  53.7 2.2 %shard_map.81 = bf16[2,4,128,256]{3,2,1,0:T(8,128)(2,1)} custom-call(s32[1]{0:T(128)} %bitcast.core, bf16[2,4,128,256]{3,2,1,0:T(8,128)(2,1)S(1)} %copy-done.7, bf16[2,1,128,256]{3,2,1,0:T(8,128)(2,1)S(1)} %collective-permute-done.6.pair, bf16[2,1,128,256]{3,2,1,0:T(8,128)(2,1)S(1)} %collective-permute-done.7.chip, bf16[9,256,256]{2,1,0:T(8,128)(2,1)S(1)} %copy-done.1), custom_call_target="tpu_custom_call" | custom-call | flops 1207959552 | bytes 4194304 | tf_op jit(solution)/shard_map/pallas_call | solution.py:55
  55.9 2.1 %all-to-all-done.got = bf16[16,32,768]{2,1,0:T(8,128)(2,1)S(1)} async-done(((bf16[16,32,768]{2,1,0:T(8,128)(2,1)}), bf16[16,32,768]{2,1,0:T(8,128)(2,1)S(1)}, u32[]{:S(2)}, u32[]{:S(2)}) %all-to-all-start) | async-done | bytes 786464 | tf_op jit(solution)/shard_map/all_to_all | solution.py:321
  58.0 0.9 %shard_map.82 = f32[16,4,384]{2,1,0:T(4,128)} custom-call(bf16[16,32,768]{2,1,0:T(8,128)(2,1)S(1)} %all-to-all-done.got), custom_call_target="tpu_custom_call" | custom-call | flops 1048576 | bytes 1048576 | tf_op jit(solution)/shard_map/pallas_call | solution.py:55
  59.0 11.4 %all-to-all-start.1 = ((f32[16,4,384]{2,1,0:T(4,128)}), f32[16,4,384]{2,1,0:T(4,128)S(1)}, u32[]{:S(2)}, u32[]{:S(2)}) async-start(f32[16,4,384]{2,1,0:T(4,128)} %shard_map.82), calls=%async_computation.1 | async-start | bytes 196608 | tf_op jit(solution)/shard_map/all_to_all | solution.py:339
  70.4 1.4 %shard_map.78 = bf16[2,4,128,256]{3,2,1,0:T(8,128)(2,1)} custom-call(bf16[2,4,128,256]{3,2,1,0:T(8,128)(2,1)S(1)} %get-tuple-element.30.hid, bf16[2,4,128,256]{3,2,1,0:T(8,128)(2,1)S(1)} %collective-permute-done.2.past, bf16[3,256,256]{2,1,0:T(8,128)(2,1)S(1)} %copy-done.5), custom_call_target="tpu_custom_call" | custom-call | flops 402653184 | bytes 2097152 | tf_op jit(solution)/shard_map/pallas_call | solution.py:55
  71.8 12.4 %all-to-all-done.1.got = f32[16,4,384]{2,1,0:T(4,128)S(1)} async-done(((f32[16,4,384]{2,1,0:T(4,128)}), f32[16,4,384]{2,1,0:T(4,128)S(1)}, u32[]{:S(2)}, u32[]{:S(2)}) %all-to-all-start.1) | async-done | bytes 98336 | tf_op jit(solution)/shard_map/all_to_all | solution.py:339
  (28 shorter events, 4.1 us)
Async XLA Ops:
  0.6 1.0 %copy-start.2 = (bf16[2,4,128,256]{3,2,1,0:T(8,128)(2,1)S(1)}, bf16[2,4,128,256]{3,2,1,0:T(8,128)(2,1)}, u32[]{:S(2)}) copy-start(bf16[2,4,128,256]{3,2,1,0:T(8,128)(2,1)} %x.3) | copy-start | bytes 1572868
  1.7 1.0 %copy-start.3 = (bf16[2,4,128,256]{3,2,1,0:T(8,128)(2,1)S(1)}, bf16[2,4,128,256]{3,2,1,0:T(8,128)(2,1)}, u32[]{:S(2)}) copy-start(bf16[2,4,128,256]{3,2,1,0:T(8,128)(2,1)} %g.3) | copy-start | bytes 1572868
  3.0 11.6 %collective-permute-start = (bf16[2,1,128,256]{3,2,1,0:T(8,128)(2,1)S(1)}, bf16[2,1,128,256]{3,2,1,0:T(8,128)(2,1)S(1)}, u32[]{:S(2)}, u32[]{:S(2)}) collective-permute-start(bf16[2,1,128,256]{3,2,1,0:T(8,128)(2,1)S(1)} %get-tuple-element.27), channel_id=1, source_target_pairs={{0,1},{1,0},{2,3},{3,2},{4,5},{5,4},{6,7},{7,6},{8,9},{9,8},{10,11... | collective-permute-start | bytes 393224 | tf_op jit(solution)/shard_map/ppermute | solution.py:261
  4.9 9.7 %collective-permute-start.1 = (bf16[2,1,128,256]{3,2,1,0:T(8,128)(2,1)S(1)}, bf16[2,1,128,256]{3,2,1,0:T(8,128)(2,1)S(1)}, u32[]{:S(2)}, u32[]{:S(2)}) collective-permute-start(bf16[2,1,128,256]{3,2,1,0:T(8,128)(2,1)S(1)} %get-tuple-element.28), channel_id=1, source_target_pairs={{1,2},{3,4},{5,6},{7,8},{9,10},{11,12},{13,14},{15,16},{17,18},{19... | collective-permute-start | bytes 393224 | tf_op jit(solution)/shard_map/ppermute | solution.py:262
  5.6 12.3 %collective-permute-start.3 = (bf16[1,4,128,256]{3,2,1,0:T(8,128)(2,1)S(1)}, bf16[1,4,128,256]{3,2,1,0:T(8,128)(2,1)S(1)}, u32[]{:S(2)}, u32[]{:S(2)}) collective-permute-start(bf16[1,4,128,256]{3,2,1,0:T(8,128)(2,1)S(1)} %get-tuple-element.31), channel_id=1, source_target_pairs={{64,0},{128,64},{192,128},{256,192},{320,256},{384,320},{448,384},... | collective-permute-start | bytes 786440 | tf_op jit(solution)/shard_map/ppermute | solution.py:276
  8.2 16.7 %collective-permute-start.4 = (bf16[1,4,128,256]{3,2,1,0:T(8,128)(2,1)S(1)}, bf16[1,4,128,256]{3,2,1,0:T(8,128)(2,1)S(1)}, u32[]{:S(2)}, u32[]{:S(2)}) collective-permute-start(bf16[1,4,128,256]{3,2,1,0:T(8,128)(2,1)S(1)} %get-tuple-element.32), channel_id=1, source_target_pairs={{64,0},{128,64},{192,128},{256,192},{320,256},{384,320},{448,384},... | collective-permute-start | bytes 786440 | tf_op jit(solution)/shard_map/ppermute | solution.py:277
  10.7 1.3 %copy-start = (bf16[9,256,256]{2,1,0:T(8,128)(2,1)S(1)}, bf16[9,256,256]{2,1,0:T(8,128)(2,1)}, u32[]{:S(2)}) copy-start(bf16[9,256,256]{2,1,0:T(8,128)(2,1)} %ws.5) | copy-start | bytes 3538948
  12.0 1.0 %copy-start.4 = (bf16[3,256,256]{2,1,0:T(8,128)(2,1)S(1)}, bf16[3,256,256]{2,1,0:T(8,128)(2,1)}, u32[]{:S(2)}) copy-start(bf16[3,256,256]{2,1,0:T(8,128)(2,1)} %wt.5) | copy-start | bytes 1179652
  13.0 1.6 %copy-start.1 = (bf16[9,256,256]{2,1,0:T(8,128)(2,1)S(1)}, bf16[9,256,256]{2,1,0:T(8,128)(2,1)}, u32[]{:S(2)}) copy-start(bf16[9,256,256]{2,1,0:T(8,128)(2,1)} %ws.5) | copy-start | bytes 3538948
  14.6 10.3 %copy-start.5 = (bf16[3,256,256]{2,1,0:T(8,128)(2,1)S(1)}, bf16[3,256,256]{2,1,0:T(8,128)(2,1)}, u32[]{:S(2)}) copy-start(bf16[3,256,256]{2,1,0:T(8,128)(2,1)} %wt.5) | copy-start | bytes 1179652
  27.3 0.8 copy-start.6
  28.1 6.0 %collective-permute-start.5 = (bf16[12,256,128]{2,1,0:T(8,128)(2,1)S(1)}, bf16[12,256,128]{2,1,0:T(8,128)(2,1)S(1)}, u32[]{:S(2)}, u32[]{:S(2)}) collective-permute-start(bf16[12,256,128]{2,1,0:T(8,128)(2,1)S(1)} %get-tuple-element.40), channel_id=1, source_target_pairs={{0,1},{1,0},{2,3},{3,2},{4,5},{5,4},{6,7},{7,6},{8,9},{9,8},{10,11... | collective-permute-start | bytes 2359304 | tf_op jit(solution)/shard_map/ppermute | solution.py:319
  35.4 22.7 %all-to-all-start = ((bf16[16,32,768]{2,1,0:T(8,128)(2,1)}), bf16[16,32,768]{2,1,0:T(8,128)(2,1)S(1)}, u32[]{:S(2)}, u32[]{:S(2)}) async-start(bf16[16,32,768]{2,1,0:T(8,128)(2,1)} %shard_map.80), calls=%async_computation | async-start | bytes 1572864 | tf_op jit(solution)/shard_map/all_to_all | solution.py:321
  45.1 7.5 %collective-permute-start.6 = (bf16[2,1,128,256]{3,2,1,0:T(8,128)(2,1)}, bf16[2,1,128,256]{3,2,1,0:T(8,128)(2,1)S(1)}, u32[]{:S(2)}, u32[]{:S(2)}) collective-permute-start(bf16[2,1,128,256]{3,2,1,0:T(8,128)(2,1)} %get-tuple-element.42), channel_id=1, source_target_pairs={{0,1},{1,0},{2,3},{3,2},{4,5},{5,4},{6,7},{7,6},{8,9},{9,8},{10,11... | collective-permute-start | bytes 393224 | tf_op jit(solution)/shard_map/ppermute | solution.py:261
  47.1 5.6 %collective-permute-start.7 = (bf16[2,1,128,256]{3,2,1,0:T(8,128)(2,1)S(1)}, bf16[2,1,128,256]{3,2,1,0:T(8,128)(2,1)S(1)}, u32[]{:S(2)}, u32[]{:S(2)}) collective-permute-start(bf16[2,1,128,256]{3,2,1,0:T(8,128)(2,1)S(1)} %get-tuple-element.43), channel_id=1, source_target_pairs={{1,2},{3,4},{5,6},{7,8},{9,10},{11,12},{13,14},{15,16},{17,18},{19... | collective-permute-start | bytes 393224 | tf_op jit(solution)/shard_map/ppermute | solution.py:262
  47.7 22.7 %collective-permute-start.2 = (bf16[2,4,128,256]{3,2,1,0:T(8,128)(2,1)S(1)}, bf16[2,4,128,256]{3,2,1,0:T(8,128)(2,1)S(1)}, u32[]{:S(2)}, u32[]{:S(2)}) collective-permute-start(bf16[2,4,128,256]{3,2,1,0:T(8,128)(2,1)S(1)} %get-tuple-element.30.hid), channel_id=1, source_target_pairs={{0,64},{64,128},{128,192},{192,256},{256,320},{320,384},{384,448},... | collective-permute-start | bytes 1572872 | tf_op jit(solution)/shard_map/ppermute | solution.py:304
  52.6 1.0 %copy-start.7 = (bf16[2,4,128,256]{3,2,1,0:T(8,128)(2,1)S(1)}, bf16[2,4,128,256]{3,2,1,0:T(8,128)(2,1)}, u32[]{:S(2)}) copy-start(bf16[2,4,128,256]{3,2,1,0:T(8,128)(2,1)} %copy-done.6) | copy-start | bytes 1572868
  59.0 25.2 %all-to-all-start.1 = ((f32[16,4,384]{2,1,0:T(4,128)}), f32[16,4,384]{2,1,0:T(4,128)S(1)}, u32[]{:S(2)}, u32[]{:S(2)}) async-start(f32[16,4,384]{2,1,0:T(4,128)} %shard_map.82), calls=%async_computation.1 | async-start | bytes 196608 | tf_op jit(solution)/shard_map/all_to_all | solution.py:339

commit v3 on v2

--- a/solution.py
+++ b/solution.py
@@ -14,6 +14,7 @@
 PIX = ROWS * COLS
 TAPS = 12
 VMEM_LIMIT = 16 * 1024 * 1024
+HINT = 1 << 33
 
 
 def mm(a, b):
@@ -51,12 +52,22 @@
     return pltpu.SMEM if arg.dtype == jnp.int32 else pltpu.VMEM
 
 
-def call(kernel, out_shape, flops, nbytes, *args):
+def call(kernel, out_shape, flops, nbytes, *args, hbm_in=(), hbm_out=(), scratch=()):
+    flat, tree = jax.tree.flatten(out_shape)
+    out_specs = [
+        pl.BlockSpec(memory_space=pltpu.HBM if n in hbm_out else pltpu.VMEM)
+        for n in range(len(flat))
+    ]
+    in_specs = [
+        pl.BlockSpec(memory_space=pltpu.HBM if n in hbm_in else place(arg))
+        for n, arg in enumerate(args)
+    ]
     return pl.pallas_call(
         kernel,
         out_shape=out_shape,
-        in_specs=[pl.BlockSpec(memory_space=place(arg)) for arg in args],
-        out_specs=jax.tree.map(lambda _: pl.BlockSpec(memory_space=pltpu.VMEM), out_shape),
+        in_specs=in_specs,
+        out_specs=jax.tree.unflatten(tree, out_specs),
+        scratch_shapes=list(scratch),
         compiler_params=pltpu.CompilerParams(vmem_limit_bytes=VMEM_LIMIT),
         cost_estimate=pl.CostEstimate(flops=flops, bytes_accessed=nbytes, transcendentals=0),
     )(*args)
@@ -69,13 +80,18 @@
 TAP_FLOPS = 2 * 2 * PIX * C * C
 
 
-def send_kernel(core, x, g, pair_ref, chip_ref, g0_ref, g1_ref, sems):
-    c = core[0]
+def order_kernel(core, out_ref):
+    row = lax.broadcasted_iota(jnp.int32, (C, C), 0)
+    col = lax.broadcasted_iota(jnp.int32, (C, C), 1)
+    side = (col // 128) ^ core[0]
+    source = ((col % 128) // 64) * 128 + ((col % 64) // 4) * 8 + side * 4 + col % 4
+    out_ref[...] = jnp.where(row == source, 1.0, 0.0).astype(BF16)
+
+
+def piece_kernel(g, pm, g0_ref, g1_ref, sems):
     copies = [
         pltpu.make_async_copy(g.at[0:1], g0_ref, sems.at[0]),
         pltpu.make_async_copy(g.at[1:2], g1_ref, sems.at[1]),
-        pltpu.make_async_copy(x.at[:, pl.ds(3 - 3 * c, 1)], pair_ref, sems.at[2]),
-        pltpu.make_async_copy(x.at[:, pl.ds(3 * c, 1)], chip_ref, sems.at[3]),
     ]
     for copy in copies:
         copy.start()
@@ -83,19 +99,15 @@
         copy.wait()
 
 
-def first_sends(core, x, g):
-    rows = shape((2, 1, COLS, C), BF16)
-    frame = shape((1, ROWS, COLS, C), BF16)
-    whole = pl.BlockSpec(memory_space=pl.ANY)
-    return pl.pallas_call(
-        send_kernel,
-        out_shape=(rows, rows, frame, frame),
-        in_specs=[pl.BlockSpec(memory_space=pltpu.SMEM), whole, whole],
-        out_specs=[pl.BlockSpec(memory_space=pltpu.VMEM)] * 4,
-        scratch_shapes=[pltpu.SemaphoreType.DMA((4,))],
-        compiler_params=pltpu.CompilerParams(vmem_limit_bytes=VMEM_LIMIT),
-        cost_estimate=pl.CostEstimate(flops=0, bytes_accessed=2 << 20, transcendentals=0),
-    )(core, x, g)
+def first_kernel(core, x, g, wt, pm, gh_ref, gp_ref, pair_ref, chip_ref):
+    c = core[0]
+    for f in range(2):
+        pair_ref[f, 0] = x[f, 3 - 3 * c]
+        chip_ref[f, 0] = x[f, 3 * c]
+        gp_ref[f] = mm(g[f].reshape(PIX, C), pm[...]).astype(BF16)
+    g0, g1 = g[0].reshape(PIX, C), g[1].reshape(PIX, C)
+    gh_ref[0] = mm_t(g0, wt[2]) + mm_t(g1, wt[1])
+    gh_ref[1] = mm_t(g1, wt[2])
 
 
 def low_high(core, pair, chip):
@@ -103,7 +115,7 @@
     return jnp.where(first, chip, pair), jnp.where(first, pair, chip)
 
 
-def own_kernel(x, g, ws, wt, pm, pre_ref, gh_ref, xt_ref, gp_ref):
+def own_kernel(x, ws, pre_ref, xt_ref):
     for f in range(2):
         for j in range(3):
             mid = mm(x[f].reshape(PIX, C), ws[3 + j])
@@ -122,10 +134,6 @@
         pre_ref[f] = acc
         for j, t in enumerate(shifted_transposes(x[f].reshape(PIX, C))):
             xt_ref[j, f] = t
-        gp_ref[f] = mm(g[f].reshape(PIX, C), pm[...]).astype(BF16)
-    g0, g1 = g[0].reshape(PIX, C), g[1].reshape(PIX, C)
-    gh_ref[0] = mm_t(g0, wt[2]) + mm_t(g1, wt[1])
-    gh_ref[1] = mm_t(g1, wt[2])
 
 
 def edge_kernel(core, pre, pair, chip, ws, gp, hid_ref, fac_ref, ht_ref, xe_ref, gt_ref):
@@ -155,7 +163,9 @@
 
 
 def grad_kernel(
-    core, n0, n1, gh, fac, xt, xe, ht, gt, wt, pm, gpre_ref, pair_ref, chip_ref, keep_ref, send_ref
+    core, n0, n1, gh, fac, xt, xe, ht, gt, wt, pm,
+    gpre_hbm, pair_ref, chip_ref, keep_ref, send_ref,
+    gpre_ref, sem,
 ):
     def store(tap, value):
         keep_ref[tap] = value[:, : C // 2]
@@ -171,6 +181,8 @@
         pair_ref[f, 0] = gpre_ref[f, 3 - 3 * core[0]]
         chip_ref[f, 0] = gpre_ref[f, 3 * core[0]]
         grads.append(mm(gpre, pm[...]).astype(BF16))
+    copy = pltpu.make_async_copy(gpre_ref, gpre_hbm, sem)
+    copy.start()
     p0 = mm(a0, pm[...]).astype(BF16)
     p1 = mm(a1, pm[...]).astype(BF16)
     store(9, mm(ht[0], p0) + mm(ht[1], p1))
@@ -188,6 +200,7 @@
                 part = mm(own, grads[f])
                 total = part if total is None else total + part
             store(3 * i + j, total)
+    copy.wait()
 
 
 def pair_kernel(keep, got, out_ref):
@@ -258,35 +271,37 @@
 
 def edges(pair, chip):
     across = [(i, i + 1) for i in range(1, 63, 2)]
+    chip = lax.ppermute(chip, SPACE, across + [(b, a) for a, b in across])
     pair = lax.ppermute(pair, "c", [(0, 1), (1, 0)])
-    chip = lax.ppermute(chip, SPACE, across + [(b, a) for a, b in across])
     return pair, chip
 
 
 def body(frames_in, w_space, w_time, grad_out):
     forward, backward = steps(8)
-    row = lax.broadcasted_iota(jnp.int32, (C, C), 0)
-    col = lax.broadcasted_iota(jnp.int32, (C, C), 1)
-    side = (col // 128) ^ lax.axis_index("c")
-    source = ((col % 128) // 64) * 128 + ((col % 64) // 4) * 8 + side * 4 + col % 4
-    order = (row == source).astype(BF16)
-
     core = lax.axis_index("c").reshape(1)
-    pair, chip, g0, g1 = first_sends(core, frames_in, grad_out)
+    order = call(order_kernel, shape((C, C), BF16), HINT, 1 << 17, core)
+    frame = shape((1, ROWS, COLS, C), BF16)
+    rows = shape((2, 1, COLS, C), BF16)
+    g0, g1 = call(
+        piece_kernel, (frame, frame), 0, 1 << 20, grad_out, order,
+        hbm_in=(0,), scratch=[pltpu.SemaphoreType.DMA((2,))],
+    )
     next0 = lax.ppermute(g0, "tm", backward)
     next1 = lax.ppermute(g1, "tm", backward)
+    gh_part, gp, pair, chip = call(
+        first_kernel,
+        (shape((2, PIX, C), F32), shape((2, PIX, C), BF16), rows, rows),
+        4 * TAP_FLOPS,
+        4 << 20,
+        core, frames_in, grad_out, w_time, order,
+    )
     pair, chip = edges(pair, chip)
-    pre_part, gh_part, xt, gp = call(
+    pre_part, xt = call(
         own_kernel,
-        (
-            shape((2, PIX, C), F32),
-            shape((2, PIX, C), F32),
-            shape((3, 2, C, PIX), BF16),
-            shape((2, PIX, C), BF16),
-        ),
-        12 * TAP_FLOPS,
-        8 << 20,
-        frames_in, grad_out, w_space, w_time, order,
+        (shape((2, PIX, C), F32), shape((3, 2, C, PIX), BF16)),
+        9 * TAP_FLOPS,
+        4 << 20,
+        frames_in, w_space,
     )
     hidden, factor, ht, xe, gt_part = call(
         edge_kernel,
@@ -301,8 +316,6 @@
         8 << 20,
         core, pre_part, pair, chip, w_space, gp,
     )
-    past = lax.ppermute(hidden, "tm", forward)
-    rows = shape((2, 1, COLS, C), BF16)
     grad_pre, pair, chip, keep, send = call(
         grad_kernel,
         (
@@ -315,10 +328,15 @@
         15 * TAP_FLOPS,
         10 << 20,
         core, next0, next1, gh_part, factor, xt, xe, ht, gt_part, w_time, order,
+        hbm_out=(0,),
+        scratch=[pltpu.VMEM((2, ROWS, COLS, C), BF16), pltpu.SemaphoreType.DMA],
     )
     got = lax.ppermute(send, "c", [(0, 1), (1, 0)])
     chunks = call(pair_kernel, shape((16, 32, 768), BF16), 1 << 20, 4 << 20, keep, got)
     chunks = lax.all_to_all(chunks, ("tm", "xl"), split_axis=0, concat_axis=0, tiled=True)
+    pair, chip = edges(pair, chip)
+    chunks, pair, chip, hidden = lax.optimization_barrier((chunks, pair, chip, hidden))
+    past = lax.ppermute(hidden, "tm", forward)
     block_out = call(
         out_kernel,
         shape((2, ROWS, COLS, C), BF16),
@@ -326,7 +344,6 @@
         2 << 20,
         hidden, past, w_time,
     )
-    pair, chip = edges(pair, chip)
     grad_in = call(
         back_kernel,
         shape((2, ROWS, COLS, C), BF16),
@@ -334,9 +351,9 @@
         4 << 20,
         core, grad_pre, pair, chip, w_space,
     )
-    chunks, grad_in = lax.optimization_barrier((chunks, grad_in))
     rows = call(plane_kernel, shape((16, 4, 384), F32), 1 << 20, 1 << 20, chunks)
     rows = lax.all_to_all(rows, "z", split_axis=0, concat_axis=0, tiled=True)
+    rows, block_out = lax.optimization_barrier((rows, block_out))
     grad_space, grad_time = call(
         last_kernel, (shape((9, 4, 32), F32), shape((3, 4, 32), F32)), 1 << 16, 1 << 18, rows
     )

time: 85.7 us -> 82.8 us (0.966)
  starting transfers between devices: 40.3 us -> 36.9 us
  waiting for transfers between devices: 25.8 us -> 28.2 us
  local copies, waits for them, and re-layouts: 6.17 us -> 4.37 us
    all_to_all x1, waiting for transfers between devices: 2.13 us -> 9 us  [body(): lax.all_to_all(chunks, ('tm', 'xl'), split_axis=0, concat_axis=0, tiled=T...]
    all_to_all x1, waiting for transfers between devices: 12.4 us -> 7.6 us  [body(): rows = lax.all_to_all(rows, 'z', split_axis=0, concat_axis=0, tiled=True)]
    ppermute x1, waiting for transfers between devices: 7.02 us -> 4.47 us  [body(): next1 = lax.ppermute(g1, 'tm', backward)]
    ppermute x1, starting transfers between devices: 4.09 us -> 1.91 us  [body(): got = lax.ppermute(send, 'c', [(0, 1), (1, 0)])]
    all_to_all x1, starting transfers between devices: 11.4 us -> 9.44 us  [body(): rows = lax.all_to_all(rows, 'z', split_axis=0, concat_axis=0, tiled=True)]
    ppermute x1, waiting for transfers between devices: 2.35 us -> 4.28 us  [body(): next0 = lax.ppermute(g0, 'tm', backward)]
    unnamed x16, local copies, waits for them, and re-layouts: 6.17 us -> 4.37 us
    all_to_all x1, starting transfers between devices: 9.8 us -> 11.2 us  [body(): lax.all_to_all(chunks, ('tm', 'xl'), split_axis=0, concat_axis=0, tiled=T...]
  transfers between devices with their start and end apart: 10 -> 10, of which waited for: 5 -> 6; matrix products, arithmetic and copies ran while one was open for 0% -> 0% of each run, Pallas kernels for 8% -> 9%
where the time goes in v3:
time: 82.8 us; the launch traced here: 82.3 us
  starting transfers between devices  36.9 us (45%)
  waiting for transfers between devices  28.2 us (34%)
  Pallas kernels  11.9 us (14%)
  local copies, waits for them, and re-layouts  4.37 us (5%)
  between operations  0.84 us (1%)
    pallas_call x11, Pallas kernels, call(): pl.pallas_call(kernel, out_shape=out_shape, in_specs=in_specs, out_specs=...  11.9 us
    all_to_all x1, starting transfers between devices, body(): lax.all_to_all(chunks, ('tm', 'xl'), split_axis=0, concat_axis=0, tiled=T...  11.2 us
    all_to_all x1, starting transfers between devices, body(): rows = lax.all_to_all(rows, 'z', split_axis=0, concat_axis=0, tiled=True)  9.44 us
    all_to_all x1, waiting for transfers between devices, body(): lax.all_to_all(chunks, ('tm', 'xl'), split_axis=0, concat_axis=0, tiled=T...  9 us
    all_to_all x1, waiting for transfers between devices, body(): rows = lax.all_to_all(rows, 'z', split_axis=0, concat_axis=0, tiled=True)  7.6 us
    ppermute x1, waiting for transfers between devices, body(): next1 = lax.ppermute(g1, 'tm', backward)  4.47 us
    unnamed x16, local copies, waits for them, and re-layouts  4.37 us
    ppermute x1, waiting for transfers between devices, body(): next0 = lax.ppermute(g0, 'tm', backward)  4.28 us
  transfers between devices with their start and end apart: 10, of which 6 were waited for; matrix products, arithmetic and copies ran while one was open for 0% of the time, Pallas kernels for 9%

profile of v3, /device:TPU:24, one launch (start us, length us, event | category | flops | bytes accessed | tf_op | source)
XLA Modules:
  0.0 82.3 jit_solution(10049420570562776564)
XLA Ops:
  0.7 1.0 %copy-done.1 = bf16[2,4,128,256]{3,2,1,0:T(8,128)(2,1)S(1)} copy-done((bf16[2,4,128,256]{3,2,1,0:T(8,128)(2,1)S(1)}, bf16[2,4,128,256]{3,2,1,0:T(8,128)(2,1)}, u32[]{:S(2)}) %copy-start.1) | copy-done | bytes 524312
  1.7 2.8 %collective-permute-start = (bf16[1,4,128,256]{3,2,1,0:T(8,128)(2,1)S(1)}, bf16[1,4,128,256]{3,2,1,0:T(8,128)(2,1)S(1)}, u32[]{:S(2)}, u32[]{:S(2)}) collective-permute-start(bf16[1,4,128,256]{3,2,1,0:T(8,128)(2,1)S(1)} %get-tuple-element.30), channel_id=1, source_target_pairs={{64,0},{128,64},{192,128},{256,192},{320,256},{384,320},{448,384},... | collective-permute-start | bytes 786440 | tf_op jit(solution)/shard_map/ppermute | solution.py:289
  4.5 2.4 %collective-permute-start.1 = (bf16[1,4,128,256]{3,2,1,0:T(8,128)(2,1)S(1)}, bf16[1,4,128,256]{3,2,1,0:T(8,128)(2,1)S(1)}, u32[]{:S(2)}, u32[]{:S(2)}) collective-permute-start(bf16[1,4,128,256]{3,2,1,0:T(8,128)(2,1)S(1)} %get-tuple-element.31), channel_id=1, source_target_pairs={{64,0},{128,64},{192,128},{256,192},{320,256},{384,320},{448,384},... | collective-permute-start | bytes 786440 | tf_op jit(solution)/shard_map/ppermute | solution.py:290
  7.4 1.9 %collective-permute-start.2 = (bf16[2,1,128,256]{3,2,1,0:T(8,128)(2,1)S(1)}, bf16[2,1,128,256]{3,2,1,0:T(8,128)(2,1)S(1)}, u32[]{:S(2)}, u32[]{:S(2)}) collective-permute-start(bf16[2,1,128,256]{3,2,1,0:T(8,128)(2,1)S(1)} %get-tuple-element.34), channel_id=1, source_target_pairs={{0,1},{1,0},{2,3},{3,2},{4,5},{5,4},{6,7},{7,6},{8,9},{9,8},{10,11... | collective-permute-start | bytes 393224 | tf_op jit(solution)/shard_map/ppermute | solution.py:275
  10.1 1.3 %shard_map.78 = (f32[2,512,256]{2,1,0:T(8,128)S(1)}, bf16[3,2,256,512]{3,2,1,0:T(8,128)(2,1)S(1)}) custom-call(bf16[2,4,128,256]{3,2,1,0:T(8,128)(2,1)S(1)} %copy-done.3, bf16[9,256,256]{2,1,0:T(8,128)(2,1)S(1)} %copy-done), custom_call_target="tpu_custom_call" | custom-call | flops 1207959552 | bytes 4194304 | tf_op jit(solution)/shard_map/pallas_call | solution.py:65
  11.3 0.9 %shard_map.79 = (bf16[2,4,128,256]{3,2,1,0:T(8,128)(2,1)S(1)}, f32[2,512,256]{2,1,0:T(8,128)S(1)}, bf16[2,256,512]{2,1,0:T(8,128)(2,1)S(1)}, bf16[3,2,2,256,128]{4,3,2,1,0:T(8,128)(2,1)S(1)}, f32[2,256,256]{2,1,0:T(8,128)S(1)}) custom-call(s32[1]{0:T(128)} %bitcast.core, f32[2,512,256]{2,1,0:T(8,128)S(1)} %get-tuple-element.33.pre, ...), custom_call_target="tpu_custom_call" | custom-call | flops 671088640 | bytes 8388608 | tf_op jit(solution)/shard_map/pallas_call | solution.py:65
  12.3 4.3 %collective-permute-done.n0 = bf16[1,4,128,256]{3,2,1,0:T(8,128)(2,1)S(1)} collective-permute-done((bf16[1,4,128,256]{3,2,1,0:T(8,128)(2,1)S(1)}, bf16[1,4,128,256]{3,2,1,0:T(8,128)(2,1)S(1)}, u32[]{:S(2)}, u32[]{:S(2)}) %collective-permute-start) | collective-permute-done | bytes 262176 | tf_op jit(solution)/shard_map/ppermute | solution.py:289
  16.6 4.5 %collective-permute-done.1.n1 = bf16[1,4,128,256]{3,2,1,0:T(8,128)(2,1)S(1)} collective-permute-done((bf16[1,4,128,256]{3,2,1,0:T(8,128)(2,1)S(1)}, bf16[1,4,128,256]{3,2,1,0:T(8,128)(2,1)S(1)}, u32[]{:S(2)}, u32[]{:S(2)}) %collective-permute-start.1) | collective-permute-done | bytes 262176 | tf_op jit(solution)/shard_map/ppermute | solution.py:290
  21.0 2.7 %shard_map.80 = (bf16[2,4,128,256]{3,2,1,0:T(8,128)(2,1)S(1)}, bf16[2,1,128,256]{3,2,1,0:T(8,128)(2,1)S(1)}, bf16[2,1,128,256]{3,2,1,0:T(8,128)(2,1)S(1)}, f32[1...) custom-call(s32[1]{0:T(128)} %bitcast.core, bf16[1,4,128,256]{3,2,1,0:T(8,128)(2,1)S(1)} %collective-permute-done.n0, ...), custom_call_target="tpu_custom_call" | custom-call | flops 2013265920 | bytes 10485760 | tf_op jit(solution)/shard_map/pallas_call | solution.py:65
  23.7 0.8 copy-done.6
  24.5 1.9 %collective-permute-start.4 = (bf16[12,256,128]{2,1,0:T(8,128)(2,1)S(1)}, bf16[12,256,128]{2,1,0:T(8,128)(2,1)S(1)}, u32[]{:S(2)}, u32[]{:S(2)}) collective-permute-start(bf16[12,256,128]{2,1,0:T(8,128)(2,1)S(1)} %get-tuple-element.43), channel_id=1, source_target_pairs={{0,1},{1,0},{2,3},{3,2},{4,5},{5,4},{6,7},{7,6},{8,9},{9,8},{10,11... | collective-permute-start | bytes 2359304 | tf_op jit(solution)/shard_map/ppermute | solution.py:334
  26.4 2.3 %collective-permute-done.4.got = bf16[12,256,128]{2,1,0:T(8,128)(2,1)S(1)} collective-permute-done((bf16[12,256,128]{2,1,0:T(8,128)(2,1)S(1)}, bf16[12,256,128]{2,1,0:T(8,128)(2,1)S(1)}, u32[]{:S(2)}, u32[]{:S(2)}) %collective-permute-start.4) | collective-permute-done | bytes 786464 | tf_op jit(solution)/shard_map/ppermute | solution.py:334
  28.7 1.2 %shard_map.81 = bf16[16,32,768]{2,1,0:T(8,128)(2,1)} custom-call(f32[12,256,128]{2,1,0:T(8,128)S(1)} %get-tuple-element.42.keep, bf16[12,256,128]{2,1,0:T(8,128)(2,1)S(1)} %collective-permute-done.4.got), custom_call_target="tpu_custom_call" | custom-call | flops 1048576 | bytes 4194304 | tf_op jit(solution)/shard_map/pallas_call | solution.py:65
  29.9 11.2 %all-to-all-start = ((bf16[16,32,768]{2,1,0:T(8,128)(2,1)}), bf16[16,32,768]{2,1,0:T(8,128)(2,1)S(1)}, u32[]{:S(2)}, u32[]{:S(2)}) async-start(bf16[16,32,768]{2,1,0:T(8,128)(2,1)} %shard_map.81), calls=%async_computation | async-start | bytes 1572864 | tf_op jit(solution)/shard_map/all_to_all | solution.py:336
  41.1 1.9 %collective-permute-start.5 = (bf16[2,1,128,256]{3,2,1,0:T(8,128)(2,1)S(1)}, bf16[2,1,128,256]{3,2,1,0:T(8,128)(2,1)S(1)}, u32[]{:S(2)}, u32[]{:S(2)}) collective-permute-start(bf16[2,1,128,256]{3,2,1,0:T(8,128)(2,1)S(1)} %get-tuple-element.44), channel_id=1, source_target_pairs={{0,1},{1,0},{2,3},{3,2},{4,5},{5,4},{6,7},{7,6},{8,9},{9,8},{10,11... | collective-permute-start | bytes 393224 | tf_op jit(solution)/shard_map/ppermute | solution.py:275
  45.0 9.0 %all-to-all-done.got = bf16[16,32,768]{2,1,0:T(8,128)(2,1)S(1)} async-done(((bf16[16,32,768]{2,1,0:T(8,128)(2,1)}), bf16[16,32,768]{2,1,0:T(8,128)(2,1)S(1)}, u32[]{:S(2)}, u32[]{:S(2)}) %all-to-all-start) | async-done | bytes 786464 | tf_op jit(solution)/shard_map/all_to_all | solution.py:336
  54.0 4.0 %collective-permute-start.7 = (bf16[2,4,128,256]{3,2,1,0:T(8,128)(2,1)S(1)}, bf16[2,4,128,256]{3,2,1,0:T(8,128)(2,1)S(1)}, u32[]{:S(2)}, u32[]{:S(2)}) collective-permute-start(bf16[2,4,128,256]{3,2,1,0:T(8,128)(2,1)S(1)} %get-tuple-element.48.hid), channel_id=1, source_target_pairs={{0,64},{64,128},{128,192},{192,256},{256,320},{320,384},{384,448},... | collective-permute-start | bytes 1572872 | tf_op jit(solution)/shard_map/ppermute | solution.py:339
  58.0 0.9 %shard_map.82 = f32[16,4,384]{2,1,0:T(4,128)} custom-call(bf16[16,32,768]{2,1,0:T(8,128)(2,1)S(1)} %all-to-all-done.got), custom_call_target="tpu_custom_call" | custom-call | flops 1048576 | bytes 1048576 | tf_op jit(solution)/shard_map/pallas_call | solution.py:65
  59.0 9.4 %all-to-all-start.1 = ((f32[16,4,384]{2,1,0:T(4,128)}), f32[16,4,384]{2,1,0:T(4,128)S(1)}, u32[]{:S(2)}, u32[]{:S(2)}) async-start(f32[16,4,384]{2,1,0:T(4,128)} %shard_map.82), calls=%async_computation.1 | async-start | bytes 196608 | tf_op jit(solution)/shard_map/all_to_all | solution.py:355
  68.4 0.9 %copy-done.5 = bf16[2,1,128,256]{3,2,1,0:T(8,128)(2,1)S(1)} copy-done((bf16[2,1,128,256]{3,2,1,0:T(8,128)(2,1)S(1)}, bf16[2,1,128,256]{3,2,1,0:T(8,128)(2,1)}, u32[]{:S(2)}) %copy-start.5) | copy-done | bytes 131096
  69.3 1.0 %copy-done.7 = bf16[2,4,128,256]{3,2,1,0:T(8,128)(2,1)S(1)} copy-done((bf16[2,4,128,256]{3,2,1,0:T(8,128)(2,1)S(1)}, bf16[2,4,128,256]{3,2,1,0:T(8,128)(2,1)}, u32[]{:S(2)}) %copy-start.7) | copy-done | bytes 524312
  70.4 2.2 %shard_map.84 = bf16[2,4,128,256]{3,2,1,0:T(8,128)(2,1)} custom-call(s32[1]{0:T(128)} %bitcast.core, bf16[2,4,128,256]{3,2,1,0:T(8,128)(2,1)S(1)} %copy-done.7, bf16[2,1,128,256]{3,2,1,0:T(8,128)(2,1)S(1)} %collective-permute-done.5.pair, bf16[2,1,128,256]{3,2,1,0:T(8,128)(2,1)S(1)} %copy-done.5, bf16[9,256,256]{2,1,0:T(8,128)(2,1)S(1)} %copy-done), custom_call_target="tpu_custom_call" | custom-call | flops 1207959552 | bytes 4194304 | tf_op jit(solution)/shard_map/pallas_call | solution.py:65
  72.6 1.4 %shard_map.83 = bf16[2,4,128,256]{3,2,1,0:T(8,128)(2,1)} custom-call(bf16[2,4,128,256]{3,2,1,0:T(8,128)(2,1)S(1)} %get-tuple-element.48.hid, bf16[2,4,128,256]{3,2,1,0:T(8,128)(2,1)S(1)} %collective-permute-done.7.past, bf16[3,256,256]{2,1,0:T(8,128)(2,1)S(1)} %copy-done.2), custom_call_target="tpu_custom_call" | custom-call | flops 402653184 | bytes 2097152 | tf_op jit(solution)/shard_map/pallas_call | solution.py:65
  74.0 7.6 %all-to-all-done.1.got = f32[16,4,384]{2,1,0:T(4,128)S(1)} async-done(((f32[16,4,384]{2,1,0:T(4,128)}), f32[16,4,384]{2,1,0:T(4,128)S(1)}, u32[]{:S(2)}, u32[]{:S(2)}) %all-to-all-start.1) | async-done | bytes 98336 | tf_op jit(solution)/shard_map/all_to_all | solution.py:355
  (23 shorter events, 4.0 us)
Async XLA Ops:
  0.6 1.0 %copy-start.1 = (bf16[2,4,128,256]{3,2,1,0:T(8,128)(2,1)S(1)}, bf16[2,4,128,256]{3,2,1,0:T(8,128)(2,1)}, u32[]{:S(2)}) copy-start(bf16[2,4,128,256]{3,2,1,0:T(8,128)(2,1)} %g.3) | copy-start | bytes 1572868
  0.6 6.3 %copy-start.2 = (bf16[3,256,256]{2,1,0:T(8,128)(2,1)S(1)}, bf16[3,256,256]{2,1,0:T(8,128)(2,1)}, u32[]{:S(2)}) copy-start(bf16[3,256,256]{2,1,0:T(8,128)(2,1)} %wt.5) | copy-start | bytes 1179652
  0.7 6.3 %copy-start.3 = (bf16[2,4,128,256]{3,2,1,0:T(8,128)(2,1)S(1)}, bf16[2,4,128,256]{3,2,1,0:T(8,128)(2,1)}, u32[]{:S(2)}) copy-start(bf16[2,4,128,256]{3,2,1,0:T(8,128)(2,1)} %x.3) | copy-start | bytes 1572868
  1.7 8.4 %copy-start = (bf16[9,256,256]{2,1,0:T(8,128)(2,1)S(1)}, bf16[9,256,256]{2,1,0:T(8,128)(2,1)}, u32[]{:S(2)}) copy-start(bf16[9,256,256]{2,1,0:T(8,128)(2,1)} %ws.5) | copy-start | bytes 3538948
  1.7 14.8 %collective-permute-start = (bf16[1,4,128,256]{3,2,1,0:T(8,128)(2,1)S(1)}, bf16[1,4,128,256]{3,2,1,0:T(8,128)(2,1)S(1)}, u32[]{:S(2)}, u32[]{:S(2)}) collective-permute-start(bf16[1,4,128,256]{3,2,1,0:T(8,128)(2,1)S(1)} %get-tuple-element.30), channel_id=1, source_target_pairs={{64,0},{128,64},{192,128},{256,192},{320,256},{384,320},{448,384},... | collective-permute-start | bytes 786440 | tf_op jit(solution)/shard_map/ppermute | solution.py:289
  4.5 16.5 %collective-permute-start.1 = (bf16[1,4,128,256]{3,2,1,0:T(8,128)(2,1)S(1)}, bf16[1,4,128,256]{3,2,1,0:T(8,128)(2,1)S(1)}, u32[]{:S(2)}, u32[]{:S(2)}) collective-permute-start(bf16[1,4,128,256]{3,2,1,0:T(8,128)(2,1)S(1)} %get-tuple-element.31), channel_id=1, source_target_pairs={{64,0},{128,64},{192,128},{256,192},{320,256},{384,320},{448,384},... | collective-permute-start | bytes 786440 | tf_op jit(solution)/shard_map/ppermute | solution.py:290
  7.4 3.9 %collective-permute-start.2 = (bf16[2,1,128,256]{3,2,1,0:T(8,128)(2,1)S(1)}, bf16[2,1,128,256]{3,2,1,0:T(8,128)(2,1)S(1)}, u32[]{:S(2)}, u32[]{:S(2)}) collective-permute-start(bf16[2,1,128,256]{3,2,1,0:T(8,128)(2,1)S(1)} %get-tuple-element.34), channel_id=1, source_target_pairs={{0,1},{1,0},{2,3},{3,2},{4,5},{5,4},{6,7},{7,6},{8,9},{9,8},{10,11... | collective-permute-start | bytes 393224 | tf_op jit(solution)/shard_map/ppermute | solution.py:275
  9.4 2.0 %collective-permute-start.3 = (bf16[2,1,128,256]{3,2,1,0:T(8,128)(2,1)S(1)}, bf16[2,1,128,256]{3,2,1,0:T(8,128)(2,1)S(1)}, u32[]{:S(2)}, u32[]{:S(2)}) collective-permute-start(bf16[2,1,128,256]{3,2,1,0:T(8,128)(2,1)S(1)} %get-tuple-element.35), channel_id=1, source_target_pairs={{1,2},{3,4},{5,6},{7,8},{9,10},{11,12},{13,14},{15,16},{17,18},{19... | collective-permute-start | bytes 393224 | tf_op jit(solution)/shard_map/ppermute | solution.py:274
  23.7 0.8 copy-start.6
  24.5 4.2 %collective-permute-start.4 = (bf16[12,256,128]{2,1,0:T(8,128)(2,1)S(1)}, bf16[12,256,128]{2,1,0:T(8,128)(2,1)S(1)}, u32[]{:S(2)}, u32[]{:S(2)}) collective-permute-start(bf16[12,256,128]{2,1,0:T(8,128)(2,1)S(1)} %get-tuple-element.43), channel_id=1, source_target_pairs={{0,1},{1,0},{2,3},{3,2},{4,5},{5,4},{6,7},{7,6},{8,9},{9,8},{10,11... | collective-permute-start | bytes 2359304 | tf_op jit(solution)/shard_map/ppermute | solution.py:334
  29.9 24.1 %all-to-all-start = ((bf16[16,32,768]{2,1,0:T(8,128)(2,1)}), bf16[16,32,768]{2,1,0:T(8,128)(2,1)S(1)}, u32[]{:S(2)}, u32[]{:S(2)}) async-start(bf16[16,32,768]{2,1,0:T(8,128)(2,1)} %shard_map.81), calls=%async_computation | async-start | bytes 1572864 | tf_op jit(solution)/shard_map/all_to_all | solution.py:336
  41.1 3.2 %collective-permute-start.5 = (bf16[2,1,128,256]{3,2,1,0:T(8,128)(2,1)S(1)}, bf16[2,1,128,256]{3,2,1,0:T(8,128)(2,1)S(1)}, u32[]{:S(2)}, u32[]{:S(2)}) collective-permute-start(bf16[2,1,128,256]{3,2,1,0:T(8,128)(2,1)S(1)} %get-tuple-element.44), channel_id=1, source_target_pairs={{0,1},{1,0},{2,3},{3,2},{4,5},{5,4},{6,7},{7,6},{8,9},{9,8},{10,11... | collective-permute-start | bytes 393224 | tf_op jit(solution)/shard_map/ppermute | solution.py:275
  43.0 1.3 %collective-permute-start.6 = (bf16[2,1,128,256]{3,2,1,0:T(8,128)(2,1)S(1)}, bf16[2,1,128,256]{3,2,1,0:T(8,128)(2,1)S(1)}, u32[]{:S(2)}, u32[]{:S(2)}) collective-permute-start(bf16[2,1,128,256]{3,2,1,0:T(8,128)(2,1)S(1)} %get-tuple-element.45), channel_id=1, source_target_pairs={{1,2},{3,4},{5,6},{7,8},{9,10},{11,12},{13,14},{15,16},{17,18},{19... | collective-permute-start | bytes 393224 | tf_op jit(solution)/shard_map/ppermute | solution.py:274
  44.3 0.7 copy-start.4
  54.0 18.6 %collective-permute-start.7 = (bf16[2,4,128,256]{3,2,1,0:T(8,128)(2,1)S(1)}, bf16[2,4,128,256]{3,2,1,0:T(8,128)(2,1)S(1)}, u32[]{:S(2)}, u32[]{:S(2)}) collective-permute-start(bf16[2,4,128,256]{3,2,1,0:T(8,128)(2,1)S(1)} %get-tuple-element.48.hid), channel_id=1, source_target_pairs={{0,64},{64,128},{128,192},{192,256},{256,320},{320,384},{384,448},... | collective-permute-start | bytes 1572872 | tf_op jit(solution)/shard_map/ppermute | solution.py:339
  59.0 22.6 %all-to-all-start.1 = ((f32[16,4,384]{2,1,0:T(4,128)}), f32[16,4,384]{2,1,0:T(4,128)S(1)}, u32[]{:S(2)}, u32[]{:S(2)}) async-start(f32[16,4,384]{2,1,0:T(4,128)} %shard_map.82), calls=%async_computation.1 | async-start | bytes 196608 | tf_op jit(solution)/shard_map/all_to_all | solution.py:355
  68.4 0.9 %copy-start.5 = (bf16[2,1,128,256]{3,2,1,0:T(8,128)(2,1)S(1)}, bf16[2,1,128,256]{3,2,1,0:T(8,128)(2,1)}, u32[]{:S(2)}) copy-start(bf16[2,1,128,256]{3,2,1,0:T(8,128)(2,1)} %copy-done.4) | copy-start | bytes 393220
  69.3 1.0 %copy-start.7 = (bf16[2,4,128,256]{3,2,1,0:T(8,128)(2,1)S(1)}, bf16[2,4,128,256]{3,2,1,0:T(8,128)(2,1)}, u32[]{:S(2)}) copy-start(bf16[2,4,128,256]{3,2,1,0:T(8,128)(2,1)} %copy-done.6) | copy-start | bytes 1572868

commit v4 on v3

--- a/solution.py
+++ b/solution.py
@@ -53,7 +53,7 @@
 
 
 def call(kernel, out_shape, flops, nbytes, *args, hbm_in=(), hbm_out=(), scratch=()):
-    flat, tree = jax.tree.flatten(out_shape)
+    flat, tree = jax.tree.flatten(out_shape, is_leaf=lambda leaf: hasattr(leaf, "dtype"))
     out_specs = [
         pl.BlockSpec(memory_space=pltpu.HBM if n in hbm_out else pltpu.VMEM)
         for n in range(len(flat))
@@ -77,6 +77,14 @@
     return jax.ShapeDtypeStruct(dims, dtype)
 
 
+def vmem(dims, dtype):
+    return pltpu.VMEM(dims, dtype)
+
+
+def hbm(dims, dtype):
+    return pltpu.HBM(dims, dtype)
+
+
 TAP_FLOPS = 2 * 2 * PIX * C * C
 
 
@@ -86,17 +94,6 @@
     side = (col // 128) ^ core[0]
     source = ((col % 128) // 64) * 128 + ((col % 64) // 4) * 8 + side * 4 + col % 4
     out_ref[...] = jnp.where(row == source, 1.0, 0.0).astype(BF16)
-
-
-def piece_kernel(g, pm, g0_ref, g1_ref, sems):
-    copies = [
-        pltpu.make_async_copy(g.at[0:1], g0_ref, sems.at[0]),
-        pltpu.make_async_copy(g.at[1:2], g1_ref, sems.at[1]),
-    ]
-    for copy in copies:
-        copy.start()
-    for copy in copies:
-        copy.wait()
 
 
 def first_kernel(core, x, g, wt, pm, gh_ref, gp_ref, pair_ref, chip_ref):
@@ -163,26 +160,30 @@
 
 
 def grad_kernel(
-    core, n0, n1, gh, fac, xt, xe, ht, gt, wt, pm,
-    gpre_hbm, pair_ref, chip_ref, keep_ref, send_ref,
-    gpre_ref, sem,
+    core, n, gh, fac, xt, xe, ht, gt, wt, pm,
+    gpre_hbm, pair_hbm, chip_hbm, keep_ref, send_ref,
+    gpre_ref, sems,
 ):
     def store(tap, value):
         keep_ref[tap] = value[:, : C // 2]
         send_ref[tap] = value[:, C // 2 :].astype(BF16)
 
-    a0, a1 = n0[0].reshape(PIX, C), n1[0].reshape(PIX, C)
+    a0, a1 = n[0].reshape(PIX, C), n[1].reshape(PIX, C)
     back0 = gh[0] + mm_t(a0, wt[0])
     back1 = gh[1] + mm_t(a0, wt[1]) + mm_t(a1, wt[0])
     grads = []
     for f, back in enumerate((back0, back1)):
         gpre = (back.astype(BF16).astype(F32) * fac[f]).astype(BF16)
         gpre_ref[f] = gpre.reshape(ROWS, COLS, C)
-        pair_ref[f, 0] = gpre_ref[f, 3 - 3 * core[0]]
-        chip_ref[f, 0] = gpre_ref[f, 3 * core[0]]
         grads.append(mm(gpre, pm[...]).astype(BF16))
-    copy = pltpu.make_async_copy(gpre_ref, gpre_hbm, sem)
-    copy.start()
+    c = core[0]
+    copies = [
+        pltpu.make_async_copy(gpre_ref.at[:, pl.ds(3 - 3 * c, 1)], pair_hbm, sems.at[0]),
+        pltpu.make_async_copy(gpre_ref.at[:, pl.ds(3 * c, 1)], chip_hbm, sems.at[1]),
+        pltpu.make_async_copy(gpre_ref, gpre_hbm, sems.at[2]),
+    ]
+    for copy in copies:
+        copy.start()
     p0 = mm(a0, pm[...]).astype(BF16)
     p1 = mm(a1, pm[...]).astype(BF16)
     store(9, mm(ht[0], p0) + mm(ht[1], p1))
@@ -200,7 +201,8 @@
                 part = mm(own, grads[f])
                 total = part if total is None else total + part
             store(3 * i + j, total)
-    copy.wait()
+    for copy in copies:
+        copy.wait()
 
 
 def pair_kernel(keep, got, out_ref):
@@ -269,25 +271,21 @@
     return forward, [(b, a) for a, b in forward]
 
 
-def edges(pair, chip):
+def to_pair(rows):
+    return lax.ppermute(rows, "c", [(0, 1), (1, 0)])
+
+
+def to_chip(rows):
     across = [(i, i + 1) for i in range(1, 63, 2)]
-    chip = lax.ppermute(chip, SPACE, across + [(b, a) for a, b in across])
-    pair = lax.ppermute(pair, "c", [(0, 1), (1, 0)])
-    return pair, chip
+    return lax.ppermute(rows, SPACE, across + [(b, a) for a, b in across])
 
 
 def body(frames_in, w_space, w_time, grad_out):
     forward, backward = steps(8)
     core = lax.axis_index("c").reshape(1)
     order = call(order_kernel, shape((C, C), BF16), HINT, 1 << 17, core)
-    frame = shape((1, ROWS, COLS, C), BF16)
     rows = shape((2, 1, COLS, C), BF16)
-    g0, g1 = call(
-        piece_kernel, (frame, frame), 0, 1 << 20, grad_out, order,
-        hbm_in=(0,), scratch=[pltpu.SemaphoreType.DMA((2,))],
-    )
-    next0 = lax.ppermute(g0, "tm", backward)
-    next1 = lax.ppermute(g1, "tm", backward)
+    later = lax.ppermute(grad_out, "tm", backward)
     gh_part, gp, pair, chip = call(
         first_kernel,
         (shape((2, PIX, C), F32), shape((2, PIX, C), BF16), rows, rows),
@@ -295,7 +293,7 @@
         4 << 20,
         core, frames_in, grad_out, w_time, order,
     )
-    pair, chip = edges(pair, chip)
+    pair, chip = to_pair(pair), to_chip(chip)
     pre_part, xt = call(
         own_kernel,
         (shape((2, PIX, C), F32), shape((3, 2, C, PIX), BF16)),
@@ -319,24 +317,27 @@
     grad_pre, pair, chip, keep, send = call(
         grad_kernel,
         (
-            shape((2, ROWS, COLS, C), BF16),
-            rows,
-            rows,
-            shape((TAPS, C, C // 2), F32),
-            shape((TAPS, C, C // 2), BF16),
+            hbm((2, ROWS, COLS, C), BF16),
+            hbm((2, 1, COLS, C), BF16),
+            hbm((2, 1, COLS, C), BF16),
+            vmem((TAPS, C, C // 2), F32),
+            vmem((TAPS, C, C // 2), BF16),
         ),
         15 * TAP_FLOPS,
         10 << 20,
-        core, next0, next1, gh_part, factor, xt, xe, ht, gt_part, w_time, order,
-        hbm_out=(0,),
-        scratch=[pltpu.VMEM((2, ROWS, COLS, C), BF16), pltpu.SemaphoreType.DMA],
+        core, later, gh_part, factor, xt, xe, ht, gt_part, w_time, order,
+        hbm_out=(0, 1, 2),
+        scratch=[pltpu.VMEM((2, ROWS, COLS, C), BF16), pltpu.SemaphoreType.DMA((3,))],
     )
     got = lax.ppermute(send, "c", [(0, 1), (1, 0)])
     chunks = call(pair_kernel, shape((16, 32, 768), BF16), 1 << 20, 4 << 20, keep, got)
     chunks = lax.all_to_all(chunks, ("tm", "xl"), split_axis=0, concat_axis=0, tiled=True)
-    pair, chip = edges(pair, chip)
-    chunks, pair, chip, hidden = lax.optimization_barrier((chunks, pair, chip, hidden))
+    pair = to_pair(pair)
+    chip, pair = lax.optimization_barrier((chip, pair))
+    chip = to_chip(chip)
+    hidden, chip = lax.optimization_barrier((hidden, chip))
     past = lax.ppermute(hidden, "tm", forward)
+    chunks, pair, chip = lax.optimization_barrier((chunks, pair, chip))
     block_out = call(
         out_kernel,
         shape((2, ROWS, COLS, C), BF16),

time: 82.8 us -> 80.3 us (0.970)
  local copies, waits for them, and re-layouts: 4.37 us -> 1.93 us
  starting transfers between devices: 36.9 us -> 38.9 us
  waiting for transfers between devices: 28.2 us -> 26.5 us
    all_to_all x1, waiting for transfers between devices: 9 us -> 3.43 us  [body(): lax.all_to_all(chunks, ('tm', 'xl'), split_axis=0, concat_axis=0, tiled=T...]
    all_to_all x1, starting transfers between devices: 9.44 us -> 15 us  [body(): rows = lax.all_to_all(rows, 'z', split_axis=0, concat_axis=0, tiled=True)]
    ppermute x6 -> x5, starting transfers between devices: 10.3 us -> 7.82 us  [the longest x2 3.84 us: to_pair(): return lax.ppermute(rows, 'c', [(0, 1), (1, 0)])]
    unnamed x16 -> x18, local copies, waits for them, and re-layouts: 4.37 us -> 1.93 us
    ppermute x6 -> x5, waiting for transfers between devices: 9.39 us -> 11.3 us  [the longest x1 10 us: body(): later = lax.ppermute(grad_out, 'tm', backward)]
    all_to_all x1, starting transfers between devices: 11.2 us -> 9.33 us  [body(): lax.all_to_all(chunks, ('tm', 'xl'), split_axis=0, concat_axis=0, tiled=T...]
    all_to_all x1, waiting for transfers between devices: 7.6 us -> 9.48 us  [body(): rows = lax.all_to_all(rows, 'z', split_axis=0, concat_axis=0, tiled=True)]
    ppermute x1, starting transfers between devices: 4.03 us -> 4.86 us  [body(): past = lax.ppermute(hidden, 'tm', forward)]
  transfers between devices with their start and end apart: 10 -> 9, of which waited for: 6 -> 5; matrix products, arithmetic and copies ran while one was open for 0% -> 0% of each run, Pallas kernels for 9% -> 9%
where the time goes in v4:
time: 80.3 us; the launch traced here: 79.8 us
  starting transfers between devices  38.9 us (48%)
  waiting for transfers between devices  26.5 us (33%)
  Pallas kernels  11.7 us (15%)
  local copies, waits for them, and re-layouts  1.93 us (2%)
  between operations  0.82 us (1%)
    all_to_all x1, starting transfers between devices, body(): rows = lax.all_to_all(rows, 'z', split_axis=0, concat_axis=0, tiled=True)  15 us
    pallas_call x10, Pallas kernels, call(): pl.pallas_call(kernel, out_shape=out_shape, in_specs=in_specs, out_specs=...  11.7 us
    ppermute x1, waiting for transfers between devices, body(): later = lax.ppermute(grad_out, 'tm', backward)  10 us
    all_to_all x1, waiting for transfers between devices, body(): rows = lax.all_to_all(rows, 'z', split_axis=0, concat_axis=0, tiled=True)  9.48 us
    all_to_all x1, starting transfers between devices, body(): lax.all_to_all(chunks, ('tm', 'xl'), split_axis=0, concat_axis=0, tiled=T...  9.33 us
    ppermute x1, starting transfers between devices, body(): past = lax.ppermute(hidden, 'tm', forward)  4.86 us
    ppermute x2, starting transfers between devices, to_pair(): return lax.ppermute(rows, 'c', [(0, 1), (1, 0)])  3.84 us
    all_to_all x1, waiting for transfers between devices, body(): lax.all_to_all(chunks, ('tm', 'xl'), split_axis=0, concat_axis=0, tiled=T...  3.43 us
  transfers between devices with their start and end apart: 9, of which 5 were waited for; matrix products, arithmetic and copies ran while one was open for 0% of the time, Pallas kernels for 9%

profile of v4, /device:TPU:24, one launch (start us, length us, event | category | flops | bytes accessed | tf_op | source)
XLA Modules:
  0.0 79.8 jit_solution(8350343112549409580)
XLA Ops:
  0.6 2.7 %collective-permute-start = (bf16[2,4,128,256]{3,2,1,0:T(8,128)(2,1)}, bf16[2,4,128,256]{3,2,1,0:T(8,128)(2,1)S(1)}, u32[]{:S(2)}, u32[]{:S(2)}) collective-permute-start(bf16[2,4,128,256]{3,2,1,0:T(8,128)(2,1)} %g.1), channel_id=1, source_target_pairs={{64,0},{128,64},{192,128},{256,192},{320,256},{384,320},{448,384},... | collective-permute-start | bytes 1572872 | tf_op jit(solution)/shard_map/ppermute | solution.py:288
  3.4 0.9 %copy-done.1 = bf16[3,256,256]{2,1,0:T(8,128)(2,1)S(1)} copy-done((bf16[3,256,256]{2,1,0:T(8,128)(2,1)S(1)}, bf16[3,256,256]{2,1,0:T(8,128)(2,1)}, u32[]{:S(2)}) %copy-start.1) | copy-done | bytes 393240
  5.1 1.9 %collective-permute-start.1 = (bf16[2,1,128,256]{3,2,1,0:T(8,128)(2,1)S(1)}, bf16[2,1,128,256]{3,2,1,0:T(8,128)(2,1)S(1)}, u32[]{:S(2)}, u32[]{:S(2)}) collective-permute-start(bf16[2,1,128,256]{3,2,1,0:T(8,128)(2,1)S(1)} %get-tuple-element.33), channel_id=1, source_target_pairs={{0,1},{1,0},{2,3},{3,2},{4,5},{5,4},{6,7},{7,6},{8,9},{9,8},{10,11... | collective-permute-start | bytes 393224 | tf_op jit(solution)/shard_map/ppermute | solution.py:275
  7.1 0.7 collective-permute-start.2
  7.8 1.3 %shard_map.77 = (f32[2,512,256]{2,1,0:T(8,128)S(1)}, bf16[3,2,256,512]{3,2,1,0:T(8,128)(2,1)S(1)}) custom-call(bf16[2,4,128,256]{3,2,1,0:T(8,128)(2,1)S(1)} %copy-done.2, bf16[9,256,256]{2,1,0:T(8,128)(2,1)S(1)} %copy-done), custom_call_target="tpu_custom_call" | custom-call | flops 1207959552 | bytes 4194304 | tf_op jit(solution)/shard_map/pallas_call | solution.py:65
  9.0 0.9 %shard_map.78 = (bf16[2,4,128,256]{3,2,1,0:T(8,128)(2,1)S(1)}, f32[2,512,256]{2,1,0:T(8,128)S(1)}, bf16[2,256,512]{2,1,0:T(8,128)(2,1)S(1)}, bf16[3,2,2,256,128]{4,3,2,1,0:T(8,128)(2,1)S(1)}, f32[2,256,256]{2,1,0:T(8,128)S(1)}) custom-call(s32[1]{0:T(128)} %bitcast.core, f32[2,512,256]{2,1,0:T(8,128)S(1)} %get-tuple-element.32.pre, ...), custom_call_target="tpu_custom_call" | custom-call | flops 671088640 | bytes 8388608 | tf_op jit(solution)/shard_map/pallas_call | solution.py:65
  10.0 10.0 %collective-permute-done.n = bf16[2,4,128,256]{3,2,1,0:T(8,128)(2,1)S(1)} collective-permute-done((bf16[2,4,128,256]{3,2,1,0:T(8,128)(2,1)}, bf16[2,4,128,256]{3,2,1,0:T(8,128)(2,1)S(1)}, u32[]{:S(2)}, u32[]{:S(2)}) %collective-permute-start) | collective-permute-done | bytes 524320 | tf_op jit(solution)/shard_map/ppermute | solution.py:288
  20.0 2.4 %shard_map.79 = (bf16[2,4,128,256]{3,2,1,0:T(8,128)(2,1)}, bf16[2,1,128,256]{3,2,1,0:T(8,128)(2,1)}, bf16[2,1,128,256]{3,2,1,0:T(8,128)(2,1)}, f32[12,256,128]{2,1,0:T(8,128)S(1)}, bf16[12,256,128]{2,1,0:T(8,128)(2,1)S(1)}) custom-call(s32[1]{0:T(128)} %bitcast.core, bf16[2,4,128,256]{3,2,1,0:T(8,128)(2,1)S(1)} %collective-permute-done.n, ...), custom_call_target="tpu_custom_call" | custom-call | flops 2013265920 | bytes 10485760 | tf_op jit(solution)/shard_map/pallas_call | solution.py:65
  22.5 1.9 %collective-permute-start.3 = (bf16[12,256,128]{2,1,0:T(8,128)(2,1)S(1)}, bf16[12,256,128]{2,1,0:T(8,128)(2,1)S(1)}, u32[]{:S(2)}, u32[]{:S(2)}) collective-permute-start(bf16[12,256,128]{2,1,0:T(8,128)(2,1)S(1)} %get-tuple-element.42), channel_id=1, source_target_pairs={{0,1},{1,0},{2,3},{3,2},{4,5},{5,4},{6,7},{7,6},{8,9},{9,8},{10,11... | collective-permute-start | bytes 2359304 | tf_op jit(solution)/shard_map/ppermute | solution.py:332
  24.4 2.3 %collective-permute-done.3.got = bf16[12,256,128]{2,1,0:T(8,128)(2,1)S(1)} collective-permute-done((bf16[12,256,128]{2,1,0:T(8,128)(2,1)S(1)}, bf16[12,256,128]{2,1,0:T(8,128)(2,1)S(1)}, u32[]{:S(2)}, u32[]{:S(2)}) %collective-permute-start.3) | collective-permute-done | bytes 786464 | tf_op jit(solution)/shard_map/ppermute | solution.py:332
  26.6 1.2 %shard_map.80 = bf16[16,32,768]{2,1,0:T(8,128)(2,1)} custom-call(f32[12,256,128]{2,1,0:T(8,128)S(1)} %get-tuple-element.41.keep, bf16[12,256,128]{2,1,0:T(8,128)(2,1)S(1)} %collective-permute-done.3.got), custom_call_target="tpu_custom_call" | custom-call | flops 1048576 | bytes 4194304 | tf_op jit(solution)/shard_map/pallas_call | solution.py:65
  27.9 9.3 %all-to-all-start = ((bf16[16,32,768]{2,1,0:T(8,128)(2,1)}), bf16[16,32,768]{2,1,0:T(8,128)(2,1)S(1)}, u32[]{:S(2)}, u32[]{:S(2)}) async-start(bf16[16,32,768]{2,1,0:T(8,128)(2,1)} %shard_map.80), calls=%async_computation | async-start | bytes 1572864 | tf_op jit(solution)/shard_map/all_to_all | solution.py:334
  37.2 1.9 %collective-permute-start.4 = (bf16[2,1,128,256]{3,2,1,0:T(8,128)(2,1)S(1)}, bf16[2,1,128,256]{3,2,1,0:T(8,128)(2,1)S(1)}, u32[]{:S(2)}, u32[]{:S(2)}) collective-permute-start(bf16[2,1,128,256]{3,2,1,0:T(8,128)(2,1)S(1)} %copy-done.8), channel_id=1, source_target_pairs={{0,1},{1,0},{2,3},{3,2},{4,5},{5,4},{6,7},{7,6},{8,9},{9,8},{10,11... | collective-permute-start | bytes 393224 | tf_op jit(solution)/shard_map/ppermute | solution.py:275
  39.1 1.3 %collective-permute-done.4.pair = bf16[2,1,128,256]{3,2,1,0:T(8,128)(2,1)S(1)} collective-permute-done((bf16[2,1,128,256]{3,2,1,0:T(8,128)(2,1)S(1)}, bf16[2,1,128,256]{3,2,1,0:T(8,128)(2,1)S(1)}, u32[]{:S(2)}, u32[]{:S(2)}) %collective-permute-start.4) | collective-permute-done | bytes 131104 | tf_op jit(solution)/shard_map/ppermute | solution.py:275
  40.5 0.7 collective-permute-start.5
  41.1 0.7 copy-done.4
  41.8 4.9 %collective-permute-start.6 = (bf16[2,4,128,256]{3,2,1,0:T(8,128)(2,1)S(1)}, bf16[2,4,128,256]{3,2,1,0:T(8,128)(2,1)S(1)}, u32[]{:S(2)}, u32[]{:S(2)}) collective-permute-start(bf16[2,4,128,256]{3,2,1,0:T(8,128)(2,1)S(1)} %get-tuple-element.50.hid), channel_id=1, source_target_pairs={{0,64},{64,128},{128,192},{192,256},{256,320},{320,384},{384,448},... | collective-permute-start | bytes 1572872 | tf_op jit(solution)/shard_map/ppermute | solution.py:339
  46.7 3.4 %all-to-all-done.got = bf16[16,32,768]{2,1,0:T(8,128)(2,1)S(1)} async-done(((bf16[16,32,768]{2,1,0:T(8,128)(2,1)}), bf16[16,32,768]{2,1,0:T(8,128)(2,1)S(1)}, u32[]{:S(2)}, u32[]{:S(2)}) %all-to-all-start) | async-done | bytes 786464 | tf_op jit(solution)/shard_map/all_to_all | solution.py:334
  50.1 0.9 %shard_map.81 = f32[16,4,384]{2,1,0:T(4,128)} custom-call(bf16[16,32,768]{2,1,0:T(8,128)(2,1)S(1)} %all-to-all-done.got), custom_call_target="tpu_custom_call" | custom-call | flops 1048576 | bytes 1048576 | tf_op jit(solution)/shard_map/pallas_call | solution.py:65
  51.0 15.0 %all-to-all-start.1 = ((f32[16,4,384]{2,1,0:T(4,128)}), f32[16,4,384]{2,1,0:T(4,128)S(1)}, u32[]{:S(2)}, u32[]{:S(2)}) async-start(f32[16,4,384]{2,1,0:T(4,128)} %shard_map.81), calls=%async_computation.1 | async-start | bytes 196608 | tf_op jit(solution)/shard_map/all_to_all | solution.py:356
  66.0 1.4 %shard_map.82 = bf16[2,4,128,256]{3,2,1,0:T(8,128)(2,1)} custom-call(bf16[2,4,128,256]{3,2,1,0:T(8,128)(2,1)S(1)} %get-tuple-element.50.hid, bf16[2,4,128,256]{3,2,1,0:T(8,128)(2,1)S(1)} %collective-permute-done.6.past, bf16[3,256,256]{2,1,0:T(8,128)(2,1)S(1)} %copy-done.1), custom_call_target="tpu_custom_call" | custom-call | flops 402653184 | bytes 2097152 | tf_op jit(solution)/shard_map/pallas_call | solution.py:65
  67.4 2.2 %shard_map.83 = bf16[2,4,128,256]{3,2,1,0:T(8,128)(2,1)} custom-call(s32[1]{0:T(128)} %bitcast.core, bf16[2,4,128,256]{3,2,1,0:T(8,128)(2,1)S(1)} %copy-done.6, bf16[2,1,128,256]{3,2,1,0:T(8,128)(2,1)S(1)} %collective-permute-done.4.pair, bf16[2,1,128,256]{3,2,1,0:T(8,128)(2,1)S(1)} %copy-done.5, bf16[9,256,256]{2,1,0:T(8,128)(2,1)S(1)} %copy-done), custom_call_target="tpu_custom_call" | custom-call | flops 1207959552 | bytes 4194304 | tf_op jit(solution)/shard_map/pallas_call | solution.py:65
  69.6 9.5 %all-to-all-done.1.got = f32[16,4,384]{2,1,0:T(4,128)S(1)} async-done(((f32[16,4,384]{2,1,0:T(4,128)}), f32[16,4,384]{2,1,0:T(4,128)S(1)}, u32[]{:S(2)}, u32[]{:S(2)}) %all-to-all-start.1) | async-done | bytes 98336 | tf_op jit(solution)/shard_map/all_to_all | solution.py:356
  79.1 0.7 shard_map.84
  (22 shorter events, 0.9 us)
Async XLA Ops:
  0.6 19.4 %collective-permute-start = (bf16[2,4,128,256]{3,2,1,0:T(8,128)(2,1)}, bf16[2,4,128,256]{3,2,1,0:T(8,128)(2,1)S(1)}, u32[]{:S(2)}, u32[]{:S(2)}) collective-permute-start(bf16[2,4,128,256]{3,2,1,0:T(8,128)(2,1)} %g.1), channel_id=1, source_target_pairs={{64,0},{128,64},{192,128},{256,192},{320,256},{384,320},{448,384},... | collective-permute-start | bytes 1572872 | tf_op jit(solution)/shard_map/ppermute | solution.py:288
  3.3 1.0 %copy-start.1 = (bf16[3,256,256]{2,1,0:T(8,128)(2,1)S(1)}, bf16[3,256,256]{2,1,0:T(8,128)(2,1)}, u32[]{:S(2)}) copy-start(bf16[3,256,256]{2,1,0:T(8,128)(2,1)} %wt.5) | copy-start | bytes 1179652
  3.3 1.2 %copy-start.2 = (bf16[2,4,128,256]{3,2,1,0:T(8,128)(2,1)S(1)}, bf16[2,4,128,256]{3,2,1,0:T(8,128)(2,1)}, u32[]{:S(2)}) copy-start(bf16[2,4,128,256]{3,2,1,0:T(8,128)(2,1)} %x.3) | copy-start | bytes 1572868
  3.3 1.3 %copy-start.3 = (bf16[2,4,128,256]{3,2,1,0:T(8,128)(2,1)S(1)}, bf16[2,4,128,256]{3,2,1,0:T(8,128)(2,1)}, u32[]{:S(2)}) copy-start(bf16[2,4,128,256]{3,2,1,0:T(8,128)(2,1)} %g.1) | copy-start | bytes 1572868
  4.6 3.1 %copy-start = (bf16[9,256,256]{2,1,0:T(8,128)(2,1)S(1)}, bf16[9,256,256]{2,1,0:T(8,128)(2,1)}, u32[]{:S(2)}) copy-start(bf16[9,256,256]{2,1,0:T(8,128)(2,1)} %ws.5) | copy-start | bytes 3538948
  5.1 3.9 %collective-permute-start.1 = (bf16[2,1,128,256]{3,2,1,0:T(8,128)(2,1)S(1)}, bf16[2,1,128,256]{3,2,1,0:T(8,128)(2,1)S(1)}, u32[]{:S(2)}, u32[]{:S(2)}) collective-permute-start(bf16[2,1,128,256]{3,2,1,0:T(8,128)(2,1)S(1)} %get-tuple-element.33), channel_id=1, source_target_pairs={{0,1},{1,0},{2,3},{3,2},{4,5},{5,4},{6,7},{7,6},{8,9},{9,8},{10,11... | collective-permute-start | bytes 393224 | tf_op jit(solution)/shard_map/ppermute | solution.py:275
  7.1 2.0 %collective-permute-start.2 = (bf16[2,1,128,256]{3,2,1,0:T(8,128)(2,1)S(1)}, bf16[2,1,128,256]{3,2,1,0:T(8,128)(2,1)S(1)}, u32[]{:S(2)}, u32[]{:S(2)}) collective-permute-start(bf16[2,1,128,256]{3,2,1,0:T(8,128)(2,1)S(1)} %get-tuple-element.34), channel_id=1, source_target_pairs={{1,2},{3,4},{5,6},{7,8},{9,10},{11,12},{13,14},{15,16},{17,18},{19... | collective-permute-start | bytes 393224 | tf_op jit(solution)/shard_map/ppermute | solution.py:280
  22.5 4.2 %collective-permute-start.3 = (bf16[12,256,128]{2,1,0:T(8,128)(2,1)S(1)}, bf16[12,256,128]{2,1,0:T(8,128)(2,1)S(1)}, u32[]{:S(2)}, u32[]{:S(2)}) collective-permute-start(bf16[12,256,128]{2,1,0:T(8,128)(2,1)S(1)} %get-tuple-element.42), channel_id=1, source_target_pairs={{0,1},{1,0},{2,3},{3,2},{4,5},{5,4},{6,7},{7,6},{8,9},{9,8},{10,11... | collective-permute-start | bytes 2359304 | tf_op jit(solution)/shard_map/ppermute | solution.py:332
  27.9 9.3 %copy-start.8 = (bf16[2,1,128,256]{3,2,1,0:T(8,128)(2,1)S(1)}, bf16[2,1,128,256]{3,2,1,0:T(8,128)(2,1)}, u32[]{:S(2)}) copy-start(bf16[2,1,128,256]{3,2,1,0:T(8,128)(2,1)} %get-tuple-element.44) | copy-start | bytes 393220
  27.9 12.6 %copy-start.7 = (bf16[2,1,128,256]{3,2,1,0:T(8,128)(2,1)S(1)}, bf16[2,1,128,256]{3,2,1,0:T(8,128)(2,1)}, u32[]{:S(2)}) copy-start(bf16[2,1,128,256]{3,2,1,0:T(8,128)(2,1)} %get-tuple-element.47) | copy-start | bytes 393220
  27.9 22.2 %all-to-all-start = ((bf16[16,32,768]{2,1,0:T(8,128)(2,1)}), bf16[16,32,768]{2,1,0:T(8,128)(2,1)S(1)}, u32[]{:S(2)}, u32[]{:S(2)}) async-start(bf16[16,32,768]{2,1,0:T(8,128)(2,1)} %shard_map.80), calls=%async_computation | async-start | bytes 1572864 | tf_op jit(solution)/shard_map/all_to_all | solution.py:334
  37.2 3.2 %collective-permute-start.4 = (bf16[2,1,128,256]{3,2,1,0:T(8,128)(2,1)S(1)}, bf16[2,1,128,256]{3,2,1,0:T(8,128)(2,1)S(1)}, u32[]{:S(2)}, u32[]{:S(2)}) collective-permute-start(bf16[2,1,128,256]{3,2,1,0:T(8,128)(2,1)S(1)} %copy-done.8), channel_id=1, source_target_pairs={{0,1},{1,0},{2,3},{3,2},{4,5},{5,4},{6,7},{7,6},{8,9},{9,8},{10,11... | collective-permute-start | bytes 393224 | tf_op jit(solution)/shard_map/ppermute | solution.py:275
  40.5 0.7 collective-permute-start.5
  41.1 0.7 copy-start.4
  41.8 24.2 %collective-permute-start.6 = (bf16[2,4,128,256]{3,2,1,0:T(8,128)(2,1)S(1)}, bf16[2,4,128,256]{3,2,1,0:T(8,128)(2,1)S(1)}, u32[]{:S(2)}, u32[]{:S(2)}) collective-permute-start(bf16[2,4,128,256]{3,2,1,0:T(8,128)(2,1)S(1)} %get-tuple-element.50.hid), channel_id=1, source_target_pairs={{0,64},{64,128},{128,192},{192,256},{256,320},{320,384},{384,448},... | collective-permute-start | bytes 1572872 | tf_op jit(solution)/shard_map/ppermute | solution.py:339
  51.0 16.4 %copy-start.5 = (bf16[2,1,128,256]{3,2,1,0:T(8,128)(2,1)S(1)}, bf16[2,1,128,256]{3,2,1,0:T(8,128)(2,1)}, u32[]{:S(2)}) copy-start(bf16[2,1,128,256]{3,2,1,0:T(8,128)(2,1)} %copy-done.4) | copy-start | bytes 393220
  51.0 16.4 %copy-start.6 = (bf16[2,4,128,256]{3,2,1,0:T(8,128)(2,1)S(1)}, bf16[2,4,128,256]{3,2,1,0:T(8,128)(2,1)}, u32[]{:S(2)}) copy-start(bf16[2,4,128,256]{3,2,1,0:T(8,128)(2,1)} %get-tuple-element.52.gpre) | copy-start | bytes 1572868
  51.0 28.1 %all-to-all-start.1 = ((f32[16,4,384]{2,1,0:T(4,128)}), f32[16,4,384]{2,1,0:T(4,128)S(1)}, u32[]{:S(2)}, u32[]{:S(2)}) async-start(f32[16,4,384]{2,1,0:T(4,128)} %shard_map.81), calls=%async_computation.1 | async-start | bytes 196608 | tf_op jit(solution)/shard_map/all_to_all | solution.py:356

commit v5 on v4

--- a/solution.py
+++ b/solution.py
@@ -240,6 +240,10 @@
         gt_ref[t] = total[:, 32 * (9 + t) : 32 * (9 + t) + 32]
 
 
+def token_kernel(rows, out_ref):
+    out_ref[...] = jnp.zeros(out_ref.shape, F32)
+
+
 def out_kernel(hid, past, wt, out_ref):
     h0, h1 = hid[0].reshape(PIX, C), hid[1].reshape(PIX, C)
     p0, p1 = past[0].reshape(PIX, C), past[1].reshape(PIX, C)
@@ -249,7 +253,7 @@
     out_ref[1] = second.astype(BF16).reshape(ROWS, COLS, C)
 
 
-def back_kernel(core, gpre, pair, chip, ws, out_ref):
+def back_kernel(core, gpre, pair, chip, ws, token, out_ref):
     for f in range(2):
         low, high = low_high(core, pair[f, 0], chip[f, 0])
         own = gpre[f].reshape(PIX, C)
@@ -333,7 +337,8 @@
     chunks = call(pair_kernel, shape((16, 32, 768), BF16), 1 << 20, 4 << 20, keep, got)
     chunks = lax.all_to_all(chunks, ("tm", "xl"), split_axis=0, concat_axis=0, tiled=True)
     pair = to_pair(pair)
-    chip, pair = lax.optimization_barrier((chip, pair))
+    token = call(token_kernel, shape((8, 128), F32), HINT, 1 << 12, pair, hbm_in=(0,))
+    chip, token = lax.optimization_barrier((chip, token))
     chip = to_chip(chip)
     hidden, chip = lax.optimization_barrier((hidden, chip))
     past = lax.ppermute(hidden, "tm", forward)
@@ -350,7 +355,7 @@
         shape((2, ROWS, COLS, C), BF16),
         9 * TAP_FLOPS,
         4 << 20,
-        core, grad_pre, pair, chip, w_space,
+        core, grad_pre, pair, chip, w_space, token,
     )
     rows = call(plane_kernel, shape((16, 4, 384), F32), 1 << 20, 1 << 20, chunks)
     rows = lax.all_to_all(rows, "z", split_axis=0, concat_axis=0, tiled=True)

time: 80.3 us -> 78 us (0.971)
  starting transfers between devices: 38.9 us -> 37 us
  waiting for transfers between devices: 26.5 us -> 25.2 us
  local copies, waits for them, and re-layouts: 1.93 us -> 2.79 us
    ppermute x1, waiting for transfers between devices: 2.25 us -> 0.01 us  [body(): got = lax.ppermute(send, 'c', [(0, 1), (1, 0)])]
    all_to_all x1, starting transfers between devices: 15 us -> 12.7 us  [body(): rows = lax.all_to_all(rows, 'z', split_axis=0, concat_axis=0, tiled=True)]
    all_to_all x1, waiting for transfers between devices: 3.43 us -> 5.67 us  [body(): lax.all_to_all(chunks, ('tm', 'xl'), split_axis=0, concat_axis=0, tiled=T...]
    ppermute x2, waiting for transfers between devices: 1.32 us -> 0.01 us  [to_pair(): return lax.ppermute(rows, 'c', [(0, 1), (1, 0)])]
    unnamed x18 -> x16, local copies, waits for them, and re-layouts: 1.93 us -> 2.79 us
    pallas_call x10 -> x11, Pallas kernels: 11.7 us -> 11.6 us  [call(): pl.pallas_call(kernel, out_shape=out_shape, in_specs=in_specs, out_specs=...]
  transfers between devices with their start and end apart: 9 -> 9, of which waited for: 5 -> 3; matrix products, arithmetic and copies ran while one was open for 0% -> 0% of each run, Pallas kernels for 9% -> 11%
where the time goes in v5:
time: 78 us; the launch traced here: 77.5 us
  starting transfers between devices  37 us (47%)
  waiting for transfers between devices  25.2 us (32%)
  Pallas kernels  11.6 us (15%)
  local copies, waits for them, and re-layouts  2.79 us (4%)
  between operations  0.84 us (1%)
    all_to_all x1, starting transfers between devices, body(): rows = lax.all_to_all(rows, 'z', split_axis=0, concat_axis=0, tiled=True)  12.7 us
    pallas_call x11, Pallas kernels, call(): pl.pallas_call(kernel, out_shape=out_shape, in_specs=in_specs, out_specs=...  11.6 us
    ppermute x1, waiting for transfers between devices, body(): later = lax.ppermute(grad_out, 'tm', backward)  10 us
    all_to_all x1, waiting for transfers between devices, body(): rows = lax.all_to_all(rows, 'z', split_axis=0, concat_axis=0, tiled=True)  9.47 us
    all_to_all x1, starting transfers between devices, body(): lax.all_to_all(chunks, ('tm', 'xl'), split_axis=0, concat_axis=0, tiled=T...  9.19 us
    all_to_all x1, waiting for transfers between devices, body(): lax.all_to_all(chunks, ('tm', 'xl'), split_axis=0, concat_axis=0, tiled=T...  5.67 us
    ppermute x1, starting transfers between devices, body(): past = lax.ppermute(hidden, 'tm', forward)  4.86 us
    ppermute x2, starting transfers between devices, to_pair(): return lax.ppermute(rows, 'c', [(0, 1), (1, 0)])  4.33 us
  transfers between devices with their start and end apart: 9, of which 3 were waited for; matrix products, arithmetic and copies ran while one was open for 0% of the time, Pallas kernels for 11%

profile of v5, /device:TPU:24, one launch (start us, length us, event | category | flops | bytes accessed | tf_op | source)
XLA Modules:
  0.0 77.5 jit_solution(11546941434629330419)
XLA Ops:
  0.6 2.7 %collective-permute-start = (bf16[2,4,128,256]{3,2,1,0:T(8,128)(2,1)}, bf16[2,4,128,256]{3,2,1,0:T(8,128)(2,1)S(1)}, u32[]{:S(2)}, u32[]{:S(2)}) collective-permute-start(bf16[2,4,128,256]{3,2,1,0:T(8,128)(2,1)} %g.1), channel_id=1, source_target_pairs={{64,0},{128,64},{192,128},{256,192},{320,256},{384,320},{448,384},... | collective-permute-start | bytes 1572872 | tf_op jit(solution)/shard_map/ppermute | solution.py:292
  3.4 0.9 %copy-done.1 = bf16[3,256,256]{2,1,0:T(8,128)(2,1)S(1)} copy-done((bf16[3,256,256]{2,1,0:T(8,128)(2,1)S(1)}, bf16[3,256,256]{2,1,0:T(8,128)(2,1)}, u32[]{:S(2)}) %copy-start.1) | copy-done | bytes 393240
  4.6 0.5 shard_map.76
  5.1 1.9 %collective-permute-start.1 = (bf16[2,1,128,256]{3,2,1,0:T(8,128)(2,1)S(1)}, bf16[2,1,128,256]{3,2,1,0:T(8,128)(2,1)S(1)}, u32[]{:S(2)}, u32[]{:S(2)}) collective-permute-start(bf16[2,1,128,256]{3,2,1,0:T(8,128)(2,1)S(1)} %get-tuple-element.33), channel_id=1, source_target_pairs={{0,1},{1,0},{2,3},{3,2},{4,5},{5,4},{6,7},{7,6},{8,9},{9,8},{10,11... | collective-permute-start | bytes 393224 | tf_op jit(solution)/shard_map/ppermute | solution.py:279
  7.1 0.7 collective-permute-start.2
  7.8 1.3 %shard_map.77 = (f32[2,512,256]{2,1,0:T(8,128)S(1)}, bf16[3,2,256,512]{3,2,1,0:T(8,128)(2,1)S(1)}) custom-call(bf16[2,4,128,256]{3,2,1,0:T(8,128)(2,1)S(1)} %copy-done.2, bf16[9,256,256]{2,1,0:T(8,128)(2,1)S(1)} %copy-done), custom_call_target="tpu_custom_call" | custom-call | flops 1207959552 | bytes 4194304 | tf_op jit(solution)/shard_map/pallas_call | solution.py:65
  9.0 0.9 %shard_map.78 = (bf16[2,4,128,256]{3,2,1,0:T(8,128)(2,1)S(1)}, f32[2,512,256]{2,1,0:T(8,128)S(1)}, bf16[2,256,512]{2,1,0:T(8,128)(2,1)S(1)}, bf16[3,2,2,256,128]{4,3,2,1,0:T(8,128)(2,1)S(1)}, f32[2,256,256]{2,1,0:T(8,128)S(1)}) custom-call(s32[1]{0:T(128)} %bitcast.core, f32[2,512,256]{2,1,0:T(8,128)S(1)} %get-tuple-element.32.pre, ...), custom_call_target="tpu_custom_call" | custom-call | flops 671088640 | bytes 8388608 | tf_op jit(solution)/shard_map/pallas_call | solution.py:65
  10.0 10.0 %collective-permute-done.n = bf16[2,4,128,256]{3,2,1,0:T(8,128)(2,1)S(1)} collective-permute-done((bf16[2,4,128,256]{3,2,1,0:T(8,128)(2,1)}, bf16[2,4,128,256]{3,2,1,0:T(8,128)(2,1)S(1)}, u32[]{:S(2)}, u32[]{:S(2)}) %collective-permute-start) | collective-permute-done | bytes 524320 | tf_op jit(solution)/shard_map/ppermute | solution.py:292
  20.0 2.4 %shard_map.79 = (bf16[2,4,128,256]{3,2,1,0:T(8,128)(2,1)}, bf16[2,1,128,256]{3,2,1,0:T(8,128)(2,1)}, bf16[2,1,128,256]{3,2,1,0:T(8,128)(2,1)}, f32[12,256,128]{2,1,0:T(8,128)S(1)}, bf16[12,256,128]{2,1,0:T(8,128)(2,1)S(1)}) custom-call(s32[1]{0:T(128)} %bitcast.core, bf16[2,4,128,256]{3,2,1,0:T(8,128)(2,1)S(1)} %collective-permute-done.n, ...), custom_call_target="tpu_custom_call" | custom-call | flops 2013265920 | bytes 10485760 | tf_op jit(solution)/shard_map/pallas_call | solution.py:65
  22.5 1.9 %collective-permute-start.3 = (bf16[12,256,128]{2,1,0:T(8,128)(2,1)S(1)}, bf16[12,256,128]{2,1,0:T(8,128)(2,1)S(1)}, u32[]{:S(2)}, u32[]{:S(2)}) collective-permute-start(bf16[12,256,128]{2,1,0:T(8,128)(2,1)S(1)} %get-tuple-element.42), channel_id=1, source_target_pairs={{0,1},{1,0},{2,3},{3,2},{4,5},{5,4},{6,7},{7,6},{8,9},{9,8},{10,11... | collective-permute-start | bytes 2359304 | tf_op jit(solution)/shard_map/ppermute | solution.py:336
  24.4 2.4 %collective-permute-start.4 = (bf16[2,1,128,256]{3,2,1,0:T(8,128)(2,1)}, bf16[2,1,128,256]{3,2,1,0:T(8,128)(2,1)S(1)}, u32[]{:S(2)}, u32[]{:S(2)}) collective-permute-start(bf16[2,1,128,256]{3,2,1,0:T(8,128)(2,1)} %get-tuple-element.43), channel_id=1, source_target_pairs={{0,1},{1,0},{2,3},{3,2},{4,5},{5,4},{6,7},{7,6},{8,9},{9,8},{10,11... | collective-permute-start | bytes 393224 | tf_op jit(solution)/shard_map/ppermute | solution.py:279
  26.8 1.2 %shard_map.80 = bf16[16,32,768]{2,1,0:T(8,128)(2,1)} custom-call(f32[12,256,128]{2,1,0:T(8,128)S(1)} %get-tuple-element.41.keep, bf16[12,256,128]{2,1,0:T(8,128)(2,1)S(1)} %collective-permute-done.3.got), custom_call_target="tpu_custom_call" | custom-call | flops 1048576 | bytes 4194304 | tf_op jit(solution)/shard_map/pallas_call | solution.py:65
  28.1 9.2 %all-to-all-start = ((bf16[16,32,768]{2,1,0:T(8,128)(2,1)}), bf16[16,32,768]{2,1,0:T(8,128)(2,1)S(1)}, u32[]{:S(2)}, u32[]{:S(2)}) async-start(bf16[16,32,768]{2,1,0:T(8,128)(2,1)} %shard_map.80), calls=%async_computation | async-start | bytes 1572864 | tf_op jit(solution)/shard_map/all_to_all | solution.py:338
  37.3 0.9 %copy-done.7 = bf16[2,1,128,256]{3,2,1,0:T(8,128)(2,1)S(1)} copy-done((bf16[2,1,128,256]{3,2,1,0:T(8,128)(2,1)S(1)}, bf16[2,1,128,256]{3,2,1,0:T(8,128)(2,1)}, u32[]{:S(2)}) %copy-start.7) | copy-done | bytes 131096
  38.1 0.7 collective-permute-start.5
  38.8 0.6 copy-done.4
  39.5 4.9 %collective-permute-start.6 = (bf16[2,4,128,256]{3,2,1,0:T(8,128)(2,1)S(1)}, bf16[2,4,128,256]{3,2,1,0:T(8,128)(2,1)S(1)}, u32[]{:S(2)}, u32[]{:S(2)}) collective-permute-start(bf16[2,4,128,256]{3,2,1,0:T(8,128)(2,1)S(1)} %get-tuple-element.49.hid), channel_id=1, source_target_pairs={{0,64},{64,128},{128,192},{192,256},{256,320},{320,384},{384,448},... | collective-permute-start | bytes 1572872 | tf_op jit(solution)/shard_map/ppermute | solution.py:344
  44.4 5.7 %all-to-all-done.got = bf16[16,32,768]{2,1,0:T(8,128)(2,1)S(1)} async-done(((bf16[16,32,768]{2,1,0:T(8,128)(2,1)}), bf16[16,32,768]{2,1,0:T(8,128)(2,1)S(1)}, u32[]{:S(2)}, u32[]{:S(2)}) %all-to-all-start) | async-done | bytes 786464 | tf_op jit(solution)/shard_map/all_to_all | solution.py:338
  50.0 0.9 %shard_map.82 = f32[16,4,384]{2,1,0:T(4,128)} custom-call(bf16[16,32,768]{2,1,0:T(8,128)(2,1)S(1)} %all-to-all-done.got), custom_call_target="tpu_custom_call" | custom-call | flops 1048576 | bytes 1048576 | tf_op jit(solution)/shard_map/pallas_call | solution.py:65
  51.0 12.7 %all-to-all-start.1 = ((f32[16,4,384]{2,1,0:T(4,128)}), f32[16,4,384]{2,1,0:T(4,128)S(1)}, u32[]{:S(2)}, u32[]{:S(2)}) async-start(f32[16,4,384]{2,1,0:T(4,128)} %shard_map.82), calls=%async_computation.1 | async-start | bytes 196608 | tf_op jit(solution)/shard_map/all_to_all | solution.py:361
  63.7 1.4 %shard_map.83 = bf16[2,4,128,256]{3,2,1,0:T(8,128)(2,1)} custom-call(bf16[2,4,128,256]{3,2,1,0:T(8,128)(2,1)S(1)} %get-tuple-element.49.hid, bf16[2,4,128,256]{3,2,1,0:T(8,128)(2,1)S(1)} %collective-permute-done.6.past, bf16[3,256,256]{2,1,0:T(8,128)(2,1)S(1)} %copy-done.1), custom_call_target="tpu_custom_call" | custom-call | flops 402653184 | bytes 2097152 | tf_op jit(solution)/shard_map/pallas_call | solution.py:65
  65.1 2.2 %shard_map.84 = bf16[2,4,128,256]{3,2,1,0:T(8,128)(2,1)} custom-call(s32[1]{0:T(128)} %bitcast.core, bf16[2,4,128,256]{3,2,1,0:T(8,128)(2,1)S(1)} %copy-done.6, bf16[2,1,128,256]{3,2,1,0:T(8,128)(2,1)S(1)} %collective-permute-done.4.rows.pair, bf16[2,1,128,256]{3,2,1,0:T(8,128)(2,1)S(1)} %copy-done.5, bf16[9,256,256]{2,1,0:T(8,128)(2,1)S(1)} %copy-done, ...), custom_call_target="tpu_custom_call" | custom-call | flops 1207959552 | bytes 4194304 | tf_op jit(solution)/shard_map/pallas_call | solution.py:65
  67.3 9.5 %all-to-all-done.1.got = f32[16,4,384]{2,1,0:T(4,128)S(1)} async-done(((f32[16,4,384]{2,1,0:T(4,128)}), f32[16,4,384]{2,1,0:T(4,128)S(1)}, u32[]{:S(2)}, u32[]{:S(2)}) %all-to-all-start.1) | async-done | bytes 98336 | tf_op jit(solution)/shard_map/all_to_all | solution.py:361
  76.8 0.7 shard_map.85
  (21 shorter events, 0.4 us)
Async XLA Ops:
  0.6 19.4 %collective-permute-start = (bf16[2,4,128,256]{3,2,1,0:T(8,128)(2,1)}, bf16[2,4,128,256]{3,2,1,0:T(8,128)(2,1)S(1)}, u32[]{:S(2)}, u32[]{:S(2)}) collective-permute-start(bf16[2,4,128,256]{3,2,1,0:T(8,128)(2,1)} %g.1), channel_id=1, source_target_pairs={{64,0},{128,64},{192,128},{256,192},{320,256},{384,320},{448,384},... | collective-permute-start | bytes 1572872 | tf_op jit(solution)/shard_map/ppermute | solution.py:292
  3.3 1.0 %copy-start.1 = (bf16[3,256,256]{2,1,0:T(8,128)(2,1)S(1)}, bf16[3,256,256]{2,1,0:T(8,128)(2,1)}, u32[]{:S(2)}) copy-start(bf16[3,256,256]{2,1,0:T(8,128)(2,1)} %wt.5) | copy-start | bytes 1179652
  3.3 1.2 %copy-start.2 = (bf16[2,4,128,256]{3,2,1,0:T(8,128)(2,1)S(1)}, bf16[2,4,128,256]{3,2,1,0:T(8,128)(2,1)}, u32[]{:S(2)}) copy-start(bf16[2,4,128,256]{3,2,1,0:T(8,128)(2,1)} %x.3) | copy-start | bytes 1572868
  3.3 1.3 %copy-start.3 = (bf16[2,4,128,256]{3,2,1,0:T(8,128)(2,1)S(1)}, bf16[2,4,128,256]{3,2,1,0:T(8,128)(2,1)}, u32[]{:S(2)}) copy-start(bf16[2,4,128,256]{3,2,1,0:T(8,128)(2,1)} %g.1) | copy-start | bytes 1572868
  4.6 3.1 %copy-start = (bf16[9,256,256]{2,1,0:T(8,128)(2,1)S(1)}, bf16[9,256,256]{2,1,0:T(8,128)(2,1)}, u32[]{:S(2)}) copy-start(bf16[9,256,256]{2,1,0:T(8,128)(2,1)} %ws.5) | copy-start | bytes 3538948
  5.1 3.9 %collective-permute-start.1 = (bf16[2,1,128,256]{3,2,1,0:T(8,128)(2,1)S(1)}, bf16[2,1,128,256]{3,2,1,0:T(8,128)(2,1)S(1)}, u32[]{:S(2)}, u32[]{:S(2)}) collective-permute-start(bf16[2,1,128,256]{3,2,1,0:T(8,128)(2,1)S(1)} %get-tuple-element.33), channel_id=1, source_target_pairs={{0,1},{1,0},{2,3},{3,2},{4,5},{5,4},{6,7},{7,6},{8,9},{9,8},{10,11... | collective-permute-start | bytes 393224 | tf_op jit(solution)/shard_map/ppermute | solution.py:279
  7.1 2.0 %collective-permute-start.2 = (bf16[2,1,128,256]{3,2,1,0:T(8,128)(2,1)S(1)}, bf16[2,1,128,256]{3,2,1,0:T(8,128)(2,1)S(1)}, u32[]{:S(2)}, u32[]{:S(2)}) collective-permute-start(bf16[2,1,128,256]{3,2,1,0:T(8,128)(2,1)S(1)} %get-tuple-element.34), channel_id=1, source_target_pairs={{1,2},{3,4},{5,6},{7,8},{9,10},{11,12},{13,14},{15,16},{17,18},{19... | collective-permute-start | bytes 393224 | tf_op jit(solution)/shard_map/ppermute | solution.py:284
  22.5 4.3 %collective-permute-start.3 = (bf16[12,256,128]{2,1,0:T(8,128)(2,1)S(1)}, bf16[12,256,128]{2,1,0:T(8,128)(2,1)S(1)}, u32[]{:S(2)}, u32[]{:S(2)}) collective-permute-start(bf16[12,256,128]{2,1,0:T(8,128)(2,1)S(1)} %get-tuple-element.42), channel_id=1, source_target_pairs={{0,1},{1,0},{2,3},{3,2},{4,5},{5,4},{6,7},{7,6},{8,9},{9,8},{10,11... | collective-permute-start | bytes 2359304 | tf_op jit(solution)/shard_map/ppermute | solution.py:336
  24.4 12.9 %collective-permute-start.4 = (bf16[2,1,128,256]{3,2,1,0:T(8,128)(2,1)}, bf16[2,1,128,256]{3,2,1,0:T(8,128)(2,1)S(1)}, u32[]{:S(2)}, u32[]{:S(2)}) collective-permute-start(bf16[2,1,128,256]{3,2,1,0:T(8,128)(2,1)} %get-tuple-element.43), channel_id=1, source_target_pairs={{0,1},{1,0},{2,3},{3,2},{4,5},{5,4},{6,7},{7,6},{8,9},{9,8},{10,11... | collective-permute-start | bytes 393224 | tf_op jit(solution)/shard_map/ppermute | solution.py:279
  28.1 22.0 %all-to-all-start = ((bf16[16,32,768]{2,1,0:T(8,128)(2,1)}), bf16[16,32,768]{2,1,0:T(8,128)(2,1)S(1)}, u32[]{:S(2)}, u32[]{:S(2)}) async-start(bf16[16,32,768]{2,1,0:T(8,128)(2,1)} %shard_map.80), calls=%async_computation | async-start | bytes 1572864 | tf_op jit(solution)/shard_map/all_to_all | solution.py:338
  37.2 0.9 %copy-start.7 = (bf16[2,1,128,256]{3,2,1,0:T(8,128)(2,1)S(1)}, bf16[2,1,128,256]{3,2,1,0:T(8,128)(2,1)}, u32[]{:S(2)}) copy-start(bf16[2,1,128,256]{3,2,1,0:T(8,128)(2,1)} %get-tuple-element.46) | copy-start | bytes 393220
  38.1 0.7 collective-permute-start.5
  38.8 0.7 copy-start.4
  39.5 24.2 %collective-permute-start.6 = (bf16[2,4,128,256]{3,2,1,0:T(8,128)(2,1)S(1)}, bf16[2,4,128,256]{3,2,1,0:T(8,128)(2,1)S(1)}, u32[]{:S(2)}, u32[]{:S(2)}) collective-permute-start(bf16[2,4,128,256]{3,2,1,0:T(8,128)(2,1)S(1)} %get-tuple-element.49.hid), channel_id=1, source_target_pairs={{0,64},{64,128},{128,192},{192,256},{256,320},{320,384},{384,448},... | collective-permute-start | bytes 1572872 | tf_op jit(solution)/shard_map/ppermute | solution.py:344
  51.0 14.1 %copy-start.5 = (bf16[2,1,128,256]{3,2,1,0:T(8,128)(2,1)S(1)}, bf16[2,1,128,256]{3,2,1,0:T(8,128)(2,1)}, u32[]{:S(2)}) copy-start(bf16[2,1,128,256]{3,2,1,0:T(8,128)(2,1)} %copy-done.4) | copy-start | bytes 393220
  51.0 14.1 %copy-start.6 = (bf16[2,4,128,256]{3,2,1,0:T(8,128)(2,1)S(1)}, bf16[2,4,128,256]{3,2,1,0:T(8,128)(2,1)}, u32[]{:S(2)}) copy-start(bf16[2,4,128,256]{3,2,1,0:T(8,128)(2,1)} %get-tuple-element.51.gpre) | copy-start | bytes 1572868
  51.0 25.8 %all-to-all-start.1 = ((f32[16,4,384]{2,1,0:T(4,128)}), f32[16,4,384]{2,1,0:T(4,128)S(1)}, u32[]{:S(2)}, u32[]{:S(2)}) async-start(f32[16,4,384]{2,1,0:T(4,128)} %shard_map.82), calls=%async_computation.1 | async-start | bytes 196608 | tf_op jit(solution)/shard_map/all_to_all | solution.py:361

commit v6 on v5

--- a/solution.py
+++ b/solution.py
@@ -205,25 +205,35 @@
         copy.wait()
 
 
-def pair_kernel(keep, got, out_ref):
+def pair_kernel(keep, got, chip, out_hbm, out_ref, sems):
     half = C // 4
+    copies = []
     for p in range(TAPS // 2):
         s0 = keep[2 * p] + got[2 * p].astype(F32)
         s1 = keep[2 * p + 1] + got[2 * p + 1].astype(F32)
         low = jnp.concatenate([s0[:, :half], s1[:, :half]], 1).astype(BF16)
         high = jnp.concatenate([s0[:, half:], s1[:, half:]], 1).astype(BF16)
         for a in range(8):
-            out_ref[2 * a, :, p * 128 : (p + 1) * 128] = low[32 * a : 32 * a + 32]
-            out_ref[2 * a + 1, :, p * 128 : (p + 1) * 128] = high[32 * a : 32 * a + 32]
-
-
-def plane_kernel(got, out_ref):
+            out_ref[a, 32 * p : 32 * p + 32] = low[32 * a : 32 * a + 32]
+            out_ref[8 + a, 32 * p : 32 * p + 32] = high[32 * a : 32 * a + 32]
+        if p % 2 == 1:
+            part = pl.ds(32 * (p - 1), 64)
+            copy = pltpu.make_async_copy(
+                out_ref.at[:, part], out_hbm.at[:, part], sems.at[p // 2]
+            )
+            copy.start()
+            copies.append(copy)
+    for copy in copies:
+        copy.wait()
+
+
+def plane_kernel(got, pair, chip, out_ref):
     total = got[0].astype(F32)
     for n in range(1, 16):
         total = total + got[n].astype(F32)
     pieces = []
     for p in range(TAPS // 2):
-        flipped = total[:, p * 128 : (p + 1) * 128].T
+        flipped = total[32 * p : 32 * p + 32].T
         pieces += [flipped[:64], flipped[64:]]
     wide = jnp.concatenate(pieces, 1)
     for z in range(16):
@@ -240,7 +250,8 @@
         gt_ref[t] = total[:, 32 * (9 + t) : 32 * (9 + t) + 32]
 
 
-def token_kernel(rows, out_ref):
+def token_kernel(*refs):
+    out_ref = refs[-1]
     out_ref[...] = jnp.zeros(out_ref.shape, F32)
 
 
@@ -253,7 +264,7 @@
     out_ref[1] = second.astype(BF16).reshape(ROWS, COLS, C)
 
 
-def back_kernel(core, gpre, pair, chip, ws, token, out_ref):
+def back_kernel(core, gpre, pair, chip, ws, token, arrived, out_ref):
     for f in range(2):
         low, high = low_high(core, pair[f, 0], chip[f, 0])
         own = gpre[f].reshape(PIX, C)
@@ -323,26 +334,31 @@
         (
             hbm((2, ROWS, COLS, C), BF16),
             hbm((2, 1, COLS, C), BF16),
-            hbm((2, 1, COLS, C), BF16),
+            vmem((2, 1, COLS, C), BF16),
             vmem((TAPS, C, C // 2), F32),
             vmem((TAPS, C, C // 2), BF16),
         ),
         15 * TAP_FLOPS,
         10 << 20,
         core, later, gh_part, factor, xt, xe, ht, gt_part, w_time, order,
-        hbm_out=(0, 1, 2),
+        hbm_out=(0, 1),
         scratch=[pltpu.VMEM((2, ROWS, COLS, C), BF16), pltpu.SemaphoreType.DMA((3,))],
     )
     got = lax.ppermute(send, "c", [(0, 1), (1, 0)])
-    chunks = call(pair_kernel, shape((16, 32, 768), BF16), 1 << 20, 4 << 20, keep, got)
-    chunks = lax.all_to_all(chunks, ("tm", "xl"), split_axis=0, concat_axis=0, tiled=True)
+    chunks = call(
+        pair_kernel, hbm((16, 192, 128), BF16), 1 << 20, 4 << 20, keep, got, chip,
+        hbm_out=(0,),
+        scratch=[pltpu.VMEM((16, 192, 128), BF16), pltpu.SemaphoreType.DMA((3,))],
+    )
+    chunks = lax.all_to_all(chunks, ("xl", "tm"), split_axis=0, concat_axis=0, tiled=True)
     pair = to_pair(pair)
-    token = call(token_kernel, shape((8, 128), F32), HINT, 1 << 12, pair, hbm_in=(0,))
+    token = call(token_kernel, shape((8, 128), F32), HINT, 1 << 12, pair, chip, hbm_in=(0,))
     chip, token = lax.optimization_barrier((chip, token))
     chip = to_chip(chip)
-    hidden, chip = lax.optimization_barrier((hidden, chip))
+    arrived = call(token_kernel, shape((8, 128), F32), 0, 1 << 12, chip, pair, hbm_in=(0, 1))
+    hidden, arrived = lax.optimization_barrier((hidden, arrived))
     past = lax.ppermute(hidden, "tm", forward)
-    chunks, pair, chip = lax.optimization_barrier((chunks, pair, chip))
+    chunks, arrived = lax.optimization_barrier((chunks, arrived))
     block_out = call(
         out_kernel,
         shape((2, ROWS, COLS, C), BF16),
@@ -355,9 +371,9 @@
         shape((2, ROWS, COLS, C), BF16),
         9 * TAP_FLOPS,
         4 << 20,
-        core, grad_pre, pair, chip, w_space, token,
-    )
-    rows = call(plane_kernel, shape((16, 4, 384), F32), 1 << 20, 1 << 20, chunks)
+        core, grad_pre, pair, chip, w_space, token, arrived,
+    )
+    rows = call(plane_kernel, shape((16, 4, 384), F32), 1 << 20, 1 << 20, chunks, pair, chip)
     rows = lax.all_to_all(rows, "z", split_axis=0, concat_axis=0, tiled=True)
     rows, block_out = lax.optimization_barrier((rows, block_out))
     grad_space, grad_time = call(

time: 78 us -> 77.3 us (level)
  starting transfers between devices: 37 us -> 35.9 us
    all_to_all x1, starting transfers between devices: 12.7 us -> 11.6 us  [body(): rows = lax.all_to_all(rows, 'z', split_axis=0, concat_axis=0, tiled=True)]
    all_to_all x1, waiting for transfers between devices: 9.47 us -> 8.46 us  [body(): rows = lax.all_to_all(rows, 'z', split_axis=0, concat_axis=0, tiled=True)]
    all_to_all x1, waiting for transfers between devices: 5.67 us -> 6.65 us  [body(): lax.all_to_all(chunks, ('xl', 'tm'), split_axis=0, concat_axis=0, tiled=T...]
    unnamed x16 -> x12, local copies, waits for them, and re-layouts: 2.79 us -> 2.26 us
    pallas_call x11 -> x12, Pallas kernels: 11.6 us -> 11.9 us  [call(): pl.pallas_call(kernel, out_shape=out_shape, in_specs=in_specs, out_specs=...]
where the time goes in v6:
time: 77.3 us; the launch traced here: 76 us
  starting transfers between devices  35.9 us (46%)
  waiting for transfers between devices  25.1 us (32%)
  Pallas kernels  11.9 us (15%)
  local copies, waits for them, and re-layouts  2.26 us (3%)
  between operations  0.85 us (1%)
    pallas_call x12, Pallas kernels, call(): pl.pallas_call(kernel, out_shape=out_shape, in_specs=in_specs, out_specs=...  11.9 us
    all_to_all x1, starting transfers between devices, body(): rows = lax.all_to_all(rows, 'z', split_axis=0, concat_axis=0, tiled=True)  11.6 us
    ppermute x1, waiting for transfers between devices, body(): later = lax.ppermute(grad_out, 'tm', backward)  9.98 us
    all_to_all x1, starting transfers between devices, body(): lax.all_to_all(chunks, ('xl', 'tm'), split_axis=0, concat_axis=0, tiled=T...  9.19 us
    all_to_all x1, waiting for transfers between devices, body(): rows = lax.all_to_all(rows, 'z', split_axis=0, concat_axis=0, tiled=True)  8.46 us
    all_to_all x1, waiting for transfers between devices, body(): lax.all_to_all(chunks, ('xl', 'tm'), split_axis=0, concat_axis=0, tiled=T...  6.65 us
    ppermute x1, starting transfers between devices, body(): past = lax.ppermute(hidden, 'tm', forward)  4.88 us
    ppermute x2, starting transfers between devices, to_pair(): return lax.ppermute(rows, 'c', [(0, 1), (1, 0)])  4.33 us
  transfers between devices with their start and end apart: 9, of which 3 were waited for; matrix products, arithmetic and copies ran while one was open for 0% of the time, Pallas kernels for 11%

profile of v6, /device:TPU:24, one launch (start us, length us, event | category | flops | bytes accessed | tf_op | source)
XLA Modules:
  0.0 76.0 jit_solution(5808896135437150341)
XLA Ops:
  0.6 2.7 %collective-permute-start = (bf16[2,4,128,256]{3,2,1,0:T(8,128)(2,1)}, bf16[2,4,128,256]{3,2,1,0:T(8,128)(2,1)S(1)}, u32[]{:S(2)}, u32[]{:S(2)}) collective-permute-start(bf16[2,4,128,256]{3,2,1,0:T(8,128)(2,1)} %g.1), channel_id=1, source_target_pairs={{64,0},{128,64},{192,128},{256,192},{320,256},{384,320},{448,384},... | collective-permute-start | bytes 1572872 | tf_op jit(solution)/shard_map/ppermute | solution.py:303
  3.4 0.9 %copy-done.1 = bf16[3,256,256]{2,1,0:T(8,128)(2,1)S(1)} copy-done((bf16[3,256,256]{2,1,0:T(8,128)(2,1)S(1)}, bf16[3,256,256]{2,1,0:T(8,128)(2,1)}, u32[]{:S(2)}) %copy-start.1) | copy-done | bytes 393240
  4.3 0.2 copy-done.3
  4.6 0.5 shard_map.76
  5.1 1.9 %collective-permute-start.1 = (bf16[2,1,128,256]{3,2,1,0:T(8,128)(2,1)S(1)}, bf16[2,1,128,256]{3,2,1,0:T(8,128)(2,1)S(1)}, u32[]{:S(2)}, u32[]{:S(2)}) collective-permute-start(bf16[2,1,128,256]{3,2,1,0:T(8,128)(2,1)S(1)} %get-tuple-element.32), channel_id=1, source_target_pairs={{0,1},{1,0},{2,3},{3,2},{4,5},{5,4},{6,7},{7,6},{8,9},{9,8},{10,11... | collective-permute-start | bytes 393224 | tf_op jit(solution)/shard_map/ppermute | solution.py:290
  7.1 0.7 collective-permute-start.2
  7.8 1.3 %shard_map.77 = (f32[2,512,256]{2,1,0:T(8,128)S(1)}, bf16[3,2,256,512]{3,2,1,0:T(8,128)(2,1)S(1)}) custom-call(bf16[2,4,128,256]{3,2,1,0:T(8,128)(2,1)S(1)} %copy-done.3, bf16[9,256,256]{2,1,0:T(8,128)(2,1)S(1)} %copy-done), custom_call_target="tpu_custom_call" | custom-call | flops 1207959552 | bytes 4194304 | tf_op jit(solution)/shard_map/pallas_call | solution.py:65
  9.1 0.9 %shard_map.78 = (bf16[2,4,128,256]{3,2,1,0:T(8,128)(2,1)S(1)}, f32[2,512,256]{2,1,0:T(8,128)S(1)}, bf16[2,256,512]{2,1,0:T(8,128)(2,1)S(1)}, bf16[3,2,2,256,128]{4,3,2,1,0:T(8,128)(2,1)S(1)}, f32[2,256,256]{2,1,0:T(8,128)S(1)}) custom-call(s32[1]{0:T(128)} %bitcast.core, f32[2,512,256]{2,1,0:T(8,128)S(1)} %get-tuple-element.31.pre, ...), custom_call_target="tpu_custom_call" | custom-call | flops 671088640 | bytes 8388608 | tf_op jit(solution)/shard_map/pallas_call | solution.py:65
  10.0 10.0 %collective-permute-done.n = bf16[2,4,128,256]{3,2,1,0:T(8,128)(2,1)S(1)} collective-permute-done((bf16[2,4,128,256]{3,2,1,0:T(8,128)(2,1)}, bf16[2,4,128,256]{3,2,1,0:T(8,128)(2,1)S(1)}, u32[]{:S(2)}, u32[]{:S(2)}) %collective-permute-start) | collective-permute-done | bytes 524320 | tf_op jit(solution)/shard_map/ppermute | solution.py:303
  20.0 2.7 %shard_map.79 = (bf16[2,4,128,256]{3,2,1,0:T(8,128)(2,1)}, bf16[2,1,128,256]{3,2,1,0:T(8,128)(2,1)}, bf16[2,1,128,256]{3,2,1,0:T(8,128)(2,1)S(1)}, f32[12,256,128]{2,1,0:T(8,128)S(1)}, bf16[12,256,128]{2,1,0:T(8,128)(2,1)S(1)}) custom-call(s32[1]{0:T(128)} %bitcast.core, bf16[2,4,128,256]{3,2,1,0:T(8,128)(2,1)S(1)} %collective-permute-done.n, ...), custom_call_target="tpu_custom_call" | custom-call | flops 2013265920 | bytes 10485760 | tf_op jit(solution)/shard_map/pallas_call | solution.py:65
  22.8 1.9 %collective-permute-start.3 = (bf16[12,256,128]{2,1,0:T(8,128)(2,1)S(1)}, bf16[12,256,128]{2,1,0:T(8,128)(2,1)S(1)}, u32[]{:S(2)}, u32[]{:S(2)}) collective-permute-start(bf16[12,256,128]{2,1,0:T(8,128)(2,1)S(1)} %get-tuple-element.41), channel_id=1, source_target_pairs={{0,1},{1,0},{2,3},{3,2},{4,5},{5,4},{6,7},{7,6},{8,9},{9,8},{10,11... | collective-permute-start | bytes 2359304 | tf_op jit(solution)/shard_map/ppermute | solution.py:347
  24.7 2.4 %collective-permute-start.4 = (bf16[2,1,128,256]{3,2,1,0:T(8,128)(2,1)}, bf16[2,1,128,256]{3,2,1,0:T(8,128)(2,1)S(1)}, u32[]{:S(2)}, u32[]{:S(2)}) collective-permute-start(bf16[2,1,128,256]{3,2,1,0:T(8,128)(2,1)} %get-tuple-element.44), channel_id=1, source_target_pairs={{0,1},{1,0},{2,3},{3,2},{4,5},{5,4},{6,7},{7,6},{8,9},{9,8},{10,11... | collective-permute-start | bytes 393224 | tf_op jit(solution)/shard_map/ppermute | solution.py:290
  27.1 1.1 %shard_map.80 = bf16[16,192,128]{2,1,0:T(8,128)(2,1)} custom-call(f32[12,256,128]{2,1,0:T(8,128)S(1)} %get-tuple-element.40.keep, bf16[12,256,128]{2,1,0:T(8,128)(2,1)S(1)} %collective-permute-done.3.got, bf16[2,1,128,256]{3,2,1,0:T(8,128)(2,1)S(1)} %get-tuple-element.45.chip.refs_1_), custom_call_target="tpu_custom_call" | custom-call | flops 1048576 | bytes 4194304 | tf_op jit(solution)/shard_map/pallas_call | solution.py:65
  28.2 9.2 %all-to-all-start = ((bf16[16,192,128]{2,1,0:T(8,128)(2,1)}), bf16[16,192,128]{2,1,0:T(8,128)(2,1)S(1)}, u32[]{:S(2)}, u32[]{:S(2)}) async-start(bf16[16,192,128]{2,1,0:T(8,128)(2,1)} %shard_map.80), calls=%async_computation | async-start | bytes 1572864 | tf_op jit(solution)/shard_map/all_to_all | solution.py:353
  37.4 0.7 collective-permute-start.5
  38.1 4.9 %collective-permute-start.6 = (bf16[2,4,128,256]{3,2,1,0:T(8,128)(2,1)S(1)}, bf16[2,4,128,256]{3,2,1,0:T(8,128)(2,1)S(1)}, u32[]{:S(2)}, u32[]{:S(2)}) collective-permute-start(bf16[2,4,128,256]{3,2,1,0:T(8,128)(2,1)S(1)} %get-tuple-element.48.hid), channel_id=1, source_target_pairs={{0,64},{64,128},{128,192},{192,256},{256,320},{320,384},{384,448},... | collective-permute-start | bytes 1572872 | tf_op jit(solution)/shard_map/ppermute | solution.py:360
  43.0 6.7 %all-to-all-done.got = bf16[16,192,128]{2,1,0:T(8,128)(2,1)S(1)} async-done(((bf16[16,192,128]{2,1,0:T(8,128)(2,1)}), bf16[16,192,128]{2,1,0:T(8,128)(2,1)S(1)}, u32[]{:S(2)}, u32[]{:S(2)}) %all-to-all-start) | async-done | bytes 786464 | tf_op jit(solution)/shard_map/all_to_all | solution.py:353
  49.7 0.9 %shard_map.83 = f32[16,4,384]{2,1,0:T(4,128)} custom-call(bf16[16,192,128]{2,1,0:T(8,128)(2,1)S(1)} %all-to-all-done.got, bf16[2,1,128,256]{3,2,1,0:T(8,128)(2,1)S(1)} %collective-permute-done.4.refs_0_.refs_1_.pair, bf16[2,1,128,256]{3,2,1,0:T(8,128)(2,1)S(1)} %collective-permute-done.5.refs_0_.chip), custom_call_target="tpu_custom_call" | custom-call | flops 1048576 | bytes 1048576 | tf_op jit(solution)/shard_map/pallas_call | solution.py:65
  50.6 11.6 %all-to-all-start.1 = ((f32[16,4,384]{2,1,0:T(4,128)}), f32[16,4,384]{2,1,0:T(4,128)S(1)}, u32[]{:S(2)}, u32[]{:S(2)}) async-start(f32[16,4,384]{2,1,0:T(4,128)} %shard_map.83), calls=%async_computation.1 | async-start | bytes 196608 | tf_op jit(solution)/shard_map/all_to_all | solution.py:377
  62.3 1.0 %copy-done.2 = bf16[3,256,256]{2,1,0:T(8,128)(2,1)S(1)} copy-done((bf16[3,256,256]{2,1,0:T(8,128)(2,1)S(1)}, bf16[3,256,256]{2,1,0:T(8,128)(2,1)}, u32[]{:S(2)}) %copy-start.2) | copy-done | bytes 393240
  63.3 1.4 %shard_map.84 = bf16[2,4,128,256]{3,2,1,0:T(8,128)(2,1)} custom-call(bf16[2,4,128,256]{3,2,1,0:T(8,128)(2,1)S(1)} %get-tuple-element.48.hid, bf16[2,4,128,256]{3,2,1,0:T(8,128)(2,1)S(1)} %collective-permute-done.6.past, bf16[3,256,256]{2,1,0:T(8,128)(2,1)S(1)} %copy-done.2), custom_call_target="tpu_custom_call" | custom-call | flops 402653184 | bytes 2097152 | tf_op jit(solution)/shard_map/pallas_call | solution.py:65
  64.6 2.2 %shard_map.85 = bf16[2,4,128,256]{3,2,1,0:T(8,128)(2,1)} custom-call(s32[1]{0:T(128)} %bitcast.core, bf16[2,4,128,256]{3,2,1,0:T(8,128)(2,1)S(1)} %copy-done.5, bf16[2,1,128,256]{3,2,1,0:T(8,128)(2,1)S(1)} %collective-permute-done.4.refs_0_.refs_1_.pair, bf16[2,1,128,256]{3,2,1,0:T(8,128)(2,1)S(1)} %collective-permute-done.5.refs_0_.chip, ...), custom_call_target="tpu_custom_call" | custom-call | flops 1207959552 | bytes 4194304 | tf_op jit(solution)/shard_map/pallas_call | solution.py:65
  66.9 8.5 %all-to-all-done.1.got = f32[16,4,384]{2,1,0:T(4,128)S(1)} async-done(((f32[16,4,384]{2,1,0:T(4,128)}), f32[16,4,384]{2,1,0:T(4,128)S(1)}, u32[]{:S(2)}, u32[]{:S(2)}) %all-to-all-start.1) | async-done | bytes 98336 | tf_op jit(solution)/shard_map/all_to_all | solution.py:377
  75.3 0.7 shard_map.86
  (18 shorter events, 0.2 us)
Async XLA Ops:
  0.6 19.4 %collective-permute-start = (bf16[2,4,128,256]{3,2,1,0:T(8,128)(2,1)}, bf16[2,4,128,256]{3,2,1,0:T(8,128)(2,1)S(1)}, u32[]{:S(2)}, u32[]{:S(2)}) collective-permute-start(bf16[2,4,128,256]{3,2,1,0:T(8,128)(2,1)} %g.1), channel_id=1, source_target_pairs={{64,0},{128,64},{192,128},{256,192},{320,256},{384,320},{448,384},... | collective-permute-start | bytes 1572872 | tf_op jit(solution)/shard_map/ppermute | solution.py:303
  3.3 1.0 %copy-start.1 = (bf16[3,256,256]{2,1,0:T(8,128)(2,1)S(1)}, bf16[3,256,256]{2,1,0:T(8,128)(2,1)}, u32[]{:S(2)}) copy-start(bf16[3,256,256]{2,1,0:T(8,128)(2,1)} %wt.5) | copy-start | bytes 1179652
  3.3 1.2 %copy-start.3 = (bf16[2,4,128,256]{3,2,1,0:T(8,128)(2,1)S(1)}, bf16[2,4,128,256]{3,2,1,0:T(8,128)(2,1)}, u32[]{:S(2)}) copy-start(bf16[2,4,128,256]{3,2,1,0:T(8,128)(2,1)} %x.3) | copy-start | bytes 1572868
  3.3 1.3 %copy-start.4 = (bf16[2,4,128,256]{3,2,1,0:T(8,128)(2,1)S(1)}, bf16[2,4,128,256]{3,2,1,0:T(8,128)(2,1)}, u32[]{:S(2)}) copy-start(bf16[2,4,128,256]{3,2,1,0:T(8,128)(2,1)} %g.1) | copy-start | bytes 1572868
  4.6 3.1 %copy-start = (bf16[9,256,256]{2,1,0:T(8,128)(2,1)S(1)}, bf16[9,256,256]{2,1,0:T(8,128)(2,1)}, u32[]{:S(2)}) copy-start(bf16[9,256,256]{2,1,0:T(8,128)(2,1)} %ws.5) | copy-start | bytes 3538948
  5.1 3.9 %collective-permute-start.1 = (bf16[2,1,128,256]{3,2,1,0:T(8,128)(2,1)S(1)}, bf16[2,1,128,256]{3,2,1,0:T(8,128)(2,1)S(1)}, u32[]{:S(2)}, u32[]{:S(2)}) collective-permute-start(bf16[2,1,128,256]{3,2,1,0:T(8,128)(2,1)S(1)} %get-tuple-element.32), channel_id=1, source_target_pairs={{0,1},{1,0},{2,3},{3,2},{4,5},{5,4},{6,7},{7,6},{8,9},{9,8},{10,11... | collective-permute-start | bytes 393224 | tf_op jit(solution)/shard_map/ppermute | solution.py:290
  7.1 2.0 %collective-permute-start.2 = (bf16[2,1,128,256]{3,2,1,0:T(8,128)(2,1)S(1)}, bf16[2,1,128,256]{3,2,1,0:T(8,128)(2,1)S(1)}, u32[]{:S(2)}, u32[]{:S(2)}) collective-permute-start(bf16[2,1,128,256]{3,2,1,0:T(8,128)(2,1)S(1)} %get-tuple-element.33), channel_id=1, source_target_pairs={{1,2},{3,4},{5,6},{7,8},{9,10},{11,12},{13,14},{15,16},{17,18},{19... | collective-permute-start | bytes 393224 | tf_op jit(solution)/shard_map/ppermute | solution.py:295
  22.8 4.3 %collective-permute-start.3 = (bf16[12,256,128]{2,1,0:T(8,128)(2,1)S(1)}, bf16[12,256,128]{2,1,0:T(8,128)(2,1)S(1)}, u32[]{:S(2)}, u32[]{:S(2)}) collective-permute-start(bf16[12,256,128]{2,1,0:T(8,128)(2,1)S(1)} %get-tuple-element.41), channel_id=1, source_target_pairs={{0,1},{1,0},{2,3},{3,2},{4,5},{5,4},{6,7},{7,6},{8,9},{9,8},{10,11... | collective-permute-start | bytes 2359304 | tf_op jit(solution)/shard_map/ppermute | solution.py:347
  24.7 12.7 %collective-permute-start.4 = (bf16[2,1,128,256]{3,2,1,0:T(8,128)(2,1)}, bf16[2,1,128,256]{3,2,1,0:T(8,128)(2,1)S(1)}, u32[]{:S(2)}, u32[]{:S(2)}) collective-permute-start(bf16[2,1,128,256]{3,2,1,0:T(8,128)(2,1)} %get-tuple-element.44), channel_id=1, source_target_pairs={{0,1},{1,0},{2,3},{3,2},{4,5},{5,4},{6,7},{7,6},{8,9},{9,8},{10,11... | collective-permute-start | bytes 393224 | tf_op jit(solution)/shard_map/ppermute | solution.py:290
  28.2 21.4 %all-to-all-start = ((bf16[16,192,128]{2,1,0:T(8,128)(2,1)}), bf16[16,192,128]{2,1,0:T(8,128)(2,1)S(1)}, u32[]{:S(2)}, u32[]{:S(2)}) async-start(bf16[16,192,128]{2,1,0:T(8,128)(2,1)} %shard_map.80), calls=%async_computation | async-start | bytes 1572864 | tf_op jit(solution)/shard_map/all_to_all | solution.py:353
  37.4 0.7 collective-permute-start.5
  38.1 24.1 %collective-permute-start.6 = (bf16[2,4,128,256]{3,2,1,0:T(8,128)(2,1)S(1)}, bf16[2,4,128,256]{3,2,1,0:T(8,128)(2,1)S(1)}, u32[]{:S(2)}, u32[]{:S(2)}) collective-permute-start(bf16[2,4,128,256]{3,2,1,0:T(8,128)(2,1)S(1)} %get-tuple-element.48.hid), channel_id=1, source_target_pairs={{0,64},{64,128},{128,192},{192,256},{256,320},{320,384},{384,448},... | collective-permute-start | bytes 1572872 | tf_op jit(solution)/shard_map/ppermute | solution.py:360
  50.6 24.7 %all-to-all-start.1 = ((f32[16,4,384]{2,1,0:T(4,128)}), f32[16,4,384]{2,1,0:T(4,128)S(1)}, u32[]{:S(2)}, u32[]{:S(2)}) async-start(f32[16,4,384]{2,1,0:T(4,128)} %shard_map.83), calls=%async_computation.1 | async-start | bytes 196608 | tf_op jit(solution)/shard_map/all_to_all | solution.py:377
  62.3 1.0 %copy-start.2 = (bf16[3,256,256]{2,1,0:T(8,128)(2,1)S(1)}, bf16[3,256,256]{2,1,0:T(8,128)(2,1)}, u32[]{:S(2)}) copy-start(bf16[3,256,256]{2,1,0:T(8,128)(2,1)} %wt.5) | copy-start | bytes 1179652
  63.3 1.4 %copy-start.5 = (bf16[2,4,128,256]{3,2,1,0:T(8,128)(2,1)S(1)}, bf16[2,4,128,256]{3,2,1,0:T(8,128)(2,1)}, u32[]{:S(2)}) copy-start(bf16[2,4,128,256]{3,2,1,0:T(8,128)(2,1)} %get-tuple-element.50.gpre) | copy-start | bytes 1572868

commit v7 on v6

--- a/solution.py
+++ b/solution.py
@@ -161,7 +161,7 @@
 
 def grad_kernel(
     core, n, gh, fac, xt, xe, ht, gt, wt, pm,
-    gpre_hbm, pair_hbm, chip_hbm, keep_ref, send_ref,
+    gpre_hbm, pair_hbm, keep_ref, send_ref,
     gpre_ref, sems,
 ):
     def store(tap, value):
@@ -179,8 +179,7 @@
     c = core[0]
     copies = [
         pltpu.make_async_copy(gpre_ref.at[:, pl.ds(3 - 3 * c, 1)], pair_hbm, sems.at[0]),
-        pltpu.make_async_copy(gpre_ref.at[:, pl.ds(3 * c, 1)], chip_hbm, sems.at[1]),
-        pltpu.make_async_copy(gpre_ref, gpre_hbm, sems.at[2]),
+        pltpu.make_async_copy(gpre_ref, gpre_hbm, sems.at[1]),
     ]
     for copy in copies:
         copy.start()
@@ -205,9 +204,11 @@
         copy.wait()
 
 
-def pair_kernel(keep, got, chip, out_hbm, out_ref, sems):
+def pair_kernel(core, keep, got, gpre, out_hbm, chip_ref, out_ref, sems):
     half = C // 4
-    copies = []
+    rows = gpre.at[:, pl.ds(3 * core[0], 1)]
+    copies = [pltpu.make_async_copy(rows, chip_ref, sems.at[3])]
+    copies[0].start()
     for p in range(TAPS // 2):
         s0 = keep[2 * p] + got[2 * p].astype(F32)
         s1 = keep[2 * p + 1] + got[2 * p + 1].astype(F32)
@@ -329,12 +330,11 @@
         8 << 20,
         core, pre_part, pair, chip, w_space, gp,
     )
-    grad_pre, pair, chip, keep, send = call(
+    grad_pre, pair, keep, send = call(
         grad_kernel,
         (
             hbm((2, ROWS, COLS, C), BF16),
             hbm((2, 1, COLS, C), BF16),
-            vmem((2, 1, COLS, C), BF16),
             vmem((TAPS, C, C // 2), F32),
             vmem((TAPS, C, C // 2), BF16),
         ),
@@ -342,13 +342,18 @@
         10 << 20,
         core, later, gh_part, factor, xt, xe, ht, gt_part, w_time, order,
         hbm_out=(0, 1),
-        scratch=[pltpu.VMEM((2, ROWS, COLS, C), BF16), pltpu.SemaphoreType.DMA((3,))],
+        scratch=[pltpu.VMEM((2, ROWS, COLS, C), BF16), pltpu.SemaphoreType.DMA((2,))],
     )
     got = lax.ppermute(send, "c", [(0, 1), (1, 0)])
-    chunks = call(
-        pair_kernel, hbm((16, 192, 128), BF16), 1 << 20, 4 << 20, keep, got, chip,
+    chunks, chip = call(
+        pair_kernel,
+        (hbm((16, 192, 128), BF16), vmem((2, 1, COLS, C), BF16)),
+        1 << 20,
+        4 << 20,
+        core, keep, got, pltpu.with_memory_space_constraint(grad_pre, pltpu.HBM),
+        hbm_in=(3,),
         hbm_out=(0,),
-        scratch=[pltpu.VMEM((16, 192, 128), BF16), pltpu.SemaphoreType.DMA((3,))],
+        scratch=[pltpu.VMEM((16, 192, 128), BF16), pltpu.SemaphoreType.DMA((4,))],
     )
     chunks = lax.all_to_all(chunks, ("xl", "tm"), split_axis=0, concat_axis=0, tiled=True)
     pair = to_pair(pair)

time: 77.3 us -> 77 us (level)
  waiting for transfers between devices: 25.1 us -> 23.9 us
    all_to_all x1, waiting for transfers between devices: 8.46 us -> 7.29 us  [body(): rows = lax.all_to_all(rows, 'z', split_axis=0, concat_axis=0, tiled=True)]
  transfers between devices with their start and end apart: 9 -> 9, of which waited for: 3 -> 3; matrix products, arithmetic and copies ran while one was open for 0% -> 0% of each run, Pallas kernels for 11% -> 12%
where the time goes in v7:
time: 77 us; the launch traced here: 75.6 us
  starting transfers between devices  36.2 us (47%)
  waiting for transfers between devices  23.9 us (31%)
  Pallas kernels  12.5 us (16%)
  local copies, waits for them, and re-layouts  2.26 us (3%)
  between operations  0.85 us (1%)
    pallas_call x12, Pallas kernels, call(): pl.pallas_call(kernel, out_shape=out_shape, in_specs=in_specs, out_specs=...  12.5 us
    all_to_all x1, starting transfers between devices, body(): rows = lax.all_to_all(rows, 'z', split_axis=0, concat_axis=0, tiled=True)  11.8 us
    ppermute x1, waiting for transfers between devices, body(): later = lax.ppermute(grad_out, 'tm', backward)  10 us
    all_to_all x1, starting transfers between devices, body(): lax.all_to_all(chunks, ('xl', 'tm'), split_axis=0, concat_axis=0, tiled=T...  9.16 us
    all_to_all x1, waiting for transfers between devices, body(): rows = lax.all_to_all(rows, 'z', split_axis=0, concat_axis=0, tiled=True)  7.29 us
    all_to_all x1, waiting for transfers between devices, body(): lax.all_to_all(chunks, ('xl', 'tm'), split_axis=0, concat_axis=0, tiled=T...  6.5 us
    ppermute x1, starting transfers between devices, body(): past = lax.ppermute(hidden, 'tm', forward)  5.01 us
    ppermute x2, starting transfers between devices, to_pair(): return lax.ppermute(rows, 'c', [(0, 1), (1, 0)])  4.33 us
  transfers between devices with their start and end apart: 9, of which 3 were waited for; matrix products, arithmetic and copies ran while one was open for 0% of the time, Pallas kernels for 12%

profile of v7, /device:TPU:24, one launch (start us, length us, event | category | flops | bytes accessed | tf_op | source)
XLA Modules:
  0.0 75.6 jit_solution(804271179554143037)
XLA Ops:
  0.6 2.7 %collective-permute-start = (bf16[2,4,128,256]{3,2,1,0:T(8,128)(2,1)}, bf16[2,4,128,256]{3,2,1,0:T(8,128)(2,1)S(1)}, u32[]{:S(2)}, u32[]{:S(2)}) collective-permute-start(bf16[2,4,128,256]{3,2,1,0:T(8,128)(2,1)} %g.1), channel_id=1, source_target_pairs={{64,0},{128,64},{192,128},{256,192},{320,256},{384,320},{448,384},... | collective-permute-start | bytes 1572872 | tf_op jit(solution)/shard_map/ppermute | solution.py:304
  3.4 0.9 %copy-done.2 = bf16[3,256,256]{2,1,0:T(8,128)(2,1)S(1)} copy-done((bf16[3,256,256]{2,1,0:T(8,128)(2,1)S(1)}, bf16[3,256,256]{2,1,0:T(8,128)(2,1)}, u32[]{:S(2)}) %copy-start.2) | copy-done | bytes 393240
  4.3 0.2 copy-done.4
  4.6 0.5 shard_map.76
  5.1 1.9 %collective-permute-start.1 = (bf16[2,1,128,256]{3,2,1,0:T(8,128)(2,1)S(1)}, bf16[2,1,128,256]{3,2,1,0:T(8,128)(2,1)S(1)}, u32[]{:S(2)}, u32[]{:S(2)}) collective-permute-start(bf16[2,1,128,256]{3,2,1,0:T(8,128)(2,1)S(1)} %get-tuple-element.33), channel_id=1, source_target_pairs={{0,1},{1,0},{2,3},{3,2},{4,5},{5,4},{6,7},{7,6},{8,9},{9,8},{10,11... | collective-permute-start | bytes 393224 | tf_op jit(solution)/shard_map/ppermute | solution.py:291
  7.1 0.7 collective-permute-start.2
  7.8 1.3 %shard_map.77 = (f32[2,512,256]{2,1,0:T(8,128)S(1)}, bf16[3,2,256,512]{3,2,1,0:T(8,128)(2,1)S(1)}) custom-call(bf16[2,4,128,256]{3,2,1,0:T(8,128)(2,1)S(1)} %copy-done.4, bf16[9,256,256]{2,1,0:T(8,128)(2,1)S(1)} %copy-done), custom_call_target="tpu_custom_call" | custom-call | flops 1207959552 | bytes 4194304 | tf_op jit(solution)/shard_map/pallas_call | solution.py:65
  9.0 0.9 %shard_map.78 = (bf16[2,4,128,256]{3,2,1,0:T(8,128)(2,1)S(1)}, f32[2,512,256]{2,1,0:T(8,128)S(1)}, bf16[2,256,512]{2,1,0:T(8,128)(2,1)S(1)}, bf16[3,2,2,256,128]{4,3,2,1,0:T(8,128)(2,1)S(1)}, f32[2,256,256]{2,1,0:T(8,128)S(1)}) custom-call(s32[1]{0:T(128)} %bitcast.core, f32[2,512,256]{2,1,0:T(8,128)S(1)} %get-tuple-element.32.pre, ...), custom_call_target="tpu_custom_call" | custom-call | flops 671088640 | bytes 8388608 | tf_op jit(solution)/shard_map/pallas_call | solution.py:65
  10.0 10.0 %collective-permute-done.n = bf16[2,4,128,256]{3,2,1,0:T(8,128)(2,1)S(1)} collective-permute-done((bf16[2,4,128,256]{3,2,1,0:T(8,128)(2,1)}, bf16[2,4,128,256]{3,2,1,0:T(8,128)(2,1)S(1)}, u32[]{:S(2)}, u32[]{:S(2)}) %collective-permute-start) | collective-permute-done | bytes 524320 | tf_op jit(solution)/shard_map/ppermute | solution.py:304
  20.0 2.4 %shard_map.79 = (bf16[2,4,128,256]{3,2,1,0:T(8,128)(2,1)}, bf16[2,1,128,256]{3,2,1,0:T(8,128)(2,1)}, f32[12,256,128]{2,1,0:T(8,128)S(1)}, bf16[12,256,128]{2,1,0:T(8,128)(2,1)S(1)}) custom-call(s32[1]{0:T(128)} %bitcast.core, bf16[2,4,128,256]{3,2,1,0:T(8,128)(2,1)S(1)} %collective-permute-done.n, f32[2,512,256]{2,1,0:T(8,128)S(1)} %get-tuple-element.31.gh, ...), custom_call_target="tpu_custom_call" | custom-call | flops 2013265920 | bytes 10485760 | tf_op jit(solution)/shard_map/pallas_call | solution.py:65
  22.4 1.9 %collective-permute-start.3 = (bf16[12,256,128]{2,1,0:T(8,128)(2,1)S(1)}, bf16[12,256,128]{2,1,0:T(8,128)(2,1)S(1)}, u32[]{:S(2)}, u32[]{:S(2)}) collective-permute-start(bf16[12,256,128]{2,1,0:T(8,128)(2,1)S(1)} %get-tuple-element.42), channel_id=1, source_target_pairs={{0,1},{1,0},{2,3},{3,2},{4,5},{5,4},{6,7},{7,6},{8,9},{9,8},{10,11... | collective-permute-start | bytes 2359304 | tf_op jit(solution)/shard_map/ppermute | solution.py:347
  24.3 2.4 %collective-permute-start.4 = (bf16[2,1,128,256]{3,2,1,0:T(8,128)(2,1)}, bf16[2,1,128,256]{3,2,1,0:T(8,128)(2,1)S(1)}, u32[]{:S(2)}, u32[]{:S(2)}) collective-permute-start(bf16[2,1,128,256]{3,2,1,0:T(8,128)(2,1)} %get-tuple-element.47), channel_id=1, source_target_pairs={{0,1},{1,0},{2,3},{3,2},{4,5},{5,4},{6,7},{7,6},{8,9},{9,8},{10,11... | collective-permute-start | bytes 393224 | tf_op jit(solution)/shard_map/ppermute | solution.py:291
  26.8 1.1 %shard_map.80 = (bf16[16,192,128]{2,1,0:T(8,128)(2,1)}, bf16[2,1,128,256]{3,2,1,0:T(8,128)(2,1)S(1)}) custom-call(s32[1]{0:T(128)} %bitcast.core, f32[12,256,128]{2,1,0:T(8,128)S(1)} %get-tuple-element.41.keep, bf16[12,256,128]{2,1,0:T(8,128)(2,1)S(1)} %collective-permute-done.3.got, bf16[2,4,128,256]{3,2,1,0:T(8,128)(2,1)} %get-tuple-element.43.gpre), custom_call_target="tpu_custom_call" | custom-call | flops 1048576 | bytes 4194304 | tf_op jit(solution)/shard_map/pallas_call | solution.py:65
  27.8 9.2 %all-to-all-start = ((bf16[16,192,128]{2,1,0:T(8,128)(2,1)}), bf16[16,192,128]{2,1,0:T(8,128)(2,1)S(1)}, u32[]{:S(2)}, u32[]{:S(2)}) async-start(bf16[16,192,128]{2,1,0:T(8,128)(2,1)} %get-tuple-element.44), calls=%async_computation | async-start | bytes 1572864 | tf_op jit(solution)/shard_map/all_to_all | solution.py:358
  37.0 0.7 collective-permute-start.5
  37.7 5.0 %collective-permute-start.6 = (bf16[2,4,128,256]{3,2,1,0:T(8,128)(2,1)S(1)}, bf16[2,4,128,256]{3,2,1,0:T(8,128)(2,1)}, u32[]{:S(2)}, u32[]{:S(2)}) collective-permute-start(bf16[2,4,128,256]{3,2,1,0:T(8,128)(2,1)S(1)} %get-tuple-element.51.hid), channel_id=1, source_target_pairs={{0,64},{64,128},{128,192},{192,256},{256,320},{320,384},{384,448},... | collective-permute-start | bytes 1572872 | tf_op jit(solution)/shard_map/ppermute | solution.py:365
  42.8 6.5 %all-to-all-done.got = bf16[16,192,128]{2,1,0:T(8,128)(2,1)S(1)} async-done(((bf16[16,192,128]{2,1,0:T(8,128)(2,1)}), bf16[16,192,128]{2,1,0:T(8,128)(2,1)S(1)}, u32[]{:S(2)}, u32[]{:S(2)}) %all-to-all-start) | async-done | bytes 786464 | tf_op jit(solution)/shard_map/all_to_all | solution.py:358
  49.3 0.9 %shard_map.83 = f32[16,4,384]{2,1,0:T(4,128)} custom-call(bf16[16,192,128]{2,1,0:T(8,128)(2,1)S(1)} %all-to-all-done.got, bf16[2,1,128,256]{3,2,1,0:T(8,128)(2,1)S(1)} %collective-permute-done.4.refs_0_.refs_1_.pair, bf16[2,1,128,256]{3,2,1,0:T(8,128)(2,1)S(1)} %collective-permute-done.5.refs_0_.chip), custom_call_target="tpu_custom_call" | custom-call | flops 1048576 | bytes 1048576 | tf_op jit(solution)/shard_map/pallas_call | solution.py:65
  50.2 11.8 %all-to-all-start.1 = ((f32[16,4,384]{2,1,0:T(4,128)}), f32[16,4,384]{2,1,0:T(4,128)S(1)}, u32[]{:S(2)}, u32[]{:S(2)}) async-start(f32[16,4,384]{2,1,0:T(4,128)} %shard_map.83), calls=%async_computation.1 | async-start | bytes 196608 | tf_op jit(solution)/shard_map/all_to_all | solution.py:382
  62.0 1.0 %copy-done.3 = bf16[3,256,256]{2,1,0:T(8,128)(2,1)S(1)} copy-done((bf16[3,256,256]{2,1,0:T(8,128)(2,1)S(1)}, bf16[3,256,256]{2,1,0:T(8,128)(2,1)}, u32[]{:S(2)}) %copy-start.3) | copy-done | bytes 393240
  63.0 2.4 %shard_map.84 = bf16[2,4,128,256]{3,2,1,0:T(8,128)(2,1)} custom-call(bf16[2,4,128,256]{3,2,1,0:T(8,128)(2,1)S(1)} %get-tuple-element.51.hid, bf16[2,4,128,256]{3,2,1,0:T(8,128)(2,1)} %collective-permute-done.6.past, bf16[3,256,256]{2,1,0:T(8,128)(2,1)S(1)} %copy-done.3), custom_call_target="tpu_custom_call" | custom-call | flops 402653184 | bytes 2097152 | tf_op jit(solution)/shard_map/pallas_call | solution.py:65
  65.4 2.2 %shard_map.85 = bf16[2,4,128,256]{3,2,1,0:T(8,128)(2,1)} custom-call(s32[1]{0:T(128)} %bitcast.core, bf16[2,4,128,256]{3,2,1,0:T(8,128)(2,1)S(1)} %copy-done.1, bf16[2,1,128,256]{3,2,1,0:T(8,128)(2,1)S(1)} %collective-permute-done.4.refs_0_.refs_1_.pair, bf16[2,1,128,256]{3,2,1,0:T(8,128)(2,1)S(1)} %collective-permute-done.5.refs_0_.chip, ...), custom_call_target="tpu_custom_call" | custom-call | flops 1207959552 | bytes 4194304 | tf_op jit(solution)/shard_map/pallas_call | solution.py:65
  67.6 7.3 %all-to-all-done.1.got = f32[16,4,384]{2,1,0:T(4,128)S(1)} async-done(((f32[16,4,384]{2,1,0:T(4,128)}), f32[16,4,384]{2,1,0:T(4,128)S(1)}, u32[]{:S(2)}, u32[]{:S(2)}) %all-to-all-start.1) | async-done | bytes 98336 | tf_op jit(solution)/shard_map/all_to_all | solution.py:382
  74.9 0.7 shard_map.86
  (18 shorter events, 0.2 us)
Async XLA Ops:
  0.6 19.4 %collective-permute-start = (bf16[2,4,128,256]{3,2,1,0:T(8,128)(2,1)}, bf16[2,4,128,256]{3,2,1,0:T(8,128)(2,1)S(1)}, u32[]{:S(2)}, u32[]{:S(2)}) collective-permute-start(bf16[2,4,128,256]{3,2,1,0:T(8,128)(2,1)} %g.1), channel_id=1, source_target_pairs={{64,0},{128,64},{192,128},{256,192},{320,256},{384,320},{448,384},... | collective-permute-start | bytes 1572872 | tf_op jit(solution)/shard_map/ppermute | solution.py:304
  3.3 1.0 %copy-start.2 = (bf16[3,256,256]{2,1,0:T(8,128)(2,1)S(1)}, bf16[3,256,256]{2,1,0:T(8,128)(2,1)}, u32[]{:S(2)}) copy-start(bf16[3,256,256]{2,1,0:T(8,128)(2,1)} %wt.5) | copy-start | bytes 1179652
  3.3 1.2 %copy-start.4 = (bf16[2,4,128,256]{3,2,1,0:T(8,128)(2,1)S(1)}, bf16[2,4,128,256]{3,2,1,0:T(8,128)(2,1)}, u32[]{:S(2)}) copy-start(bf16[2,4,128,256]{3,2,1,0:T(8,128)(2,1)} %x.3) | copy-start | bytes 1572868
  3.3 1.3 %copy-start.5 = (bf16[2,4,128,256]{3,2,1,0:T(8,128)(2,1)S(1)}, bf16[2,4,128,256]{3,2,1,0:T(8,128)(2,1)}, u32[]{:S(2)}) copy-start(bf16[2,4,128,256]{3,2,1,0:T(8,128)(2,1)} %g.1) | copy-start | bytes 1572868
  4.6 3.1 %copy-start = (bf16[9,256,256]{2,1,0:T(8,128)(2,1)S(1)}, bf16[9,256,256]{2,1,0:T(8,128)(2,1)}, u32[]{:S(2)}) copy-start(bf16[9,256,256]{2,1,0:T(8,128)(2,1)} %ws.5) | copy-start | bytes 3538948
  5.1 3.9 %collective-permute-start.1 = (bf16[2,1,128,256]{3,2,1,0:T(8,128)(2,1)S(1)}, bf16[2,1,128,256]{3,2,1,0:T(8,128)(2,1)S(1)}, u32[]{:S(2)}, u32[]{:S(2)}) collective-permute-start(bf16[2,1,128,256]{3,2,1,0:T(8,128)(2,1)S(1)} %get-tuple-element.33), channel_id=1, source_target_pairs={{0,1},{1,0},{2,3},{3,2},{4,5},{5,4},{6,7},{7,6},{8,9},{9,8},{10,11... | collective-permute-start | bytes 393224 | tf_op jit(solution)/shard_map/ppermute | solution.py:291
  7.1 2.0 %collective-permute-start.2 = (bf16[2,1,128,256]{3,2,1,0:T(8,128)(2,1)S(1)}, bf16[2,1,128,256]{3,2,1,0:T(8,128)(2,1)S(1)}, u32[]{:S(2)}, u32[]{:S(2)}) collective-permute-start(bf16[2,1,128,256]{3,2,1,0:T(8,128)(2,1)S(1)} %get-tuple-element.34), channel_id=1, source_target_pairs={{1,2},{3,4},{5,6},{7,8},{9,10},{11,12},{13,14},{15,16},{17,18},{19... | collective-permute-start | bytes 393224 | tf_op jit(solution)/shard_map/ppermute | solution.py:296
  22.4 4.3 %collective-permute-start.3 = (bf16[12,256,128]{2,1,0:T(8,128)(2,1)S(1)}, bf16[12,256,128]{2,1,0:T(8,128)(2,1)S(1)}, u32[]{:S(2)}, u32[]{:S(2)}) collective-permute-start(bf16[12,256,128]{2,1,0:T(8,128)(2,1)S(1)} %get-tuple-element.42), channel_id=1, source_target_pairs={{0,1},{1,0},{2,3},{3,2},{4,5},{5,4},{6,7},{7,6},{8,9},{9,8},{10,11... | collective-permute-start | bytes 2359304 | tf_op jit(solution)/shard_map/ppermute | solution.py:347
  24.3 12.7 %collective-permute-start.4 = (bf16[2,1,128,256]{3,2,1,0:T(8,128)(2,1)}, bf16[2,1,128,256]{3,2,1,0:T(8,128)(2,1)S(1)}, u32[]{:S(2)}, u32[]{:S(2)}) collective-permute-start(bf16[2,1,128,256]{3,2,1,0:T(8,128)(2,1)} %get-tuple-element.47), channel_id=1, source_target_pairs={{0,1},{1,0},{2,3},{3,2},{4,5},{5,4},{6,7},{7,6},{8,9},{9,8},{10,11... | collective-permute-start | bytes 393224 | tf_op jit(solution)/shard_map/ppermute | solution.py:291
  27.8 21.4 %all-to-all-start = ((bf16[16,192,128]{2,1,0:T(8,128)(2,1)}), bf16[16,192,128]{2,1,0:T(8,128)(2,1)S(1)}, u32[]{:S(2)}, u32[]{:S(2)}) async-start(bf16[16,192,128]{2,1,0:T(8,128)(2,1)} %get-tuple-element.44), calls=%async_computation | async-start | bytes 1572864 | tf_op jit(solution)/shard_map/all_to_all | solution.py:358
  37.0 0.7 collective-permute-start.5
  37.7 27.7 %copy-start.1 = (bf16[2,4,128,256]{3,2,1,0:T(8,128)(2,1)S(1)}, bf16[2,4,128,256]{3,2,1,0:T(8,128)(2,1)}, u32[]{:S(2)}) copy-start(bf16[2,4,128,256]{3,2,1,0:T(8,128)(2,1)} %get-tuple-element.43.gpre) | copy-start | bytes 1572868
  37.7 24.3 %collective-permute-start.6 = (bf16[2,4,128,256]{3,2,1,0:T(8,128)(2,1)S(1)}, bf16[2,4,128,256]{3,2,1,0:T(8,128)(2,1)}, u32[]{:S(2)}, u32[]{:S(2)}) collective-permute-start(bf16[2,4,128,256]{3,2,1,0:T(8,128)(2,1)S(1)} %get-tuple-element.51.hid), channel_id=1, source_target_pairs={{0,64},{64,128},{128,192},{192,256},{256,320},{320,384},{384,448},... | collective-permute-start | bytes 1572872 | tf_op jit(solution)/shard_map/ppermute | solution.py:365
  50.2 24.7 %all-to-all-start.1 = ((f32[16,4,384]{2,1,0:T(4,128)}), f32[16,4,384]{2,1,0:T(4,128)S(1)}, u32[]{:S(2)}, u32[]{:S(2)}) async-start(f32[16,4,384]{2,1,0:T(4,128)} %shard_map.83), calls=%async_computation.1 | async-start | bytes 196608 | tf_op jit(solution)/shard_map/all_to_all | solution.py:382
  62.0 1.0 %copy-start.3 = (bf16[3,256,256]{2,1,0:T(8,128)(2,1)S(1)}, bf16[3,256,256]{2,1,0:T(8,128)(2,1)}, u32[]{:S(2)}) copy-start(bf16[3,256,256]{2,1,0:T(8,128)(2,1)} %wt.5) | copy-start | bytes 1179652

commit v8 on v7

--- a/solution.py
+++ b/solution.py
@@ -207,7 +207,7 @@
 def pair_kernel(core, keep, got, gpre, out_hbm, chip_ref, out_ref, sems):
     half = C // 4
     rows = gpre.at[:, pl.ds(3 * core[0], 1)]
-    copies = [pltpu.make_async_copy(rows, chip_ref, sems.at[3])]
+    copies = [pltpu.make_async_copy(rows, chip_ref, sems.at[6])]
     copies[0].start()
     for p in range(TAPS // 2):
         s0 = keep[2 * p] + got[2 * p].astype(F32)
@@ -217,26 +217,20 @@
         for a in range(8):
             out_ref[a, 32 * p : 32 * p + 32] = low[32 * a : 32 * a + 32]
             out_ref[8 + a, 32 * p : 32 * p + 32] = high[32 * a : 32 * a + 32]
-        if p % 2 == 1:
-            part = pl.ds(32 * (p - 1), 64)
-            copy = pltpu.make_async_copy(
-                out_ref.at[:, part], out_hbm.at[:, part], sems.at[p // 2]
-            )
-            copy.start()
-            copies.append(copy)
+        part = pl.ds(32 * p, 32)
+        copy = pltpu.make_async_copy(out_ref.at[:, part], out_hbm.at[:, part], sems.at[p])
+        copy.start()
+        copies.append(copy)
     for copy in copies:
         copy.wait()
 
 
 def plane_kernel(got, pair, chip, out_ref):
-    total = got[0].astype(F32)
-    for n in range(1, 16):
-        total = total + got[n].astype(F32)
-    pieces = []
-    for p in range(TAPS // 2):
-        flipped = total[32 * p : 32 * p + 32].T
-        pieces += [flipped[:64], flipped[64:]]
-    wide = jnp.concatenate(pieces, 1)
+    parts = [got[n].astype(F32) for n in range(16)]
+    while len(parts) > 1:
+        parts = [parts[n] + parts[n + 1] for n in range(0, len(parts), 2)]
+    four, two = parts[0][:128].T, parts[0][128:].T
+    wide = jnp.concatenate([four[:64], two[:64], four[64:], two[64:]], 1)
     for z in range(16):
         out_ref[z] = wide[4 * z : 4 * z + 4]
 
@@ -245,10 +239,12 @@
     total = got[0]
     for n in range(1, 16):
         total = total + got[n]
-    for t in range(9):
-        gs_ref[t] = total[:, 32 * t : 32 * t + 32]
-    for t in range(3):
-        gt_ref[t] = total[:, 32 * (9 + t) : 32 * (9 + t) + 32]
+    for t in range(TAPS):
+        at = 32 * (6 * (t % 2) + t // 2)
+        if t < 9:
+            gs_ref[t] = total[:, at : at + 32]
+        else:
+            gt_ref[t - 9] = total[:, at : at + 32]
 
 
 def token_kernel(*refs):
@@ -353,7 +349,7 @@
         core, keep, got, pltpu.with_memory_space_constraint(grad_pre, pltpu.HBM),
         hbm_in=(3,),
         hbm_out=(0,),
-        scratch=[pltpu.VMEM((16, 192, 128), BF16), pltpu.SemaphoreType.DMA((4,))],
+        scratch=[pltpu.VMEM((16, 192, 128), BF16), pltpu.SemaphoreType.DMA((7,))],
     )
     chunks = lax.all_to_all(chunks, ("xl", "tm"), split_axis=0, concat_axis=0, tiled=True)
     pair = to_pair(pair)

time: 77 us -> 76.9 us (level)
  no operation moved by 1% of the time
where the time goes in v8:
time: 76.9 us; the launch traced here: 75.6 us
  starting transfers between devices  36.2 us (47%)
  waiting for transfers between devices  23.9 us (31%)
  Pallas kernels  12.4 us (16%)
  local copies, waits for them, and re-layouts  2.26 us (3%)
  between operations  0.85 us (1%)
    pallas_call x12, Pallas kernels, call(): pl.pallas_call(kernel, out_shape=out_shape, in_specs=in_specs, out_specs=...  12.4 us
    all_to_all x1, starting transfers between devices, body(): rows = lax.all_to_all(rows, 'z', split_axis=0, concat_axis=0, tiled=True)  11.8 us
    ppermute x1, waiting for transfers between devices, body(): later = lax.ppermute(grad_out, 'tm', backward)  10 us
    all_to_all x1, starting transfers between devices, body(): lax.all_to_all(chunks, ('xl', 'tm'), split_axis=0, concat_axis=0, tiled=T...  9.16 us
    all_to_all x1, waiting for transfers between devices, body(): rows = lax.all_to_all(rows, 'z', split_axis=0, concat_axis=0, tiled=True)  7.29 us
    all_to_all x1, waiting for transfers between devices, body(): lax.all_to_all(chunks, ('xl', 'tm'), split_axis=0, concat_axis=0, tiled=T...  6.5 us
    ppermute x1, starting transfers between devices, body(): past = lax.ppermute(hidden, 'tm', forward)  5.01 us
    ppermute x2, starting transfers between devices, to_pair(): return lax.ppermute(rows, 'c', [(0, 1), (1, 0)])  4.33 us
  transfers between devices with their start and end apart: 9, of which 3 were waited for; matrix products, arithmetic and copies ran while one was open for 0% of the time, Pallas kernels for 12%

profile of v8, /device:TPU:24, one launch (start us, length us, event | category | flops | bytes accessed | tf_op | source)
XLA Modules:
  0.0 75.6 jit_solution(4656646550175452922)
XLA Ops:
  0.6 2.7 %collective-permute-start = (bf16[2,4,128,256]{3,2,1,0:T(8,128)(2,1)}, bf16[2,4,128,256]{3,2,1,0:T(8,128)(2,1)S(1)}, u32[]{:S(2)}, u32[]{:S(2)}) collective-permute-start(bf16[2,4,128,256]{3,2,1,0:T(8,128)(2,1)} %g.1), channel_id=1, source_target_pairs={{64,0},{128,64},{192,128},{256,192},{320,256},{384,320},{448,384},... | collective-permute-start | bytes 1572872 | tf_op jit(solution)/shard_map/ppermute | solution.py:300
  3.4 0.9 %copy-done.2 = bf16[3,256,256]{2,1,0:T(8,128)(2,1)S(1)} copy-done((bf16[3,256,256]{2,1,0:T(8,128)(2,1)S(1)}, bf16[3,256,256]{2,1,0:T(8,128)(2,1)}, u32[]{:S(2)}) %copy-start.2) | copy-done | bytes 393240
  4.3 0.2 copy-done.4
  4.6 0.5 shard_map.76
  5.1 1.9 %collective-permute-start.1 = (bf16[2,1,128,256]{3,2,1,0:T(8,128)(2,1)S(1)}, bf16[2,1,128,256]{3,2,1,0:T(8,128)(2,1)S(1)}, u32[]{:S(2)}, u32[]{:S(2)}) collective-permute-start(bf16[2,1,128,256]{3,2,1,0:T(8,128)(2,1)S(1)} %get-tuple-element.33), channel_id=1, source_target_pairs={{0,1},{1,0},{2,3},{3,2},{4,5},{5,4},{6,7},{7,6},{8,9},{9,8},{10,11... | collective-permute-start | bytes 393224 | tf_op jit(solution)/shard_map/ppermute | solution.py:287
  7.1 0.7 collective-permute-start.2
  7.8 1.3 %shard_map.77 = (f32[2,512,256]{2,1,0:T(8,128)S(1)}, bf16[3,2,256,512]{3,2,1,0:T(8,128)(2,1)S(1)}) custom-call(bf16[2,4,128,256]{3,2,1,0:T(8,128)(2,1)S(1)} %copy-done.4, bf16[9,256,256]{2,1,0:T(8,128)(2,1)S(1)} %copy-done), custom_call_target="tpu_custom_call" | custom-call | flops 1207959552 | bytes 4194304 | tf_op jit(solution)/shard_map/pallas_call | solution.py:65
  9.0 0.9 %shard_map.78 = (bf16[2,4,128,256]{3,2,1,0:T(8,128)(2,1)S(1)}, f32[2,512,256]{2,1,0:T(8,128)S(1)}, bf16[2,256,512]{2,1,0:T(8,128)(2,1)S(1)}, bf16[3,2,2,256,128]{4,3,2,1,0:T(8,128)(2,1)S(1)}, f32[2,256,256]{2,1,0:T(8,128)S(1)}) custom-call(s32[1]{0:T(128)} %bitcast.core, f32[2,512,256]{2,1,0:T(8,128)S(1)} %get-tuple-element.32.pre, ...), custom_call_target="tpu_custom_call" | custom-call | flops 671088640 | bytes 8388608 | tf_op jit(solution)/shard_map/pallas_call | solution.py:65
  10.0 10.0 %collective-permute-done.n = bf16[2,4,128,256]{3,2,1,0:T(8,128)(2,1)S(1)} collective-permute-done((bf16[2,4,128,256]{3,2,1,0:T(8,128)(2,1)}, bf16[2,4,128,256]{3,2,1,0:T(8,128)(2,1)S(1)}, u32[]{:S(2)}, u32[]{:S(2)}) %collective-permute-start) | collective-permute-done | bytes 524320 | tf_op jit(solution)/shard_map/ppermute | solution.py:300
  20.0 2.4 %shard_map.79 = (bf16[2,4,128,256]{3,2,1,0:T(8,128)(2,1)}, bf16[2,1,128,256]{3,2,1,0:T(8,128)(2,1)}, f32[12,256,128]{2,1,0:T(8,128)S(1)}, bf16[12,256,128]{2,1,0:T(8,128)(2,1)S(1)}) custom-call(s32[1]{0:T(128)} %bitcast.core, bf16[2,4,128,256]{3,2,1,0:T(8,128)(2,1)S(1)} %collective-permute-done.n, f32[2,512,256]{2,1,0:T(8,128)S(1)} %get-tuple-element.31.gh, ...), custom_call_target="tpu_custom_call" | custom-call | flops 2013265920 | bytes 10485760 | tf_op jit(solution)/shard_map/pallas_call | solution.py:65
  22.4 1.9 %collective-permute-start.3 = (bf16[12,256,128]{2,1,0:T(8,128)(2,1)S(1)}, bf16[12,256,128]{2,1,0:T(8,128)(2,1)S(1)}, u32[]{:S(2)}, u32[]{:S(2)}) collective-permute-start(bf16[12,256,128]{2,1,0:T(8,128)(2,1)S(1)} %get-tuple-element.42), channel_id=1, source_target_pairs={{0,1},{1,0},{2,3},{3,2},{4,5},{5,4},{6,7},{7,6},{8,9},{9,8},{10,11... | collective-permute-start | bytes 2359304 | tf_op jit(solution)/shard_map/ppermute | solution.py:343
  24.3 2.4 %collective-permute-start.4 = (bf16[2,1,128,256]{3,2,1,0:T(8,128)(2,1)}, bf16[2,1,128,256]{3,2,1,0:T(8,128)(2,1)S(1)}, u32[]{:S(2)}, u32[]{:S(2)}) collective-permute-start(bf16[2,1,128,256]{3,2,1,0:T(8,128)(2,1)} %get-tuple-element.47), channel_id=1, source_target_pairs={{0,1},{1,0},{2,3},{3,2},{4,5},{5,4},{6,7},{7,6},{8,9},{9,8},{10,11... | collective-permute-start | bytes 393224 | tf_op jit(solution)/shard_map/ppermute | solution.py:287
  26.8 1.1 %shard_map.80 = (bf16[16,192,128]{2,1,0:T(8,128)(2,1)}, bf16[2,1,128,256]{3,2,1,0:T(8,128)(2,1)S(1)}) custom-call(s32[1]{0:T(128)} %bitcast.core, f32[12,256,128]{2,1,0:T(8,128)S(1)} %get-tuple-element.41.keep, bf16[12,256,128]{2,1,0:T(8,128)(2,1)S(1)} %collective-permute-done.3.got, bf16[2,4,128,256]{3,2,1,0:T(8,128)(2,1)} %get-tuple-element.43.gpre), custom_call_target="tpu_custom_call" | custom-call | flops 1048576 | bytes 4194304 | tf_op jit(solution)/shard_map/pallas_call | solution.py:65
  27.8 9.2 %all-to-all-start = ((bf16[16,192,128]{2,1,0:T(8,128)(2,1)}), bf16[16,192,128]{2,1,0:T(8,128)(2,1)S(1)}, u32[]{:S(2)}, u32[]{:S(2)}) async-start(bf16[16,192,128]{2,1,0:T(8,128)(2,1)} %get-tuple-element.44), calls=%async_computation | async-start | bytes 1572864 | tf_op jit(solution)/shard_map/all_to_all | solution.py:354
  37.0 0.7 collective-permute-start.5
  37.7 5.0 %collective-permute-start.6 = (bf16[2,4,128,256]{3,2,1,0:T(8,128)(2,1)S(1)}, bf16[2,4,128,256]{3,2,1,0:T(8,128)(2,1)}, u32[]{:S(2)}, u32[]{:S(2)}) collective-permute-start(bf16[2,4,128,256]{3,2,1,0:T(8,128)(2,1)S(1)} %get-tuple-element.51.hid), channel_id=1, source_target_pairs={{0,64},{64,128},{128,192},{192,256},{256,320},{320,384},{384,448},... | collective-permute-start | bytes 1572872 | tf_op jit(solution)/shard_map/ppermute | solution.py:361
  42.7 6.5 %all-to-all-done.got = bf16[16,192,128]{2,1,0:T(8,128)(2,1)S(1)} async-done(((bf16[16,192,128]{2,1,0:T(8,128)(2,1)}), bf16[16,192,128]{2,1,0:T(8,128)(2,1)S(1)}, u32[]{:S(2)}, u32[]{:S(2)}) %all-to-all-start) | async-done | bytes 786464 | tf_op jit(solution)/shard_map/all_to_all | solution.py:354
  49.3 0.9 %shard_map.83 = f32[16,4,384]{2,1,0:T(4,128)} custom-call(bf16[16,192,128]{2,1,0:T(8,128)(2,1)S(1)} %all-to-all-done.got, bf16[2,1,128,256]{3,2,1,0:T(8,128)(2,1)S(1)} %collective-permute-done.4.refs_0_.refs_1_.pair, bf16[2,1,128,256]{3,2,1,0:T(8,128)(2,1)S(1)} %collective-permute-done.5.refs_0_.chip), custom_call_target="tpu_custom_call" | custom-call | flops 1048576 | bytes 1048576 | tf_op jit(solution)/shard_map/pallas_call | solution.py:65
  50.1 11.8 %all-to-all-start.1 = ((f32[16,4,384]{2,1,0:T(4,128)}), f32[16,4,384]{2,1,0:T(4,128)S(1)}, u32[]{:S(2)}, u32[]{:S(2)}) async-start(f32[16,4,384]{2,1,0:T(4,128)} %shard_map.83), calls=%async_computation.1 | async-start | bytes 196608 | tf_op jit(solution)/shard_map/all_to_all | solution.py:378
  62.0 1.0 %copy-done.3 = bf16[3,256,256]{2,1,0:T(8,128)(2,1)S(1)} copy-done((bf16[3,256,256]{2,1,0:T(8,128)(2,1)S(1)}, bf16[3,256,256]{2,1,0:T(8,128)(2,1)}, u32[]{:S(2)}) %copy-start.3) | copy-done | bytes 393240
  62.9 2.4 %shard_map.84 = bf16[2,4,128,256]{3,2,1,0:T(8,128)(2,1)} custom-call(bf16[2,4,128,256]{3,2,1,0:T(8,128)(2,1)S(1)} %get-tuple-element.51.hid, bf16[2,4,128,256]{3,2,1,0:T(8,128)(2,1)} %collective-permute-done.6.past, bf16[3,256,256]{2,1,0:T(8,128)(2,1)S(1)} %copy-done.3), custom_call_target="tpu_custom_call" | custom-call | flops 402653184 | bytes 2097152 | tf_op jit(solution)/shard_map/pallas_call | solution.py:65
  65.4 2.2 %shard_map.85 = bf16[2,4,128,256]{3,2,1,0:T(8,128)(2,1)} custom-call(s32[1]{0:T(128)} %bitcast.core, bf16[2,4,128,256]{3,2,1,0:T(8,128)(2,1)S(1)} %copy-done.1, bf16[2,1,128,256]{3,2,1,0:T(8,128)(2,1)S(1)} %collective-permute-done.4.refs_0_.refs_1_.pair, bf16[2,1,128,256]{3,2,1,0:T(8,128)(2,1)S(1)} %collective-permute-done.5.refs_0_.chip, ...), custom_call_target="tpu_custom_call" | custom-call | flops 1207959552 | bytes 4194304 | tf_op jit(solution)/shard_map/pallas_call | solution.py:65
  67.6 7.3 %all-to-all-done.1.got = f32[16,4,384]{2,1,0:T(4,128)S(1)} async-done(((f32[16,4,384]{2,1,0:T(4,128)}), f32[16,4,384]{2,1,0:T(4,128)S(1)}, u32[]{:S(2)}, u32[]{:S(2)}) %all-to-all-start.1) | async-done | bytes 98336 | tf_op jit(solution)/shard_map/all_to_all | solution.py:378
  74.9 0.7 shard_map.86
  (18 shorter events, 0.2 us)
Async XLA Ops:
  0.6 19.4 %collective-permute-start = (bf16[2,4,128,256]{3,2,1,0:T(8,128)(2,1)}, bf16[2,4,128,256]{3,2,1,0:T(8,128)(2,1)S(1)}, u32[]{:S(2)}, u32[]{:S(2)}) collective-permute-start(bf16[2,4,128,256]{3,2,1,0:T(8,128)(2,1)} %g.1), channel_id=1, source_target_pairs={{64,0},{128,64},{192,128},{256,192},{320,256},{384,320},{448,384},... | collective-permute-start | bytes 1572872 | tf_op jit(solution)/shard_map/ppermute | solution.py:300
  3.3 1.0 %copy-start.2 = (bf16[3,256,256]{2,1,0:T(8,128)(2,1)S(1)}, bf16[3,256,256]{2,1,0:T(8,128)(2,1)}, u32[]{:S(2)}) copy-start(bf16[3,256,256]{2,1,0:T(8,128)(2,1)} %wt.5) | copy-start | bytes 1179652
  3.3 1.2 %copy-start.4 = (bf16[2,4,128,256]{3,2,1,0:T(8,128)(2,1)S(1)}, bf16[2,4,128,256]{3,2,1,0:T(8,128)(2,1)}, u32[]{:S(2)}) copy-start(bf16[2,4,128,256]{3,2,1,0:T(8,128)(2,1)} %x.3) | copy-start | bytes 1572868
  3.3 1.3 %copy-start.5 = (bf16[2,4,128,256]{3,2,1,0:T(8,128)(2,1)S(1)}, bf16[2,4,128,256]{3,2,1,0:T(8,128)(2,1)}, u32[]{:S(2)}) copy-start(bf16[2,4,128,256]{3,2,1,0:T(8,128)(2,1)} %g.1) | copy-start | bytes 1572868
  4.6 3.1 %copy-start = (bf16[9,256,256]{2,1,0:T(8,128)(2,1)S(1)}, bf16[9,256,256]{2,1,0:T(8,128)(2,1)}, u32[]{:S(2)}) copy-start(bf16[9,256,256]{2,1,0:T(8,128)(2,1)} %ws.5) | copy-start | bytes 3538948
  5.1 3.9 %collective-permute-start.1 = (bf16[2,1,128,256]{3,2,1,0:T(8,128)(2,1)S(1)}, bf16[2,1,128,256]{3,2,1,0:T(8,128)(2,1)S(1)}, u32[]{:S(2)}, u32[]{:S(2)}) collective-permute-start(bf16[2,1,128,256]{3,2,1,0:T(8,128)(2,1)S(1)} %get-tuple-element.33), channel_id=1, source_target_pairs={{0,1},{1,0},{2,3},{3,2},{4,5},{5,4},{6,7},{7,6},{8,9},{9,8},{10,11... | collective-permute-start | bytes 393224 | tf_op jit(solution)/shard_map/ppermute | solution.py:287
  7.1 2.0 %collective-permute-start.2 = (bf16[2,1,128,256]{3,2,1,0:T(8,128)(2,1)S(1)}, bf16[2,1,128,256]{3,2,1,0:T(8,128)(2,1)S(1)}, u32[]{:S(2)}, u32[]{:S(2)}) collective-permute-start(bf16[2,1,128,256]{3,2,1,0:T(8,128)(2,1)S(1)} %get-tuple-element.34), channel_id=1, source_target_pairs={{1,2},{3,4},{5,6},{7,8},{9,10},{11,12},{13,14},{15,16},{17,18},{19... | collective-permute-start | bytes 393224 | tf_op jit(solution)/shard_map/ppermute | solution.py:292
  22.4 4.3 %collective-permute-start.3 = (bf16[12,256,128]{2,1,0:T(8,128)(2,1)S(1)}, bf16[12,256,128]{2,1,0:T(8,128)(2,1)S(1)}, u32[]{:S(2)}, u32[]{:S(2)}) collective-permute-start(bf16[12,256,128]{2,1,0:T(8,128)(2,1)S(1)} %get-tuple-element.42), channel_id=1, source_target_pairs={{0,1},{1,0},{2,3},{3,2},{4,5},{5,4},{6,7},{7,6},{8,9},{9,8},{10,11... | collective-permute-start | bytes 2359304 | tf_op jit(solution)/shard_map/ppermute | solution.py:343
  24.3 12.7 %collective-permute-start.4 = (bf16[2,1,128,256]{3,2,1,0:T(8,128)(2,1)}, bf16[2,1,128,256]{3,2,1,0:T(8,128)(2,1)S(1)}, u32[]{:S(2)}, u32[]{:S(2)}) collective-permute-start(bf16[2,1,128,256]{3,2,1,0:T(8,128)(2,1)} %get-tuple-element.47), channel_id=1, source_target_pairs={{0,1},{1,0},{2,3},{3,2},{4,5},{5,4},{6,7},{7,6},{8,9},{9,8},{10,11... | collective-permute-start | bytes 393224 | tf_op jit(solution)/shard_map/ppermute | solution.py:287
  27.8 21.4 %all-to-all-start = ((bf16[16,192,128]{2,1,0:T(8,128)(2,1)}), bf16[16,192,128]{2,1,0:T(8,128)(2,1)S(1)}, u32[]{:S(2)}, u32[]{:S(2)}) async-start(bf16[16,192,128]{2,1,0:T(8,128)(2,1)} %get-tuple-element.44), calls=%async_computation | async-start | bytes 1572864 | tf_op jit(solution)/shard_map/all_to_all | solution.py:354
  37.0 0.7 collective-permute-start.5
  37.7 27.6 %copy-start.1 = (bf16[2,4,128,256]{3,2,1,0:T(8,128)(2,1)S(1)}, bf16[2,4,128,256]{3,2,1,0:T(8,128)(2,1)}, u32[]{:S(2)}) copy-start(bf16[2,4,128,256]{3,2,1,0:T(8,128)(2,1)} %get-tuple-element.43.gpre) | copy-start | bytes 1572868
  37.7 24.2 %collective-permute-start.6 = (bf16[2,4,128,256]{3,2,1,0:T(8,128)(2,1)S(1)}, bf16[2,4,128,256]{3,2,1,0:T(8,128)(2,1)}, u32[]{:S(2)}, u32[]{:S(2)}) collective-permute-start(bf16[2,4,128,256]{3,2,1,0:T(8,128)(2,1)S(1)} %get-tuple-element.51.hid), channel_id=1, source_target_pairs={{0,64},{64,128},{128,192},{192,256},{256,320},{320,384},{384,448},... | collective-permute-start | bytes 1572872 | tf_op jit(solution)/shard_map/ppermute | solution.py:361
  50.1 24.7 %all-to-all-start.1 = ((f32[16,4,384]{2,1,0:T(4,128)}), f32[16,4,384]{2,1,0:T(4,128)S(1)}, u32[]{:S(2)}, u32[]{:S(2)}) async-start(f32[16,4,384]{2,1,0:T(4,128)} %shard_map.83), calls=%async_computation.1 | async-start | bytes 196608 | tf_op jit(solution)/shard_map/all_to_all | solution.py:378
  61.9 1.0 %copy-start.3 = (bf16[3,256,256]{2,1,0:T(8,128)(2,1)S(1)}, bf16[3,256,256]{2,1,0:T(8,128)(2,1)}, u32[]{:S(2)}) copy-start(bf16[3,256,256]{2,1,0:T(8,128)(2,1)} %wt.5) | copy-start | bytes 1179652

commit v9 on v8

--- a/solution.py
+++ b/solution.py
@@ -169,6 +169,11 @@
         send_ref[tap] = value[:, C // 2 :].astype(BF16)
 
     a0, a1 = n[0].reshape(PIX, C), n[1].reshape(PIX, C)
+    p0 = mm(a0, pm[...]).astype(BF16)
+    p1 = mm(a1, pm[...]).astype(BF16)
+    store(9, mm(ht[0], p0) + mm(ht[1], p1))
+    store(10, gt[0] + mm(ht[1], p0))
+    store(11, gt[1])
     back0 = gh[0] + mm_t(a0, wt[0])
     back1 = gh[1] + mm_t(a0, wt[1]) + mm_t(a1, wt[0])
     grads = []
@@ -183,11 +188,6 @@
     ]
     for copy in copies:
         copy.start()
-    p0 = mm(a0, pm[...]).astype(BF16)
-    p1 = mm(a1, pm[...]).astype(BF16)
-    store(9, mm(ht[0], p0) + mm(ht[1], p1))
-    store(10, gt[0] + mm(ht[1], p0))
-    store(11, gt[1])
     for j in range(3):
         for i in range(3):
             total = None

time: 76.9 us -> 77.7 us (1.010)
  Pallas kernels: 12.4 us -> 13.2 us
    pallas_call x12, Pallas kernels: 12.4 us -> 13.2 us  [call(): pl.pallas_call(kernel, out_shape=out_shape, in_specs=in_specs, out_specs=...]
where the time goes in v9:
time: 77.7 us; the launch traced here: 76.4 us
  starting transfers between devices  36.2 us (47%)
  waiting for transfers between devices  23.9 us (31%)
  Pallas kernels  13.2 us (17%)
  local copies, waits for them, and re-layouts  2.26 us (3%)
  between operations  0.85 us (1%)
    pallas_call x12, Pallas kernels, call(): pl.pallas_call(kernel, out_shape=out_shape, in_specs=in_specs, out_specs=...  13.2 us
    all_to_all x1, starting transfers between devices, body(): rows = lax.all_to_all(rows, 'z', split_axis=0, concat_axis=0, tiled=True)  11.8 us
    ppermute x1, waiting for transfers between devices, body(): later = lax.ppermute(grad_out, 'tm', backward)  10 us
    all_to_all x1, starting transfers between devices, body(): lax.all_to_all(chunks, ('xl', 'tm'), split_axis=0, concat_axis=0, tiled=T...  9.16 us
    all_to_all x1, waiting for transfers between devices, body(): rows = lax.all_to_all(rows, 'z', split_axis=0, concat_axis=0, tiled=True)  7.29 us
    all_to_all x1, waiting for transfers between devices, body(): lax.all_to_all(chunks, ('xl', 'tm'), split_axis=0, concat_axis=0, tiled=T...  6.5 us
    ppermute x1, starting transfers between devices, body(): past = lax.ppermute(hidden, 'tm', forward)  5.01 us
    ppermute x2, starting transfers between devices, to_pair(): return lax.ppermute(rows, 'c', [(0, 1), (1, 0)])  4.33 us
  transfers between devices with their start and end apart: 9, of which 3 were waited for; matrix products, arithmetic and copies ran while one was open for 0% of the time, Pallas kernels for 12%

profile of v9, /device:TPU:24, one launch (start us, length us, event | category | flops | bytes accessed | tf_op | source)
XLA Modules:
  0.0 76.4 jit_solution(2719289574750196478)
XLA Ops:
  0.6 2.7 %collective-permute-start = (bf16[2,4,128,256]{3,2,1,0:T(8,128)(2,1)}, bf16[2,4,128,256]{3,2,1,0:T(8,128)(2,1)S(1)}, u32[]{:S(2)}, u32[]{:S(2)}) collective-permute-start(bf16[2,4,128,256]{3,2,1,0:T(8,128)(2,1)} %g.1), channel_id=1, source_target_pairs={{64,0},{128,64},{192,128},{256,192},{320,256},{384,320},{448,384},... | collective-permute-start | bytes 1572872 | tf_op jit(solution)/shard_map/ppermute | solution.py:300
  3.4 0.9 %copy-done.2 = bf16[3,256,256]{2,1,0:T(8,128)(2,1)S(1)} copy-done((bf16[3,256,256]{2,1,0:T(8,128)(2,1)S(1)}, bf16[3,256,256]{2,1,0:T(8,128)(2,1)}, u32[]{:S(2)}) %copy-start.2) | copy-done | bytes 393240
  4.3 0.2 copy-done.4
  4.6 0.5 shard_map.76
  5.1 1.9 %collective-permute-start.1 = (bf16[2,1,128,256]{3,2,1,0:T(8,128)(2,1)S(1)}, bf16[2,1,128,256]{3,2,1,0:T(8,128)(2,1)S(1)}, u32[]{:S(2)}, u32[]{:S(2)}) collective-permute-start(bf16[2,1,128,256]{3,2,1,0:T(8,128)(2,1)S(1)} %get-tuple-element.33), channel_id=1, source_target_pairs={{0,1},{1,0},{2,3},{3,2},{4,5},{5,4},{6,7},{7,6},{8,9},{9,8},{10,11... | collective-permute-start | bytes 393224 | tf_op jit(solution)/shard_map/ppermute | solution.py:287
  7.1 0.7 collective-permute-start.2
  7.8 1.3 %shard_map.77 = (f32[2,512,256]{2,1,0:T(8,128)S(1)}, bf16[3,2,256,512]{3,2,1,0:T(8,128)(2,1)S(1)}) custom-call(bf16[2,4,128,256]{3,2,1,0:T(8,128)(2,1)S(1)} %copy-done.4, bf16[9,256,256]{2,1,0:T(8,128)(2,1)S(1)} %copy-done), custom_call_target="tpu_custom_call" | custom-call | flops 1207959552 | bytes 4194304 | tf_op jit(solution)/shard_map/pallas_call | solution.py:65
  9.0 0.9 %shard_map.78 = (bf16[2,4,128,256]{3,2,1,0:T(8,128)(2,1)S(1)}, f32[2,512,256]{2,1,0:T(8,128)S(1)}, bf16[2,256,512]{2,1,0:T(8,128)(2,1)S(1)}, bf16[3,2,2,256,128]{4,3,2,1,0:T(8,128)(2,1)S(1)}, f32[2,256,256]{2,1,0:T(8,128)S(1)}) custom-call(s32[1]{0:T(128)} %bitcast.core, f32[2,512,256]{2,1,0:T(8,128)S(1)} %get-tuple-element.32.pre, ...), custom_call_target="tpu_custom_call" | custom-call | flops 671088640 | bytes 8388608 | tf_op jit(solution)/shard_map/pallas_call | solution.py:65
  10.0 10.0 %collective-permute-done.n = bf16[2,4,128,256]{3,2,1,0:T(8,128)(2,1)S(1)} collective-permute-done((bf16[2,4,128,256]{3,2,1,0:T(8,128)(2,1)}, bf16[2,4,128,256]{3,2,1,0:T(8,128)(2,1)S(1)}, u32[]{:S(2)}, u32[]{:S(2)}) %collective-permute-start) | collective-permute-done | bytes 524320 | tf_op jit(solution)/shard_map/ppermute | solution.py:300
  20.0 3.2 %shard_map.79 = (bf16[2,4,128,256]{3,2,1,0:T(8,128)(2,1)}, bf16[2,1,128,256]{3,2,1,0:T(8,128)(2,1)}, f32[12,256,128]{2,1,0:T(8,128)S(1)}, bf16[12,256,128]{2,1,0:T(8,128)(2,1)S(1)}) custom-call(s32[1]{0:T(128)} %bitcast.core, bf16[2,4,128,256]{3,2,1,0:T(8,128)(2,1)S(1)} %collective-permute-done.n, f32[2,512,256]{2,1,0:T(8,128)S(1)} %get-tuple-element.31.gh, ...), custom_call_target="tpu_custom_call" | custom-call | flops 2013265920 | bytes 10485760 | tf_op jit(solution)/shard_map/pallas_call | solution.py:65
  23.2 1.9 %collective-permute-start.3 = (bf16[12,256,128]{2,1,0:T(8,128)(2,1)S(1)}, bf16[12,256,128]{2,1,0:T(8,128)(2,1)S(1)}, u32[]{:S(2)}, u32[]{:S(2)}) collective-permute-start(bf16[12,256,128]{2,1,0:T(8,128)(2,1)S(1)} %get-tuple-element.42), channel_id=1, source_target_pairs={{0,1},{1,0},{2,3},{3,2},{4,5},{5,4},{6,7},{7,6},{8,9},{9,8},{10,11... | collective-permute-start | bytes 2359304 | tf_op jit(solution)/shard_map/ppermute | solution.py:343
  25.1 2.4 %collective-permute-start.4 = (bf16[2,1,128,256]{3,2,1,0:T(8,128)(2,1)}, bf16[2,1,128,256]{3,2,1,0:T(8,128)(2,1)S(1)}, u32[]{:S(2)}, u32[]{:S(2)}) collective-permute-start(bf16[2,1,128,256]{3,2,1,0:T(8,128)(2,1)} %get-tuple-element.47), channel_id=1, source_target_pairs={{0,1},{1,0},{2,3},{3,2},{4,5},{5,4},{6,7},{7,6},{8,9},{9,8},{10,11... | collective-permute-start | bytes 393224 | tf_op jit(solution)/shard_map/ppermute | solution.py:287
  27.6 1.1 %shard_map.80 = (bf16[16,192,128]{2,1,0:T(8,128)(2,1)}, bf16[2,1,128,256]{3,2,1,0:T(8,128)(2,1)S(1)}) custom-call(s32[1]{0:T(128)} %bitcast.core, f32[12,256,128]{2,1,0:T(8,128)S(1)} %get-tuple-element.41.keep, bf16[12,256,128]{2,1,0:T(8,128)(2,1)S(1)} %collective-permute-done.3.got, bf16[2,4,128,256]{3,2,1,0:T(8,128)(2,1)} %get-tuple-element.43.gpre), custom_call_target="tpu_custom_call" | custom-call | flops 1048576 | bytes 4194304 | tf_op jit(solution)/shard_map/pallas_call | solution.py:65
  28.7 9.2 %all-to-all-start = ((bf16[16,192,128]{2,1,0:T(8,128)(2,1)}), bf16[16,192,128]{2,1,0:T(8,128)(2,1)S(1)}, u32[]{:S(2)}, u32[]{:S(2)}) async-start(bf16[16,192,128]{2,1,0:T(8,128)(2,1)} %get-tuple-element.44), calls=%async_computation | async-start | bytes 1572864 | tf_op jit(solution)/shard_map/all_to_all | solution.py:354
  37.8 0.7 collective-permute-start.5
  38.5 5.0 %collective-permute-start.6 = (bf16[2,4,128,256]{3,2,1,0:T(8,128)(2,1)S(1)}, bf16[2,4,128,256]{3,2,1,0:T(8,128)(2,1)}, u32[]{:S(2)}, u32[]{:S(2)}) collective-permute-start(bf16[2,4,128,256]{3,2,1,0:T(8,128)(2,1)S(1)} %get-tuple-element.51.hid), channel_id=1, source_target_pairs={{0,64},{64,128},{128,192},{192,256},{256,320},{320,384},{384,448},... | collective-permute-start | bytes 1572872 | tf_op jit(solution)/shard_map/ppermute | solution.py:361
  43.6 6.5 %all-to-all-done.got = bf16[16,192,128]{2,1,0:T(8,128)(2,1)S(1)} async-done(((bf16[16,192,128]{2,1,0:T(8,128)(2,1)}), bf16[16,192,128]{2,1,0:T(8,128)(2,1)S(1)}, u32[]{:S(2)}, u32[]{:S(2)}) %all-to-all-start) | async-done | bytes 786464 | tf_op jit(solution)/shard_map/all_to_all | solution.py:354
  50.1 0.9 %shard_map.83 = f32[16,4,384]{2,1,0:T(4,128)} custom-call(bf16[16,192,128]{2,1,0:T(8,128)(2,1)S(1)} %all-to-all-done.got, bf16[2,1,128,256]{3,2,1,0:T(8,128)(2,1)S(1)} %collective-permute-done.4.refs_0_.refs_1_.pair, bf16[2,1,128,256]{3,2,1,0:T(8,128)(2,1)S(1)} %collective-permute-done.5.refs_0_.chip), custom_call_target="tpu_custom_call" | custom-call | flops 1048576 | bytes 1048576 | tf_op jit(solution)/shard_map/pallas_call | solution.py:65
  51.0 11.8 %all-to-all-start.1 = ((f32[16,4,384]{2,1,0:T(4,128)}), f32[16,4,384]{2,1,0:T(4,128)S(1)}, u32[]{:S(2)}, u32[]{:S(2)}) async-start(f32[16,4,384]{2,1,0:T(4,128)} %shard_map.83), calls=%async_computation.1 | async-start | bytes 196608 | tf_op jit(solution)/shard_map/all_to_all | solution.py:378
  62.8 1.0 %copy-done.3 = bf16[3,256,256]{2,1,0:T(8,128)(2,1)S(1)} copy-done((bf16[3,256,256]{2,1,0:T(8,128)(2,1)S(1)}, bf16[3,256,256]{2,1,0:T(8,128)(2,1)}, u32[]{:S(2)}) %copy-start.3) | copy-done | bytes 393240
  63.8 2.4 %shard_map.84 = bf16[2,4,128,256]{3,2,1,0:T(8,128)(2,1)} custom-call(bf16[2,4,128,256]{3,2,1,0:T(8,128)(2,1)S(1)} %get-tuple-element.51.hid, bf16[2,4,128,256]{3,2,1,0:T(8,128)(2,1)} %collective-permute-done.6.past, bf16[3,256,256]{2,1,0:T(8,128)(2,1)S(1)} %copy-done.3), custom_call_target="tpu_custom_call" | custom-call | flops 402653184 | bytes 2097152 | tf_op jit(solution)/shard_map/pallas_call | solution.py:65
  66.2 2.2 %shard_map.85 = bf16[2,4,128,256]{3,2,1,0:T(8,128)(2,1)} custom-call(s32[1]{0:T(128)} %bitcast.core, bf16[2,4,128,256]{3,2,1,0:T(8,128)(2,1)S(1)} %copy-done.1, bf16[2,1,128,256]{3,2,1,0:T(8,128)(2,1)S(1)} %collective-permute-done.4.refs_0_.refs_1_.pair, bf16[2,1,128,256]{3,2,1,0:T(8,128)(2,1)S(1)} %collective-permute-done.5.refs_0_.chip, ...), custom_call_target="tpu_custom_call" | custom-call | flops 1207959552 | bytes 4194304 | tf_op jit(solution)/shard_map/pallas_call | solution.py:65
  68.4 7.3 %all-to-all-done.1.got = f32[16,4,384]{2,1,0:T(4,128)S(1)} async-done(((f32[16,4,384]{2,1,0:T(4,128)}), f32[16,4,384]{2,1,0:T(4,128)S(1)}, u32[]{:S(2)}, u32[]{:S(2)}) %all-to-all-start.1) | async-done | bytes 98336 | tf_op jit(solution)/shard_map/all_to_all | solution.py:378
  75.7 0.7 shard_map.86
  (18 shorter events, 0.2 us)
Async XLA Ops:
  0.6 19.4 %collective-permute-start = (bf16[2,4,128,256]{3,2,1,0:T(8,128)(2,1)}, bf16[2,4,128,256]{3,2,1,0:T(8,128)(2,1)S(1)}, u32[]{:S(2)}, u32[]{:S(2)}) collective-permute-start(bf16[2,4,128,256]{3,2,1,0:T(8,128)(2,1)} %g.1), channel_id=1, source_target_pairs={{64,0},{128,64},{192,128},{256,192},{320,256},{384,320},{448,384},... | collective-permute-start | bytes 1572872 | tf_op jit(solution)/shard_map/ppermute | solution.py:300
  3.3 1.0 %copy-start.2 = (bf16[3,256,256]{2,1,0:T(8,128)(2,1)S(1)}, bf16[3,256,256]{2,1,0:T(8,128)(2,1)}, u32[]{:S(2)}) copy-start(bf16[3,256,256]{2,1,0:T(8,128)(2,1)} %wt.5) | copy-start | bytes 1179652
  3.3 1.2 %copy-start.4 = (bf16[2,4,128,256]{3,2,1,0:T(8,128)(2,1)S(1)}, bf16[2,4,128,256]{3,2,1,0:T(8,128)(2,1)}, u32[]{:S(2)}) copy-start(bf16[2,4,128,256]{3,2,1,0:T(8,128)(2,1)} %x.3) | copy-start | bytes 1572868
  3.3 1.3 %copy-start.5 = (bf16[2,4,128,256]{3,2,1,0:T(8,128)(2,1)S(1)}, bf16[2,4,128,256]{3,2,1,0:T(8,128)(2,1)}, u32[]{:S(2)}) copy-start(bf16[2,4,128,256]{3,2,1,0:T(8,128)(2,1)} %g.1) | copy-start | bytes 1572868
  4.6 3.1 %copy-start = (bf16[9,256,256]{2,1,0:T(8,128)(2,1)S(1)}, bf16[9,256,256]{2,1,0:T(8,128)(2,1)}, u32[]{:S(2)}) copy-start(bf16[9,256,256]{2,1,0:T(8,128)(2,1)} %ws.5) | copy-start | bytes 3538948
  5.1 3.9 %collective-permute-start.1 = (bf16[2,1,128,256]{3,2,1,0:T(8,128)(2,1)S(1)}, bf16[2,1,128,256]{3,2,1,0:T(8,128)(2,1)S(1)}, u32[]{:S(2)}, u32[]{:S(2)}) collective-permute-start(bf16[2,1,128,256]{3,2,1,0:T(8,128)(2,1)S(1)} %get-tuple-element.33), channel_id=1, source_target_pairs={{0,1},{1,0},{2,3},{3,2},{4,5},{5,4},{6,7},{7,6},{8,9},{9,8},{10,11... | collective-permute-start | bytes 393224 | tf_op jit(solution)/shard_map/ppermute | solution.py:287
  7.1 2.0 %collective-permute-start.2 = (bf16[2,1,128,256]{3,2,1,0:T(8,128)(2,1)S(1)}, bf16[2,1,128,256]{3,2,1,0:T(8,128)(2,1)S(1)}, u32[]{:S(2)}, u32[]{:S(2)}) collective-permute-start(bf16[2,1,128,256]{3,2,1,0:T(8,128)(2,1)S(1)} %get-tuple-element.34), channel_id=1, source_target_pairs={{1,2},{3,4},{5,6},{7,8},{9,10},{11,12},{13,14},{15,16},{17,18},{19... | collective-permute-start | bytes 393224 | tf_op jit(solution)/shard_map/ppermute | solution.py:292
  23.2 4.3 %collective-permute-start.3 = (bf16[12,256,128]{2,1,0:T(8,128)(2,1)S(1)}, bf16[12,256,128]{2,1,0:T(8,128)(2,1)S(1)}, u32[]{:S(2)}, u32[]{:S(2)}) collective-permute-start(bf16[12,256,128]{2,1,0:T(8,128)(2,1)S(1)} %get-tuple-element.42), channel_id=1, source_target_pairs={{0,1},{1,0},{2,3},{3,2},{4,5},{5,4},{6,7},{7,6},{8,9},{9,8},{10,11... | collective-permute-start | bytes 2359304 | tf_op jit(solution)/shard_map/ppermute | solution.py:343
  25.1 12.7 %collective-permute-start.4 = (bf16[2,1,128,256]{3,2,1,0:T(8,128)(2,1)}, bf16[2,1,128,256]{3,2,1,0:T(8,128)(2,1)S(1)}, u32[]{:S(2)}, u32[]{:S(2)}) collective-permute-start(bf16[2,1,128,256]{3,2,1,0:T(8,128)(2,1)} %get-tuple-element.47), channel_id=1, source_target_pairs={{0,1},{1,0},{2,3},{3,2},{4,5},{5,4},{6,7},{7,6},{8,9},{9,8},{10,11... | collective-permute-start | bytes 393224 | tf_op jit(solution)/shard_map/ppermute | solution.py:287
  28.7 21.4 %all-to-all-start = ((bf16[16,192,128]{2,1,0:T(8,128)(2,1)}), bf16[16,192,128]{2,1,0:T(8,128)(2,1)S(1)}, u32[]{:S(2)}, u32[]{:S(2)}) async-start(bf16[16,192,128]{2,1,0:T(8,128)(2,1)} %get-tuple-element.44), calls=%async_computation | async-start | bytes 1572864 | tf_op jit(solution)/shard_map/all_to_all | solution.py:354
  37.8 0.7 collective-permute-start.5
  38.5 27.6 %copy-start.1 = (bf16[2,4,128,256]{3,2,1,0:T(8,128)(2,1)S(1)}, bf16[2,4,128,256]{3,2,1,0:T(8,128)(2,1)}, u32[]{:S(2)}) copy-start(bf16[2,4,128,256]{3,2,1,0:T(8,128)(2,1)} %get-tuple-element.43.gpre) | copy-start | bytes 1572868
  38.5 24.2 %collective-permute-start.6 = (bf16[2,4,128,256]{3,2,1,0:T(8,128)(2,1)S(1)}, bf16[2,4,128,256]{3,2,1,0:T(8,128)(2,1)}, u32[]{:S(2)}, u32[]{:S(2)}) collective-permute-start(bf16[2,4,128,256]{3,2,1,0:T(8,128)(2,1)S(1)} %get-tuple-element.51.hid), channel_id=1, source_target_pairs={{0,64},{64,128},{128,192},{192,256},{256,320},{320,384},{384,448},... | collective-permute-start | bytes 1572872 | tf_op jit(solution)/shard_map/ppermute | solution.py:361
  51.0 24.7 %all-to-all-start.1 = ((f32[16,4,384]{2,1,0:T(4,128)}), f32[16,4,384]{2,1,0:T(4,128)S(1)}, u32[]{:S(2)}, u32[]{:S(2)}) async-start(f32[16,4,384]{2,1,0:T(4,128)} %shard_map.83), calls=%async_computation.1 | async-start | bytes 196608 | tf_op jit(solution)/shard_map/all_to_all | solution.py:378
  62.8 1.0 %copy-start.3 = (bf16[3,256,256]{2,1,0:T(8,128)(2,1)S(1)}, bf16[3,256,256]{2,1,0:T(8,128)(2,1)}, u32[]{:S(2)}) copy-start(bf16[3,256,256]{2,1,0:T(8,128)(2,1)} %wt.5) | copy-start | bytes 1179652
